TPU v7x, 32 devices: a whole 2x2x4 slice. The times are simulated.
32 devices in a mesh: seq: 16 (over z, y, core), fsdp: 2 (over x).
Axes of the slice: x: 2, y: 2, z: 4, core: 2. Of those that a mesh axis runs over, the one named last changes fastest.
Arguments:
- tokens: bfloat16 [2, 2048, 2048], P('fsdp', 'seq'), may hold values from -6 to 6
- segment_ids: int32 [2, 2048], P('fsdp'), may hold values from 0 to 3, as said below
- routes: int32 [2, 2048, 6], P('fsdp', 'seq'), may hold values from 0 to 15, all different within a row; in each aligned block of 128 rows (0 to 127, 128 to 255, ..., all dimensions but the last counted through in order) at most 96 rows name the same one
- gate_weights: float32 [2, 2048, 6], P('fsdp', 'seq'), may hold values from 0.2 to 0.5
- out_grad: bfloat16 [2, 2048, 2048], P('fsdp', 'seq'), may hold values from -6 to 6
- attn_gain: float32 [2048], P('fsdp'), may hold values from 0.5 to 1.5
- q_weight: float32 [2048, 3072], P('fsdp'), may hold values from -0.1875 to 0.1875
- latent_weight: float32 [2048, 576], P('fsdp'), may hold values from -0.125 to 0.125
- latent_gain: float32 [512], P('fsdp'), may hold values from 0.5 to 1.5
- kv_weight: float32 [512, 4096], P('fsdp'), may hold values from -0.25 to 0.25
- out_weight: float32 [2048, 2048], P('fsdp'), may hold values from -2 to 2
- ffn_gain: float32 [2048], P('fsdp'), may hold values from 0.5 to 1.5
- shared_gate: float32 [2048, 2816], P('fsdp'), may hold values from -0.125 to 0.125
- shared_up: float32 [2048, 2816], P('fsdp'), may hold values from -0.125 to 0.125
- shared_down: float32 [2816, 2048], P('fsdp'), may hold values from -0.109375 to 0.109375
- expert_gate: float32 [16, 2048, 1408], P('seq', 'fsdp'), may hold values from -0.125 to 0.125
- expert_up: float32 [16, 2048, 1408], P('seq', 'fsdp'), may hold values from -0.125 to 0.125
- expert_down: float32 [16, 1408, 2048], P('seq', 'fsdp'), may hold values from -0.15625 to 0.15625
Outputs:
- output: bfloat16 [2, 2048, 2048], P('fsdp', 'seq')
- input_grad: float32 [2, 2048, 2048], P('fsdp', 'seq')
- attn_gain_grad: float32 [2048], P('fsdp')
- q_weight_grad: float32 [2048, 3072], P('fsdp')
- latent_weight_grad: float32 [2048, 576], P('fsdp')
- latent_gain_grad: float32 [512], P('fsdp')
- kv_weight_grad: float32 [512, 4096], P('fsdp')
- out_weight_grad: float32 [2048, 2048], P('fsdp')
- ffn_gain_grad: float32 [2048], P('fsdp')
- shared_gate_grad: float32 [2048, 2816], P('fsdp')
- shared_up_grad: float32 [2048, 2816], P('fsdp')
- shared_down_grad: float32 [2816, 2048], P('fsdp')
- expert_gate_grad: float32 [16, 2048, 1408], P('seq', 'fsdp')
- expert_up_grad: float32 [16, 2048, 1408], P('seq', 'fsdp')
- expert_down_grad: float32 [16, 1408, 2048], P('seq', 'fsdp')
Inputs may be any that keep to these rules, and one draw needn't show every extreme that they name: `routes`: each token names 6 different experts; in each aligned block of 128 positions of a sequence, no expert is named by more than 96 tokens, a bound that some block reaches. `segment_ids`: each sequence holds four documents, ids never falling along it; the k-th boundary lies within 256 positions of k * 512.
All inputs are finite; a program needn't handle non-finite values.
Results may differ from a plain program's by a relative error of at most 0.024.
The roundings to bfloat16 on the way count: a program that leaves them out, or rounds other values in their place, can miss the bound.
Values may be sent and summed in bfloat16 or wider, within the bound.
A program may use at most 448 MiB of HBM per device.

v0:
```python
import math

import jax
import jax.numpy as jnp
from jax import lax
from jax.sharding import PartitionSpec as P

HEADS = 16
NOPE = 128
ROPE = 64
KV_RANK = 512
V_DIM = 128
TOP = 6


EPS = 1e-06
NEG = -1e30
THETA = 10000.0


def norm_scale(values):
    return lax.rsqrt(jnp.mean(values * values, axis=-1, keepdims=True) + EPS)


def norm_back(values, inverse, gradient):
    return inverse * gradient - values * inverse * inverse * inverse * jnp.mean(
        gradient * values, axis=-1, keepdims=True
    )


def matmul(left_matrix, right_matrix):
    return jnp.dot(left_matrix, right_matrix, preferred_element_type=jnp.float32)


def matmul_tn(left_matrix, right_matrix):
    return lax.dot_general(
        left_matrix, right_matrix, (((0,), (0,)), ((), ())), preferred_element_type=jnp.float32
    )


def matmul_nt(left_matrix, right_matrix):
    return lax.dot_general(
        left_matrix, right_matrix, (((1,), (1,)), ((), ())), preferred_element_type=jnp.float32
    )


def rope_tables(length):
    places = jnp.arange(length, dtype=jnp.float32)
    exponent = jnp.arange(ROPE // 2, dtype=jnp.float32) * (-2.0 / ROPE)
    frequency = jnp.power(THETA, exponent)
    angles = places[:, None] * frequency[None, :]
    angles = jnp.concatenate([angles, angles], axis=-1)
    return (jnp.cos(angles)[None, :, None, :], jnp.sin(angles)[None, :, None, :])


def rotate(values, cosine_table, sine_table):
    half_dims = values.shape[-1] // 2
    turned = jnp.concatenate([-values[..., half_dims:], values[..., :half_dims]], axis=-1)
    return values * cosine_table + turned * sine_table


def unrotate(gradient, cosine_table, sine_table):
    half_dims = gradient.shape[-1] // 2
    scaled = gradient * sine_table
    return gradient * cosine_table + jnp.concatenate(
        [scaled[..., half_dims:], -scaled[..., :half_dims]], axis=-1
    )


def rotated_heads(packed, length):
    q_dim = NOPE + ROPE
    cosine_table, sine_table = rope_tables(length)
    queries = packed[..., :q_dim].astype(jnp.float32)
    keys = packed[..., q_dim:].astype(jnp.float32)
    query_rot = jnp.concatenate(
        [queries[..., :NOPE], rotate(queries[..., NOPE:], cosine_table, sine_table)], axis=-1
    )
    key_rot = jnp.concatenate(
        [keys[..., :NOPE], rotate(keys[..., NOPE:], cosine_table, sine_table)], axis=-1
    )
    return (query_rot.astype(jnp.bfloat16), key_rot.astype(jnp.bfloat16), cosine_table, sine_table)


def score_block(query_block, key_rot, segments, offset):
    block_rows = query_block.shape[1]
    length = key_rot.shape[1]
    scale_factor = 1.0 / math.sqrt(NOPE + ROPE)
    scores = (
        jnp.einsum("sqhd,skhd->shqk", query_block, key_rot, preferred_element_type=jnp.float32)
        * scale_factor
    )
    query_place = offset + jnp.arange(block_rows, dtype=jnp.int32)
    key_place = jnp.arange(length, dtype=jnp.int32)
    query_segment = lax.dynamic_slice_in_dim(segments, offset, block_rows, 1)
    allowed = (key_place[None, None, :] <= query_place[None, :, None]) & (
        segments[:, None, :] == query_segment[:, :, None]
    )
    return (scores, allowed[:, None, :, :])


def attend_heads(packed, values, segments):
    seq_count, length, head_count = (packed.shape[0], packed.shape[1], packed.shape[2])
    query_rot, key_rot, cosine_table, sine_table = rotated_heads(packed, length)
    block_rows = min(512, length)
    block_count = length // block_rows

    def attend_block_fn(block_index):
        offset = block_index * block_rows
        query_block = lax.dynamic_slice_in_dim(query_rot, offset, block_rows, 1)
        scores, allowed = score_block(query_block, key_rot, segments, offset)
        scores = jnp.where(allowed, scores, NEG)
        row_peak = jnp.max(scores, axis=-1, keepdims=True)
        raised = jnp.exp(scores - row_peak)
        row_total = jnp.sum(raised, axis=-1, keepdims=True)
        layer_weights = (raised / row_total).astype(jnp.bfloat16)
        attended = jnp.einsum(
            "shqk,skhd->sqhd", layer_weights, values, preferred_element_type=jnp.float32
        )
        log_total = (row_peak + jnp.log(row_total))[..., 0]
        return (attended.astype(jnp.bfloat16), jnp.swapaxes(log_total, 1, 2))

    attended, log_totals = lax.map(attend_block_fn, jnp.arange(block_count, dtype=jnp.int32))
    attended = jnp.moveaxis(attended, 0, 1).reshape(seq_count, length, head_count, V_DIM)
    log_totals = jnp.moveaxis(log_totals, 0, 1).reshape(seq_count, length, head_count)
    return (attended, log_totals)


def run_back(packed, values, log_totals, grad_out, segments):
    seq_count, length, head_count = (packed.shape[0], packed.shape[1], packed.shape[2])
    q_dim = NOPE + ROPE
    query_rot, key_rot, cosine_table, sine_table = rotated_heads(packed, length)
    scale_factor = 1.0 / math.sqrt(NOPE + ROPE)
    block_rows = min(512, length)
    block_count = length // block_rows
    lse_heads = jnp.swapaxes(log_totals, 1, 2)

    def run_block_fn(running, block_index):
        key_grad, value_grad = running
        offset = block_index * block_rows
        query_block = lax.dynamic_slice_in_dim(query_rot, offset, block_rows, 1)
        grad_block = lax.dynamic_slice_in_dim(grad_out, offset, block_rows, 1)
        lse_block = lax.dynamic_slice_in_dim(lse_heads, offset, block_rows, 2)
        scores, allowed = score_block(query_block, key_rot, segments, offset)
        layer_weights = jnp.where(allowed, jnp.exp(scores - lse_block[..., None]), 0.0)
        value_grad = value_grad + jnp.einsum(
            "shqk,sqhd->skhd",
            layer_weights.astype(jnp.bfloat16),
            grad_block,
            preferred_element_type=jnp.float32,
        )
        weight_grad = jnp.einsum(
            "sqhd,skhd->shqk", grad_block, values, preferred_element_type=jnp.float32
        )
        row_delta = jnp.sum(layer_weights * weight_grad, axis=-1, keepdims=True)
        score_grad = (layer_weights * (weight_grad - row_delta) * scale_factor).astype(jnp.bfloat16)
        query_grad = jnp.einsum(
            "shqk,skhd->sqhd", score_grad, key_rot, preferred_element_type=jnp.float32
        )
        key_grad = key_grad + jnp.einsum(
            "shqk,sqhd->skhd", score_grad, query_block, preferred_element_type=jnp.float32
        )
        return ((key_grad, value_grad), query_grad)

    start_keys = jnp.zeros((seq_count, length, head_count, q_dim), jnp.float32)
    start_values = jnp.zeros((seq_count, length, head_count, V_DIM), jnp.float32)
    (key_grad, value_grad), query_grads = lax.scan(
        run_block_fn, (start_keys, start_values), jnp.arange(block_count, dtype=jnp.int32)
    )
    query_grad = jnp.moveaxis(query_grads, 0, 1).reshape(seq_count, length, head_count, q_dim)
    query_full = jnp.concatenate(
        [query_grad[..., :NOPE], unrotate(query_grad[..., NOPE:], cosine_table, sine_table)],
        axis=-1,
    )
    key_full = jnp.concatenate(
        [key_grad[..., :NOPE], unrotate(key_grad[..., NOPE:], cosine_table, sine_table)], axis=-1
    )
    return (
        jnp.concatenate([query_full, key_full], axis=-1).astype(jnp.bfloat16),
        value_grad.astype(jnp.bfloat16),
    )


def per_device(
    tokens,
    segment_ids,
    routes,
    gate_weights,
    out_grad,
    attn_gain,
    q_weight,
    latent_weight,
    latent_gain,
    kv_weight,
    out_weight,
    ffn_gain,
    shared_gate,
    shared_up,
    shared_down,
    expert_gate,
    expert_up,
    expert_down,
):
    seq_count, local_len, model_width = tokens.shape
    row_count = seq_count * local_len
    seq_devices = lax.axis_size("seq")
    local_heads = HEADS // seq_devices
    q_dim = NOPE + ROPE
    kv_dim = NOPE + V_DIM
    brain_float_half = jnp.bfloat16
    single_float = jnp.float32
    gathered = (
        lax.all_gather(attn_gain.astype(brain_float_half), "fsdp", axis=0, tiled=True),
        lax.all_gather(q_weight.astype(brain_float_half), "fsdp", axis=0, tiled=True),
        lax.all_gather(latent_weight.astype(brain_float_half), "fsdp", axis=0, tiled=True),
        lax.all_gather(latent_gain.astype(brain_float_half), "fsdp", axis=0, tiled=True),
        lax.all_gather(kv_weight.astype(brain_float_half), "fsdp", axis=0, tiled=True),
        lax.all_gather(out_weight.astype(brain_float_half), "fsdp", axis=0, tiled=True),
        lax.all_gather(ffn_gain.astype(brain_float_half), "fsdp", axis=0, tiled=True),
        lax.all_gather(shared_gate.astype(brain_float_half), "fsdp", axis=0, tiled=True),
        lax.all_gather(shared_up.astype(brain_float_half), "fsdp", axis=0, tiled=True),
        lax.all_gather(shared_down.astype(brain_float_half), "fsdp", axis=0, tiled=True),
        lax.all_gather(expert_gate.astype(brain_float_half), "fsdp", axis=1, tiled=True),
        lax.all_gather(expert_up.astype(brain_float_half), "fsdp", axis=1, tiled=True),
        lax.all_gather(expert_down.astype(brain_float_half), "fsdp", axis=1, tiled=True),
    )
    (
        first_norm_gain,
        w_query,
        w_latent,
        gain_latent,
        w_expand,
        w_output,
        second_norm_gain,
        w_sgate,
        w_sup,
        w_sdown,
        w_egate,
        expert_up_matrix,
        w_edown,
    ) = gathered
    local_experts = w_egate.shape[0]
    tok_f32 = tokens.reshape(row_count, model_width).astype(single_float)
    scale_one = norm_scale(tok_f32)
    normed_one = tok_f32 * scale_one
    gain_one_f = first_norm_gain.astype(single_float)
    act_one = (normed_one * gain_one_f).astype(brain_float_half)
    q_proj = matmul(act_one, w_query).astype(brain_float_half)
    latent = matmul(act_one, w_latent)
    compressed = latent[:, :KV_RANK]
    key_rope = latent[:, KV_RANK:].astype(brain_float_half)
    scale_lat = norm_scale(compressed)
    normed_lat = compressed * scale_lat
    gain_lat_f = gain_latent.astype(single_float)
    comp_low = (normed_lat * gain_lat_f).astype(brain_float_half)
    kv_heads = matmul(comp_low, w_expand).astype(brain_float_half).reshape(row_count, HEADS, kv_dim)
    rope_heads = jnp.broadcast_to(key_rope[:, None, :], (row_count, HEADS, ROPE))
    packed = jnp.concatenate(
        [q_proj.reshape(row_count, HEADS, q_dim), kv_heads[..., :NOPE], rope_heads], axis=-1
    )
    packed = packed.reshape(seq_count, local_len, seq_devices, local_heads, 2 * q_dim)
    value_tok = kv_heads[..., NOPE:].reshape(seq_count, local_len, seq_devices, local_heads, V_DIM)
    piece_packed = lax.all_to_all(packed, "seq", split_axis=2, concat_axis=1, tiled=True)
    piece_values = lax.all_to_all(value_tok, "seq", split_axis=2, concat_axis=1, tiled=True)
    piece_seqs = piece_packed.shape[0]
    piece_len = piece_packed.shape[1]
    piece_heads = piece_packed.shape[3]
    attended, log_totals = attend_heads(
        piece_packed.reshape(piece_seqs, piece_len, piece_heads, 2 * q_dim),
        piece_values.reshape(piece_seqs, piece_len, piece_heads, V_DIM),
        segment_ids,
    )
    head_out = attended[:, :, None]
    head_lse = log_totals[:, :, None]
    full_len = head_out.shape[1]
    attn_tok = lax.all_to_all(head_out, "seq", split_axis=1, concat_axis=2, tiled=True).reshape(
        row_count, HEADS * V_DIM
    )
    resid = tok_f32 + matmul(attn_tok, w_output)
    scale_two = norm_scale(resid)
    normed_two = resid * scale_two
    gain_two_f = second_norm_gain.astype(single_float)
    act_two = (normed_two * gain_two_f).astype(brain_float_half)
    shared_g = matmul(act_two, w_sgate)
    shared_u = matmul(act_two, w_sup)
    shared_hid = (jax.nn.silu(shared_g) * shared_u).astype(brain_float_half)
    shared_out = matmul(shared_hid, w_sdown)
    total_experts = local_experts * seq_devices
    most_rows = min(local_len, 2 * local_len * TOP // total_experts)
    capacity = seq_count * most_rows
    slots_total = total_experts * capacity
    route_flat = routes.reshape(seq_count, local_len * TOP)
    one_hot = (
        route_flat[:, :, None] == jnp.arange(total_experts, dtype=jnp.int32)[None, None, :]
    ).astype(jnp.int32)
    before = jnp.cumsum(one_hot, axis=1) - one_hot
    slot_rank = jnp.sum(before * one_hot, axis=-1)
    seq_place = jnp.arange(seq_count, dtype=jnp.int32)[:, None]
    target = (route_flat * capacity + seq_place * most_rows + slot_rank).reshape(-1)
    slot_owner = (
        jnp.full((slots_total,), -1, jnp.int32)
        .at[target]
        .set(jnp.arange(row_count * TOP, dtype=jnp.int32))
    )
    filled = slot_owner >= 0
    owner_safe = jnp.maximum(slot_owner, 0)
    owner_row = owner_safe // TOP
    send_rows = jnp.where(filled[:, None], act_two[owner_row], jnp.zeros((), brain_float_half))
    send_rows = send_rows.reshape(seq_devices, local_experts, capacity, model_width)
    received_tokens = lax.all_to_all(send_rows, "seq", split_axis=0, concat_axis=0, tiled=True)
    gate_pre = jnp.einsum(
        "ongy,nyh->ongh", received_tokens, w_egate, preferred_element_type=single_float
    )
    up_preactivation = jnp.einsum(
        "ongy,nyh->ongh", received_tokens, expert_up_matrix, preferred_element_type=single_float
    )
    hidden = (jax.nn.silu(gate_pre) * up_preactivation).astype(brain_float_half)
    expert_out = jnp.einsum(
        "secf,efd->secd", hidden, w_edown, preferred_element_type=single_float
    ).astype(brain_float_half)
    expert_out, saved_input, kept_gate, kept_up = (
        expert_out,
        received_tokens,
        gate_pre,
        up_preactivation,
    )
    returned = lax.all_to_all(expert_out, "seq", split_axis=0, concat_axis=0, tiled=True)
    picked = (
        returned.reshape(slots_total, model_width)[target]
        .astype(single_float)
        .reshape(row_count, TOP, model_width)
    )
    gates_flat = gate_weights.reshape(row_count, TOP)
    routed_tokens = jnp.sum(gates_flat[:, :, None] * picked, axis=1)
    output = (
        (resid + shared_out + routed_tokens)
        .astype(brain_float_half)
        .reshape(seq_count, local_len, model_width)
    )
    grad_b = out_grad.reshape(row_count, model_width)
    grad_f = grad_b.astype(single_float)
    owner_gate = gates_flat.reshape(-1)[owner_safe]
    d_send = jnp.where(filled[:, None], owner_gate[:, None] * grad_f[owner_row], 0.0).astype(
        brain_float_half
    )
    d_send = d_send.reshape(seq_devices, local_experts, capacity, model_width)
    d_recv = lax.all_to_all(d_send, "seq", split_axis=0, concat_axis=0, tiled=True)
    sig_e = jax.nn.sigmoid(kept_gate)
    expert_activation = kept_gate * sig_e
    hid_e = (expert_activation * kept_up).astype(brain_float_half)
    grad_edown = jnp.einsum("secf,secd->efd", hid_e, d_recv, preferred_element_type=single_float)
    hidden_cotangent = jnp.einsum(
        "secd,efd->secf", d_recv, w_edown, preferred_element_type=single_float
    )
    d_egate = (hidden_cotangent * kept_up * sig_e * (1.0 + kept_gate * (1.0 - sig_e))).astype(
        brain_float_half
    )
    expert_up_cotangent = (hidden_cotangent * expert_activation).astype(brain_float_half)
    grad_egate = jnp.einsum(
        "urgw,urgt->rwt", saved_input, d_egate, preferred_element_type=single_float
    )
    expert_up_gradient = jnp.einsum(
        "urgw,urgt->rwt", saved_input, expert_up_cotangent, preferred_element_type=single_float
    )
    d_entry = (
        jnp.einsum("bupy,uiy->bupi", d_egate, w_egate, preferred_element_type=single_float)
        + jnp.einsum(
            "bupy,uiy->bupi",
            expert_up_cotangent,
            expert_up_matrix,
            preferred_element_type=single_float,
        )
    ).astype(brain_float_half)
    d_returned = lax.all_to_all(d_entry, "seq", split_axis=0, concat_axis=0, tiled=True)
    routed_grad = jnp.sum(
        d_returned.reshape(slots_total, model_width)[target]
        .astype(single_float)
        .reshape(row_count, TOP, model_width),
        axis=1,
    )
    d_shared = matmul_nt(grad_b, w_sdown)
    grad_sdown = matmul_tn(shared_hid, grad_b)
    sig_s = jax.nn.sigmoid(shared_g)
    act_s = shared_g * sig_s
    d_sgate = (d_shared * shared_u * sig_s * (1.0 + shared_g * (1.0 - sig_s))).astype(
        brain_float_half
    )
    d_sup = (d_shared * act_s).astype(brain_float_half)
    grad_sgate = matmul_tn(act_two, d_sgate)
    grad_sup = matmul_tn(act_two, d_sup)
    d_act_two = matmul_nt(d_sgate, w_sgate) + matmul_nt(d_sup, w_sup) + routed_grad
    grad_gain_two = jnp.sum(d_act_two * normed_two, axis=0)
    d_resid = grad_f + norm_back(resid, scale_two, d_act_two * gain_two_f)
    d_attn = d_resid.astype(brain_float_half)
    grad_output = matmul_tn(attn_tok, d_attn)
    d_heads_tok = (
        matmul_nt(d_attn, w_output)
        .astype(brain_float_half)
        .reshape(seq_count, local_len, HEADS, V_DIM)
    )
    d_heads = lax.all_to_all(d_heads_tok, "seq", split_axis=2, concat_axis=1, tiled=True)
    packed_heads = piece_packed.reshape(seq_count, full_len, local_heads, 2 * q_dim)
    values_heads = piece_values.reshape(seq_count, full_len, local_heads, V_DIM)
    lse_heads = head_lse.reshape(seq_count, full_len, local_heads)
    d_packed_h, d_values_h = run_back(packed_heads, values_heads, lse_heads, d_heads, segment_ids)
    d_packed, d_values = (
        lax.all_to_all(d_packed_h, "seq", split_axis=1, concat_axis=2, tiled=True),
        lax.all_to_all(d_values_h, "seq", split_axis=1, concat_axis=2, tiled=True),
    )
    d_query = d_packed[..., :q_dim].reshape(row_count, HEADS * q_dim)
    d_expand = jnp.concatenate([d_packed[..., q_dim : q_dim + NOPE], d_values], axis=-1).reshape(
        row_count, HEADS * kv_dim
    )
    d_rope = jnp.sum(d_packed[..., q_dim + NOPE :].astype(single_float), axis=2).reshape(
        row_count, ROPE
    )
    grad_query = matmul_tn(act_one, d_query)
    grad_expand = matmul_tn(comp_low, d_expand)
    d_comp = matmul_nt(d_expand, w_expand)
    grad_gain_lat = jnp.sum(d_comp * normed_lat, axis=0)
    d_compressed = norm_back(compressed, scale_lat, d_comp * gain_lat_f)
    d_latent = jnp.concatenate([d_compressed, d_rope], axis=-1).astype(brain_float_half)
    grad_latent = matmul_tn(act_one, d_latent)
    d_act_one = matmul_nt(d_query, w_query) + matmul_nt(d_latent, w_latent)
    grad_gain_one = jnp.sum(d_act_one * normed_one, axis=0)
    input_grad = (d_resid + norm_back(tok_f32, scale_one, d_act_one * gain_one_f)).reshape(
        seq_count, local_len, model_width
    )
    owned_grads = (
        lax.psum_scatter(
            grad_gain_one.astype(jnp.bfloat16), "fsdp", scatter_dimension=0, tiled=True
        ).astype(jnp.float32),
        lax.psum_scatter(
            grad_query.astype(jnp.bfloat16), "fsdp", scatter_dimension=0, tiled=True
        ).astype(jnp.float32),
        lax.psum_scatter(
            grad_latent.astype(jnp.bfloat16), "fsdp", scatter_dimension=0, tiled=True
        ).astype(jnp.float32),
        lax.psum_scatter(
            grad_gain_lat.astype(jnp.bfloat16), "fsdp", scatter_dimension=0, tiled=True
        ).astype(jnp.float32),
        lax.psum_scatter(
            grad_expand.astype(jnp.bfloat16), "fsdp", scatter_dimension=0, tiled=True
        ).astype(jnp.float32),
        lax.psum_scatter(
            grad_output.astype(jnp.bfloat16), "fsdp", scatter_dimension=0, tiled=True
        ).astype(jnp.float32),
        lax.psum_scatter(
            grad_gain_two.astype(jnp.bfloat16), "fsdp", scatter_dimension=0, tiled=True
        ).astype(jnp.float32),
        lax.psum_scatter(
            grad_sgate.astype(jnp.bfloat16), "fsdp", scatter_dimension=0, tiled=True
        ).astype(jnp.float32),
        lax.psum_scatter(
            grad_sup.astype(jnp.bfloat16), "fsdp", scatter_dimension=0, tiled=True
        ).astype(jnp.float32),
        lax.psum_scatter(
            grad_sdown.astype(jnp.bfloat16), "fsdp", scatter_dimension=0, tiled=True
        ).astype(jnp.float32),
        lax.psum_scatter(
            grad_egate.astype(jnp.bfloat16), "fsdp", scatter_dimension=1, tiled=True
        ).astype(jnp.float32),
        lax.psum_scatter(
            expert_up_gradient.astype(jnp.bfloat16), "fsdp", scatter_dimension=1, tiled=True
        ).astype(jnp.float32),
        lax.psum_scatter(
            grad_edown.astype(jnp.bfloat16), "fsdp", scatter_dimension=1, tiled=True
        ).astype(jnp.float32),
    )
    dense_grads = (
        lax.psum(owned_grads[0].astype(jnp.bfloat16), "seq").astype(jnp.float32),
        lax.psum(owned_grads[1].astype(jnp.bfloat16), "seq").astype(jnp.float32),
        lax.psum(owned_grads[2].astype(jnp.bfloat16), "seq").astype(jnp.float32),
        lax.psum(owned_grads[3].astype(jnp.bfloat16), "seq").astype(jnp.float32),
        lax.psum(owned_grads[4].astype(jnp.bfloat16), "seq").astype(jnp.float32),
        lax.psum(owned_grads[5].astype(jnp.bfloat16), "seq").astype(jnp.float32),
        lax.psum(owned_grads[6].astype(jnp.bfloat16), "seq").astype(jnp.float32),
        lax.psum(owned_grads[7].astype(jnp.bfloat16), "seq").astype(jnp.float32),
        lax.psum(owned_grads[8].astype(jnp.bfloat16), "seq").astype(jnp.float32),
        lax.psum(owned_grads[9].astype(jnp.bfloat16), "seq").astype(jnp.float32),
    )
    expert_grads = (owned_grads[10], owned_grads[11], owned_grads[12])
    return (
        output,
        input_grad,
        dense_grads[0],
        dense_grads[1],
        dense_grads[2],
        dense_grads[3],
        dense_grads[4],
        dense_grads[5],
        dense_grads[6],
        dense_grads[7],
        dense_grads[8],
        dense_grads[9],
        expert_grads[0],
        expert_grads[1],
        expert_grads[2],
    )


def solution(mesh):
    return jax.shard_map(
        per_device,
        mesh=mesh,
        in_specs=(
            P("fsdp", "seq", None),
            P("fsdp", None),
            P("fsdp", "seq", None),
            P("fsdp", "seq", None),
            P("fsdp", "seq", None),
            P("fsdp"),
            P("fsdp", None),
            P("fsdp", None),
            P("fsdp"),
            P("fsdp", None),
            P("fsdp", None),
            P("fsdp"),
            P("fsdp", None),
            P("fsdp", None),
            P("fsdp", None),
            P("seq", "fsdp", None),
            P("seq", "fsdp", None),
            P("seq", "fsdp", None),
        ),
        out_specs=(
            P("fsdp", "seq", None),
            P("fsdp", "seq", None),
            P("fsdp"),
            P("fsdp", None),
            P("fsdp", None),
            P("fsdp"),
            P("fsdp", None),
            P("fsdp", None),
            P("fsdp"),
            P("fsdp", None),
            P("fsdp", None),
            P("fsdp", None),
            P("seq", "fsdp", None),
            P("seq", "fsdp", None),
            P("seq", "fsdp", None),
        ),
        check_vma=False,
    )
```

profile of v0, /device:TPU:9, one launch (start us, length us, event | category | flops | bytes accessed | tf_op | source)
XLA Modules:
  0.0 2795.5 jit_solution(772924073717632866)
XLA Ops:
  14.0 8.5 convert_element_type.348
  28.7 7.4 convert_element_type.362
  36.1 7.4 convert_element_type.363
  43.6 7.7 convert_element_type.365
  71.5 35.0 %all-gather.16.cloned.1.call-done = bf16[512,4096]{1,0:T(8,128)(2,1)} async-done(((bf16[256,4096]{1,0:T(8,128)(2,1)}), bf16[512,4096]{1,0:T(8,128)(2,1)}) %all-gather.16.cloned.1.call-update) | async-done | bytes 4194320 | tf_op jit(solution)/shard_map/all_gather | solution.py:216
  111.2 149.9 %all-gather.12.cloned.1.call-done = bf16[2048,3072]{1,0:T(8,128)(2,1)} async-done(((bf16[1024,3072]{1,0:T(8,128)(2,1)}), bf16[2048,3072]{1,0:T(8,128)(2,1)}) %all-gather.12.cloned.1.call-update) | async-done | bytes 12582928 | tf_op jit(solution)/shard_map/all_gather | solution.py:213
  283.5 27.7 all-to-all-done
  332.5 28.9 %while.27 = (s32[]{:T(128)}, bf16[4,1,512,1,128]{4,2,3,1,0:T(8,128)(2,1)S(1)}, f32[4,1,512,1]{2,3,1,0:T(1,128)}, s32[4]{0:T(128)S(1)}, s32[1,2048]{1,0:T(1,128)S...) while((s32[]{:T(128)}, ...), condition=%wide.region_5.6_spmd, body=%wide.region_2.5_spmd.sunk | while | flops 682688512 | bytes 14260427 | solution.py:122
  361.4 8.1 copy.218
  370.0 11.5 reduce.14
  394.8 7.5 all-to-all-done.2
  402.3 10.9 reshape.968
  419.7 90.5 %all-gather.20.cloned.1.call-done = bf16[2048,2816]{1,0:T(8,128)(2,1)} async-done(((bf16[1024,2816]{1,0:T(8,128)(2,1)}), bf16[2048,2816]{1,0:T(8,128)(2,1)}) %all-gather.20.cloned.1.call-update) | async-done | bytes 11534352 | tf_op jit(solution)/shard_map/all_gather | solution.py:219
  510.2 7.0 fusion.136
  517.3 136.0 %all-gather.22.cloned.1.call-done = bf16[2048,2816]{1,0:T(8,128)(2,1)} async-done(((bf16[1024,2816]{1,0:T(8,128)(2,1)}), bf16[2048,2816]{1,0:T(8,128)(2,1)}) %all-gather.22.cloned.1.call-update) | async-done | bytes 11534352 | tf_op jit(solution)/shard_map/all_gather | solution.py:220
  653.3 7.0 fusion.137
  660.3 136.1 %all-gather.24.cloned.1.call-done = bf16[2816,2048]{1,0:T(8,128)(2,1)} async-done(((bf16[1408,2048]{1,0:T(8,128)(2,1)}), bf16[2816,2048]{1,0:T(8,128)(2,1)}) %all-gather.24.cloned.1.call-update) | async-done | bytes 11534352 | tf_op jit(solution)/shard_map/all_gather | solution.py:221
  796.5 10.1 multiply_convert_fusion.1
  823.4 7.9 gather_fusion.3
  831.3 8.3 select_convert_fusion
  845.9 7.0 gather_fusion
  858.9 122.3 %all-to-all-done.5 = bf16[16,1,96,2048]{3,2,1,0:T(8,128)(2,1)} async-done(((bf16[16,1,96,2048]{3,2,1,0:T(8,128)(2,1)}), bf16[16,1,96,2048]{3,2,1,0:T(8,128)(2,1)}, u32[]{:S(2)}, u32[]{:S(2)}) %all-to-all-start.5) | async-done | bytes 6291488 | tf_op jit(solution)/shard_map/all_to_all | solution.py:346
  981.2 7.1 all-to-all-start.3
  994.7 15.2 fusion.45
  1009.9 113.5 %all-to-all-done.3 = bf16[16,1,96,2048]{3,2,1,0:T(8,128)(2,1)} async-done(((bf16[16,1,96,2048]{3,2,1,0:T(8,128)(2,1)}), bf16[16,1,96,2048]{3,2,1,0:T(8,128)(2,1)}, u32[]{:S(2)}, u32[]{:S(2)}) %all-to-all-start.3) | async-done | bytes 6291488 | tf_op jit(solution)/shard_map/all_to_all | solution.py:309
  1123.5 15.1 fusion.49
  1138.6 22.3 fusion.33
  1160.9 14.9 fusion.56
  1175.8 16.9 fusion.43
  1192.7 7.5 all-to-all-start.6
  1207.7 9.0 fusion.138
  1216.7 118.7 %all-to-all-done.6 = bf16[16,1,96,2048]{3,2,1,0:T(8,128)(2,1)} async-done(((bf16[16,1,96,2048]{3,2,1,0:T(8,128)(2,1)}), bf16[16,1,96,2048]{3,2,1,0:T(8,128)(2,1)}, u32[]{:S(2)}, u32[]{:S(2)}) %all-to-all-start.6) | async-done | bytes 6291488 | tf_op jit(solution)/shard_map/all_to_all | solution.py:373
  1335.4 9.9 gather_fusion.4
  1355.5 9.2 multiply_reduce_fusion.2
  1372.9 7.6 all-to-all-start.7
  1380.5 14.1 all-to-all-done.7
  1394.6 98.6 %while.28 = (s32[]{:T(128)}, f32[1,2048,1,192]{1,3,2,0:T(8,128)}, f32[1,2048,1,128]{1,3,2,0:T(8,128)S(1)}, f32[4,1,512,1,192]{2,0,4,3,1:T(4,128)}, s32[4]{0:T(12...) while((s32[]{:T(128)}, f32[1,2048,1,192]{1,3,2,0:T(8,128)}, ...), condition=%wide.region_16.17_spmd.clone, body=%wide.region_14.16_spmd.clone.sunk | while | flops 1759772672 | bytes 75002160 | solution.py:166
  1410.2 8.6 dynamic_update_slice.20
  1435.1 8.6 dynamic_update_slice.20
  1459.9 8.6 dynamic_update_slice.20
  1484.6 8.6 dynamic_update_slice.20
  1505.1 12.7 reduce.16
  1541.6 7.9 copy.180
  1549.5 34.4 %reduce.15 = bf16[2048,384]{1,0:T(8,128)(2,1)} reduce(bf16[2048,1,1,384]{3,2,1,0:T(2,128)(2,1)S(1)} %bitcast.449, bf16[]{:T(256)} %broadcast.395), dimensions={1,2}, to_apply=%bitcast.334.reduce_sub_computation | reduce | bytes 3145730
  1597.7 32.2 %all-to-all-done.8 = bf16[16,2,24576]{2,1,0:T(2,128)(2,1)} async-done(((bf16[16,2,24576]{2,1,0:T(2,128)(2,1)}), bf16[16,2,24576]{2,1,0:T(2,128)(2,1)}, u32[]{:S(2)}, u32[]{:S(2)}) %all-to-all-start.8) | async-done | bytes 1572896 | tf_op jit(solution)/shard_map/all_to_all | solution.py:406
  1629.9 8.1 reshape.970
  1661.0 6.7 convolution_convert_fusion.3
  1667.7 15.5 fusion.40
  1683.4 15.0 fusion.41
  1698.5 14.7 fusion.42
  1713.3 25.8 reduce-scatter.15.cloned.1.call-done
  1739.2 102.0 %reduce-scatter.17.cloned.1.call-done = bf16[1024,2048]{1,0:T(8,128)(2,1)} async-done(((bf16[2048,2048]{1,0:T(8,128)(2,1)}), bf16[1024,2048]{1,0:T(8,128)(2,1)}) %reduce-scatter.17.cloned.1.call-update) | async-done | bytes 4194320 | tf_op jit(solution)/shard_map/reduce_scatter | solution.py:444
  1841.2 147.3 %reduce-scatter.11.cloned.1.call-done = bf16[1024,3072]{1,0:T(8,128)(2,1)} async-done(((bf16[2048,3072]{1,0:T(8,128)(2,1)}), bf16[1024,3072]{1,0:T(8,128)(2,1)}) %reduce-scatter.11.cloned.1.call-update) | async-done | bytes 6291472 | tf_op jit(solution)/shard_map/reduce_scatter | solution.py:432
  1988.6 15.1 convert_bitcast_fusion
  2012.0 50.7 %reduce-scatter.25.cloned.1.call-done = bf16[1,1024,1408]{2,1,0:T(8,128)(2,1)} async-done(((bf16[1,2048,1408]{2,1,0:T(8,128)(2,1)}), bf16[1,1024,1408]{2,1,0:T(8,128)(2,1)}) %reduce-scatter.25.cloned.1.call-update) | async-done | bytes 2883600 | tf_op jit(solution)/shard_map/reduce_scatter | solution.py:459
  2067.5 69.6 %reduce-scatter.27.cloned.1.call-done = bf16[1,1024,1408]{2,1,0:T(8,128)(2,1)} async-done(((bf16[1,2048,1408]{2,1,0:T(8,128)(2,1)}), bf16[1,1024,1408]{2,1,0:T(8,128)(2,1)}) %reduce-scatter.27.cloned.1.call-update) | async-done | bytes 2883600 | tf_op jit(solution)/shard_map/reduce_scatter | solution.py:462
  2141.8 68.9 %reduce-scatter.29.cloned.1.call-done = bf16[1,704,2048]{2,1,0:T(8,128)(2,1)} async-done(((bf16[1,1408,2048]{2,1,0:T(8,128)(2,1)}), bf16[1,704,2048]{2,1,0:T(8,128)(2,1)}) %reduce-scatter.29.cloned.1.call-update) | async-done | bytes 2883600 | tf_op jit(solution)/shard_map/reduce_scatter | solution.py:465
  2215.8 10.7 gather_fusion.1
  2226.5 6.8 reshape.893
  2233.3 6.9 multiply_reduce_fusion.1
  2240.3 7.2 fusion.75
  2259.6 26.2 all-reduce.3
  2290.2 461.8 %all-reduce.8.cloned.1.call-done = (bf16[1024,3072]{1,0:T(8,128)(2,1)}, bf16[1024,576]{0,1:T(8,128)(2,1)}, bf16[256,4096]{1,0:T(8,128)(2,1)}, bf16[1024,2048]{1,...) async-done(((bf16[1024,3072]{1,0:T(8,128)(2,1)}, bf16[1024,576]{0,1:T(8,128)(2,1)}, ...) | async-done | bytes 31064080 | tf_op jit(solution)/shard_map/psum | solution.py:471
  2752.0 9.3 convert_element_type.400
  (456 shorter events, 387.6 us)
Async XLA Ops:
  7.2 61.7 %all-gather.14.cloned.1.call-start = ((), (), s32[]{:S(2)}) async-start(), calls=%async_computation.21 | async-start | bytes 3538944 | tf_op jit(solution)/shard_map/all_gather | solution.py:214
  10.1 96.3 %all-gather.16.cloned.1.call-start = ((), (), s32[]{:S(2)}) async-start(), calls=%async_computation.22 | async-start | bytes 6291456 | tf_op jit(solution)/shard_map/all_gather | solution.py:216
  14.0 247.2 %all-gather.12.cloned.1.call-start = ((), (), s32[]{:S(2)}) async-start(), calls=%async_computation.20 | async-start | bytes 18874368 | tf_op jit(solution)/shard_map/all_gather | solution.py:213
  22.5 391.1 %all-gather.18.cloned.1.call-start = ((), (), s32[]{:S(2)}) async-start(), calls=%async_computation.23 | async-start | bytes 12582912 | tf_op jit(solution)/shard_map/all_gather | solution.py:217
  28.6 481.6 %all-gather.20.cloned.1.call-start = ((), (), s32[]{:S(2)}) async-start(), calls=%async_computation.24 | async-start | bytes 17301504 | tf_op jit(solution)/shard_map/all_gather | solution.py:219
  36.1 617.2 %all-gather.22.cloned.1.call-start = ((), (), s32[]{:S(2)}) async-start(), calls=%async_computation.25 | async-start | bytes 17301504 | tf_op jit(solution)/shard_map/all_gather | solution.py:220
  43.5 752.9 %all-gather.24.cloned.1.call-start = ((), (), s32[]{:S(2)}) async-start(), calls=%async_computation.26 | async-start | bytes 17301504 | tf_op jit(solution)/shard_map/all_gather | solution.py:221
  51.3 943.4 %all-gather.30.cloned.1.call-start = ((), (), s32[]{:S(2)}) async-start(), calls=%async_computation.29 | async-start | bytes 8650752 | tf_op jit(solution)/shard_map/all_gather | solution.py:224
  56.1 9.0 copy-start.65
  56.1 12.5 copy-start.3
  56.1 953.9 %all-gather.28.cloned.1.call-start = ((), (), s32[]{:S(2)}) async-start(), calls=%async_computation.28 | async-start | bytes 8650752 | tf_op jit(solution)/shard_map/all_gather | solution.py:223
  65.1 196.1 %copy-start.36 = (f32[2048]{0:T(1024)}, f32[2048]{0:T(1024)S(1)}, u32[]{:S(2)}) copy-start(f32[2048]{0:T(1024)S(1)} %convert_element_type.346) | copy-start | bytes 24580
  68.6 40.9 %copy-start.45 = (f32[2,1,256]{2,1,0:T(1,128)}, f32[2,1,256]{2,1,0:T(1,128)S(1)}, u32[]{:S(2)}) copy-start(f32[2,1,256]{2,1,0:T(1,128)S(1)} %convert_element_type.429) | copy-start | bytes 6148
  68.8 192.3 %copy-start.51 = (f32[128]{0:T(128)}, f32[128]{0:T(128)S(1)}, u32[]{:S(2)}) copy-start(f32[128]{0:T(128)S(1)} %add_rsqrt_fusion.2) | copy-start | bytes 1540
  71.4 39.4 %copy-start.18 = (f32[128,576]{0,1:T(8,128)}, f32[128,576]{0,1:T(8,128)S(1)}, u32[]{:S(2)}) copy-start(f32[128,576]{0,1:T(8,128)S(1)} %fusion.123) | copy-start | bytes 884740
  71.5 38.3 %copy-start.57 = (f32[128]{0:T(128)}, f32[128]{0:T(128)S(1)}, u32[]{:S(2)}) copy-start(f32[128]{0:T(128)S(1)} %add_rsqrt_fusion.1) | copy-start | bytes 1540
  269.4 41.8 %all-to-all-start = ((bf16[1,128,16,1,384]{1,4,3,0,2:T(8,128)(2,1)}), bf16[1,128,16,1,384]{1,4,3,0,2:T(8,128)(2,1)S(1)}, u32[]{:S(2)}, u32[]{:S(2)}) async-start(bf16[1,128,16,1,384]{1,4,3,0,2:T(8,128)(2,1)} %maximum_bitcast_fusion), calls=%async_computation | async-start | bytes 3145728 | tf_op jit(solution)/shard_map/all_to_all | solution.py:262
  275.8 862.9 %all-gather.26.cloned.1.call-start = ((), (), s32[]{:S(2)}) async-start(), calls=%async_computation.27 | async-start | bytes 8650752 | tf_op jit(solution)/shard_map/all_gather | solution.py:222
  281.1 40.3 %copy-start.8 = (f32[1,2048,1,32]{3,1,2,0:T(8,128)}, f32[1,2048,1,32]{3,1,2,0:T(8,128)S(1)}, u32[]{:S(2)}) copy-start(f32[1,2048,1,32]{3,1,2,0:T(8,128)S(1)} %multiply_bitcast_fusion) | copy-start | bytes 786436
  312.4 20.1 all-to-all-start.1
  361.4 26.9 copy-start.56
  361.4 29.6 %copy-start.63 = (f32[1,128,6]{1,0,2:T(1,128)S(1)}, f32[1,128,6]{1,0,2:T(1,128)}, u32[]{:S(2)}) copy-start(f32[1,128,6]{1,0,2:T(1,128)} %param.25) | copy-start | bytes 9220
  361.4 29.9 %copy-start.62 = (f32[1024]{0:T(1024)S(1)}, f32[1024]{0:T(1024)}, u32[]{:S(2)}) copy-start(f32[1024]{0:T(1024)} %param.33) | copy-start | bytes 12292
  382.5 19.9 all-to-all-start.2
  388.2 1325.1 %reduce-scatter.19.cloned.1.call-start = ((), (), s32[]{:S(2)}) async-start(), calls=%async_computation.34 | async-start | bytes 17301504 | tf_op jit(solution)/shard_map/reduce_scatter | solution.py:450
  394.8 23.8 copy-start.43
  418.6 98.7 %copy-start.59 = (f32[128]{0:T(128)}, f32[128]{0:T(128)S(1)}, u32[]{:S(2)}) copy-start(f32[128]{0:T(128)S(1)} %add_rsqrt_fusion) | copy-start | bytes 1540
  517.3 279.2 %copy-start.23 = (bf16[1,128,2048]{2,1,0:T(8,128)(2,1)S(1)}, bf16[1,128,2048]{2,1,0:T(8,128)(2,1)}, u32[]{:S(2)}) copy-start(bf16[1,128,2048]{2,1,0:T(8,128)(2,1)} %param.26) | copy-start | bytes 1572868
  806.6 181.7 %copy-start.28 = (bf16[128,2816]{1,0:T(8,128)(2,1)}, bf16[128,2816]{1,0:T(8,128)(2,1)S(1)}, u32[]{:S(2)}) copy-start(bf16[128,2816]{1,0:T(8,128)(2,1)S(1)} %get-tuple-element.317) | copy-start | bytes 2162692
  839.6 141.5 %all-to-all-start.5 = ((bf16[16,1,96,2048]{3,2,1,0:T(8,128)(2,1)}), bf16[16,1,96,2048]{3,2,1,0:T(8,128)(2,1)}, u32[]{:S(2)}, u32[]{:S(2)}) async-start(bf16[16,1,96,2048]{3,2,1,0:T(8,128)(2,1)} %select_convert_fusion), calls=%async_computation.5 | async-start | bytes 12582912 | tf_op jit(solution)/shard_map/all_to_all | solution.py:346
  981.2 142.3 %all-to-all-start.3 = ((bf16[16,1,96,2048]{3,2,1,0:T(8,128)(2,1)}), bf16[16,1,96,2048]{3,2,1,0:T(8,128)(2,1)}, u32[]{:S(2)}, u32[]{:S(2)}) async-start(bf16[16,1,96,2048]{3,2,1,0:T(8,128)(2,1)} %broadcast_select_fusion), calls=%async_computation.3 | async-start | bytes 12582912 | tf_op jit(solution)/shard_map/all_to_all | solution.py:309
  988.2 725.0 %reduce-scatter.21.cloned.1.call-start = ((), (), s32[]{:S(2)}) async-start(), calls=%async_computation.35 | async-start | bytes 17301504 | tf_op jit(solution)/shard_map/reduce_scatter | solution.py:453
  1138.6 22.3 copy-start.64
  1192.7 7.5 copy-start.21
  1192.7 7.5 copy-start.24
  1192.7 142.7 %all-to-all-start.6 = ((bf16[16,1,96,2048]{3,2,1,0:T(8,128)(2,1)}), bf16[16,1,96,2048]{3,2,1,0:T(8,128)(2,1)}, u32[]{:S(2)}, u32[]{:S(2)}) async-start(bf16[16,1,96,2048]{3,2,1,0:T(8,128)(2,1)} %fusion.43), calls=%async_computation.6 | async-start | bytes 12582912 | tf_op jit(solution)/shard_map/all_to_all | solution.py:373
  1200.2 513.1 %reduce-scatter.23.cloned.1.call-start = ((), (), s32[]{:S(2)}) async-start(), calls=%async_computation.36 | async-start | bytes 17301504 | tf_op jit(solution)/shard_map/reduce_scatter | solution.py:456
  1207.7 127.8 %copy-start.49 = (s32[1024]{0:T(1024)}, s32[1024]{0:T(1024)S(1)}, u32[]{:S(2)}) copy-start(s32[1024]{0:T(1024)S(1)} %pad_clamp_fusion.2) | copy-start | bytes 12292
  1355.5 9.2 copy-start.25
  1365.2 29.4 %copy-start.48 = (s32[1,2048]{1,0:T(1,128)S(1)}, s32[1,2048]{1,0:T(1,128)}, u32[]{:S(2)}) copy-start(s32[1,2048]{1,0:T(1,128)} %param.23) | copy-start | bytes 24580
  1372.9 21.6 all-to-all-start.7
  1501.5 21.8 copy-start.9
  1518.8 69.6 %all-to-all-start.9 = ((bf16[16,2,8192]{2,1,0:T(2,128)(2,1)}), bf16[16,2,8192]{2,1,0:T(2,128)(2,1)}, u32[]{:S(2)}, u32[]{:S(2)}) async-start(bf16[16,2,8192]{2,1,0:T(2,128)(2,1)} %reshape.971), calls=%async_computation.9 | async-start | bytes 1048576 | tf_op jit(solution)/shard_map/all_to_all | solution.py:407
  1588.3 41.6 %all-to-all-start.8 = ((bf16[16,2,24576]{2,1,0:T(2,128)(2,1)}), bf16[16,2,24576]{2,1,0:T(2,128)(2,1)}, u32[]{:S(2)}, u32[]{:S(2)}) async-start(bf16[16,2,24576]{2,1,0:T(2,128)(2,1)} %reshape.969), calls=%async_computation.8 | async-start | bytes 3145728 | tf_op jit(solution)/shard_map/all_to_all | solution.py:406
  1594.3 119.0 %reduce-scatter.13.cloned.1.call-start = ((), (), s32[]{:S(2)}) async-start(), calls=%async_computation.31 | async-start | bytes 3538944 | tf_op jit(solution)/shard_map/reduce_scatter | solution.py:435
  1647.7 91.5 %reduce-scatter.15.cloned.1.call-start = ((), (), s32[]{:S(2)}) async-start(), calls=%async_computation.32 | async-start | bytes 6291456 | tf_op jit(solution)/shard_map/reduce_scatter | solution.py:441
  1651.1 190.1 %reduce-scatter.17.cloned.1.call-start = ((), (), s32[]{:S(2)}) async-start(), calls=%async_computation.33 | async-start | bytes 12582912 | tf_op jit(solution)/shard_map/reduce_scatter | solution.py:444
  1656.9 331.6 %reduce-scatter.11.cloned.1.call-start = ((), (), s32[]{:S(2)}) async-start(), calls=%async_computation.30 | async-start | bytes 18874368 | tf_op jit(solution)/shard_map/reduce_scatter | solution.py:432
  1667.7 395.1 %reduce-scatter.25.cloned.1.call-start = ((), (), s32[]{:S(2)}) async-start(), calls=%async_computation.37 | async-start | bytes 8650752 | tf_op jit(solution)/shard_map/reduce_scatter | solution.py:459
  1683.3 453.8 %reduce-scatter.27.cloned.1.call-start = ((), (), s32[]{:S(2)}) async-start(), calls=%async_computation.38 | async-start | bytes 8650752 | tf_op jit(solution)/shard_map/reduce_scatter | solution.py:462
  1698.4 512.3 %reduce-scatter.29.cloned.1.call-start = ((), (), s32[]{:S(2)}) async-start(), calls=%async_computation.39 | async-start | bytes 8650752 | tf_op jit(solution)/shard_map/reduce_scatter | solution.py:465
  1713.2 1038.8 %all-reduce.8.cloned.1.call-start = ((), (), s32[]{:S(2)}) async-start(), calls=%async_computation.40 | async-start | bytes 62128128 | tf_op jit(solution)/shard_map/psum | solution.py:471
  2003.6 212.2 %all-to-all-start.4 = ((bf16[16,1,96,2048]{3,2,1,0:T(8,128)(2,1)}), bf16[16,1,96,2048]{3,2,1,0:T(8,128)(2,1)}, u32[]{:S(2)}, u32[]{:S(2)}) async-start(bf16[16,1,96,2048]{3,2,1,0:T(8,128)(2,1)} %convert_bitcast_fusion), calls=%async_computation.4 | async-start | bytes 12582912 | tf_op jit(solution)/shard_map/all_to_all | solution.py:326
  2141.8 74.1 %copy-start.50 = (s32[1024]{0:T(1024)S(1)}, s32[1024]{0:T(1024)}, u32[]{:S(2)}) copy-start(s32[1024]{0:T(1024)} %copy-done.49) | copy-start | bytes 12292
  2226.5 6.8 copy-start.39
  2233.3 6.9 copy-start.7
  2233.3 6.9 copy-start.22
  2233.3 14.1 slice-start
  2240.2 7.2 slice-start.1
  2240.2 7.2 slice-start.2
  2752.0 9.3 copy-start.33
  2763.7 7.6 slice-start.7
  2766.3 10.6 slice-start.5
  2771.3 10.9 slice-start.3
  (49 other events, 192.0 us)
Sparse Core Ops, SparseCore 0:
  10.2 37.2 all-gather.13
  49.6 56.8 all-gather.15
  108.6 152.5 all-gather.11
  263.1 104.0 all-gather.17
  369.2 141.0 all-gather.19
  512.2 141.0 all-gather.21
  655.4 141.0 all-gather.23
  798.6 74.4 all-gather.29
  874.6 74.4 all-gather.27
  950.5 74.4 all-gather.25
  1027.9 133.1 reduce-scatter.18
  1163.9 133.1 reduce-scatter.20
  1299.9 133.1 reduce-scatter.22
  1647.8 34.1 reduce-scatter.12
  1684.9 54.2 reduce-scatter.14
  1741.9 99.2 reduce-scatter.16
  1844.0 144.4 reduce-scatter.10
  1991.4 71.3 reduce-scatter.24
  2065.6 71.3 reduce-scatter.26
  2139.3 71.3 reduce-scatter.28
  2216.5 535.4 all-reduce.7
where the time goes:
time: 2810 us; the launch traced here: 2800 us
  waiting for transfers between devices  1910 us (68%)
  matrix products  332 us (12%)
  other arithmetic  235 us (8%)
  local copies, waits for them, and re-layouts  189 us (7%)
  starting transfers between devices  64.5 us (2%)
  blocking collectives  41.1 us (1%)
    psum x1, waiting for transfers between devices, per_device(): lax.psum(owned_grads[1].astype(jnp.bfloat16), 'seq').astype(jnp.float32)  462 us
    all_gather x1, waiting for transfers between devices, per_device(): lax.all_gather(q_weight.astype(brain_float_half), 'fsdp', axis=0, tiled=T...  150 us
    reduce_scatter x1, waiting for transfers between devices, per_device(): lax.psum_scatter(grad_query.astype(jnp.bfloat16), 'fsdp', scatter_dimensi...  147 us
    all_gather x1, waiting for transfers between devices, per_device(): lax.all_gather(shared_down.astype(brain_float_half), 'fsdp', axis=0, tile...  136 us
    all_gather x1, waiting for transfers between devices, per_device(): lax.all_gather(shared_up.astype(brain_float_half), 'fsdp', axis=0, tiled=...  136 us
    all_to_all x1, waiting for transfers between devices, per_device(): lax.all_to_all(d_send, 'seq', split_axis=0, concat_axis=0, tiled=True)  122 us
    all_to_all x1, waiting for transfers between devices, per_device(): lax.all_to_all(d_entry, 'seq', split_axis=0, concat_axis=0, tiled=True)  119 us
    all_to_all x1, waiting for transfers between devices, per_device(): lax.all_to_all(send_rows, 'seq', split_axis=0, concat_axis=0, tiled=True)  114 us
  transfers between devices with their start and end apart: 31, of which 20 were waited for; matrix products, arithmetic and copies ran while one was open for 25% of the time, Pallas kernels for 0%

commit v1 on v0

v1 whole, which is shorter than its diff:
```python
import functools
import math

import jax
import jax.numpy as jnp
import numpy as np
from jax import lax
from jax.experimental import pallas as pl
from jax.experimental.pallas import tpu as pltpu
from jax.sharding import PartitionSpec as P

HEADS = 16
NOPE = 128
ROPE = 64
QD = NOPE + ROPE
KV_RANK = 512
V_DIM = 128
TOP = 6
MOST = 96

EPS = 1e-06
NEG = -1e30
THETA = 10000.0
SCALE = 1.0 / math.sqrt(QD)
MESH = pl.DeviceIdType.MESH
BF = jnp.bfloat16
F32 = jnp.float32
VMEM_LIMIT = 60 * 2**20


def norm_scale(values):
    return lax.rsqrt(jnp.mean(values * values, axis=-1, keepdims=True) + EPS)


def norm_back(values, inverse, gradient):
    return inverse * gradient - values * inverse * inverse * inverse * jnp.mean(
        gradient * values, axis=-1, keepdims=True
    )


def mm(a, b):
    return jnp.dot(a, b, preferred_element_type=F32)


def mm_tn(a, b):
    return lax.dot_general(a, b, (((0,), (0,)), ((), ())), preferred_element_type=F32)


def mm_nt(a, b):
    return lax.dot_general(a, b, (((1,), (1,)), ((), ())), preferred_element_type=F32)


def rope_tables(length):
    places = np.arange(length, dtype=np.float32)
    frequency = np.power(np.float32(THETA), np.arange(ROPE // 2, dtype=np.float32) * np.float32(-2.0 / ROPE))
    angles = places[:, None] * frequency[None, :].astype(np.float32)
    angles = np.concatenate([angles, angles], axis=-1)
    return jnp.asarray(np.cos(angles), F32), jnp.asarray(np.sin(angles), F32)


def ring_place():
    me = lax.axis_index("seq")
    core, chip = me % 2, me // 2
    z, y = chip // 2, chip % 2
    half = lax.axis_size("seq") // 4
    return me, core, jnp.where(y == 0, z, 2 * half - 1 - z), 2 * half


def ring_seq(r, core, n):
    low = r < n // 2
    return (jnp.where(low, r, n - 1 - r) * 2 + jnp.where(low, 0, 1)) * 2 + core


def greet(devices):
    barrier = pltpu.get_barrier_semaphore()
    for device in devices:
        pl.semaphore_signal(barrier, inc=1, device_id={"seq": device}, device_id_type=MESH)
    pl.semaphore_wait(barrier, len(devices))


def remote(src, dst, send, recv, device):
    return pltpu.make_async_remote_copy(src, dst, send, recv, device_id={"seq": device}, device_id_type=MESH)


def gather_kernel(n, pieces, x_ref, o_ref, own_sem, local_sem, send, recv, fsend, frecv):
    me, core, r, _ = ring_place()
    targets = (ring_seq((r + 1) % n, core, n), ring_seq((r + n - 1) % n, core, n))
    sibling = ring_seq(r, 1 - core, n)
    greet((*targets, sibling))
    height = x_ref.shape[0] // (2 * pieces)

    def rows(d, k):
        return pl.ds((d * pieces + k) * height, height)

    def block(t, d):
        return ring_seq((r + (-t if d == 0 else t) + n) % n, core, n)

    def onward(t, d, k):
        at = o_ref.at[block(t, d), rows(d, k)]
        source = x_ref.at[rows(d, k)] if t == 0 else at
        return remote(source, at, send.at[t, d, k], recv.at[t, d, k], targets[d])

    def across(t, d, k):
        at = o_ref.at[block(t, d), rows(d, k)]
        return remote(at, at, fsend.at[t - 1, d, k], frecv.at[t - 1, d, k], sibling)

    local = pltpu.make_async_copy(x_ref, o_ref.at[me], local_sem)
    local.start()
    own = remote(x_ref, o_ref.at[me], own_sem.at[0], own_sem.at[1], sibling)
    for k in range(pieces):
        for d in range(2):
            onward(0, d, k).start()
    own.start()
    for t in range(n - 1):
        for k in range(pieces):
            for d in range(2):
                onward(t, d, k).wait_recv()
                if t < n - 2:
                    onward(t + 1, d, k).start()
                across(t + 1, d, k).start()
    local.wait()
    own.wait()
    for t in range(n - 1):
        for k in range(pieces):
            for d in range(2):
                onward(t, d, k).wait_send()
                across(t + 1, d, k).wait()


def ring_gather(x, collective_id, pieces=2):
    devices = lax.axis_size("seq")
    n = devices // 2
    rows, columns = x.shape
    size = devices * rows * columns * x.dtype.itemsize
    sems = pltpu.SemaphoreType.DMA((n - 1, 2, pieces))
    out = pl.pallas_call(
        functools.partial(gather_kernel, n, pieces),
        out_shape=jax.ShapeDtypeStruct((devices, rows, columns), x.dtype),
        in_specs=[pl.BlockSpec(memory_space=pl.ANY)],
        out_specs=pl.BlockSpec(memory_space=pl.ANY),
        scratch_shapes=[pltpu.SemaphoreType.DMA((2,)), pltpu.SemaphoreType.DMA] + [sems] * 4,
        compiler_params=pltpu.CompilerParams(collective_id=collective_id, has_side_effects=True),
        cost_estimate=pl.CostEstimate(flops=0, bytes_accessed=22 * size, transcendentals=0),
        name="ring_gather",
    )(x)
    return out.reshape(devices * rows, columns)


def scatter_kernel(n, cut, with_weight, *refs):
    if with_weight:
        a_ref, w_ref, o_ref, stage, sibbuf, rbuf, sbuf, send, recv, fsend, frecv = refs
    else:
        a_ref, o_ref, sibbuf, rbuf, sbuf, send, recv, fsend, frecv = refs
    me, core, r, _ = ring_place()
    targets = (ring_seq((r + 1) % n, core, n), ring_seq((r + n - 1) % n, core, n))
    sibling = ring_seq(r, 1 - core, n)
    greet((*targets, sibling))
    height, columns = o_ref.shape
    spans = (pl.ds(0, cut), pl.ds(cut, columns - cut))

    def chip(t, d):
        return (r + (-t - 1 if d == 0 else t + 1) + n) % n

    def part(t, d, c):
        block = ring_seq(chip(t, d), c, n)
        if not with_weight:
            return a_ref[block, :, spans[d]].astype(F32)
        rows = a_ref[pl.ds(block * height, height), :]
        return mm_nt(rows, w_ref[spans[d], :])

    def across(t, d):
        if with_weight:
            source = stage.at[t, :, spans[d]]
        else:
            source = a_ref.at[ring_seq(chip(t, d), 1 - core, n), :, spans[d]]
        return remote(source, sibbuf.at[t, :, spans[d]], fsend.at[t, d], frecv.at[t, d], sibling)

    def onward(t, d):
        return remote(sbuf.at[t, :, spans[d]], rbuf.at[t, :, spans[d]], send.at[t, d], recv.at[t, d], targets[d])

    def give(t, d):
        if with_weight:
            stage[t, :, spans[d]] = part(t, d, 1 - core).astype(BF)
        across(t, d).start()

    if with_weight:
        for d in range(2):
            give(0, d)
    else:
        for t in range(n):
            for d in range(2):
                give(t, d)
    for t in range(n):
        for d in range(2):
            if with_weight and t < n - 1:
                give(t + 1, d)
            value = part(t, d, core)
            across(t, d).wait_recv()
            value = value + sibbuf[t, :, spans[d]].astype(F32)
            if t > 0:
                onward(t - 1, d).wait_recv()
                value = value + rbuf[t - 1, :, spans[d]].astype(F32)
            if t < n - 1:
                sbuf[t, :, spans[d]] = value.astype(BF)
                onward(t, d).start()
            else:
                o_ref[:, spans[d]] = value
    for t in range(n):
        for d in range(2):
            across(t, d).wait_send()
            if t < n - 1:
                onward(t, d).wait_send()


def ring_scatter(a, w, collective_id):
    devices = lax.axis_size("seq")
    n = devices // 2
    rows = a.shape[0] // devices
    columns = a.shape[1] if w is None else w.shape[0]
    cut = columns // 256 * 128
    size = devices * rows * columns * 2
    vmem = pl.BlockSpec(memory_space=pltpu.VMEM)
    operands = (a.reshape(devices, rows, columns),) if w is None else (a, w)
    buffers = [
        pltpu.VMEM((n, rows, columns), BF),
        pltpu.VMEM((n - 1, rows, columns), BF),
        pltpu.VMEM((n - 1, rows, columns), BF),
    ]
    if w is not None:
        buffers = [pltpu.VMEM((n, rows, columns), BF)] + buffers
    return pl.pallas_call(
        functools.partial(scatter_kernel, n, cut, w is not None),
        out_shape=jax.ShapeDtypeStruct((rows, columns), F32),
        in_specs=[vmem] * len(operands),
        out_specs=vmem,
        scratch_shapes=buffers
        + [pltpu.SemaphoreType.DMA((n - 1, 2))] * 2
        + [pltpu.SemaphoreType.DMA((n, 2))] * 2,
        compiler_params=pltpu.CompilerParams(
            collective_id=collective_id, has_side_effects=True, vmem_limit_bytes=VMEM_LIMIT
        ),
        cost_estimate=pl.CostEstimate(flops=0, bytes_accessed=22 * size, transcendentals=0),
        name="ring_scatter",
    )(*operands)


def fsdp_pair(x):
    return lax.ppermute(x, "fsdp", [(0, 1), (1, 0)])


def fsdp_gather(x):
    count = lax.axis_size("fsdp")
    if count != 2:
        return lax.all_gather(x, "fsdp", axis=0, tiled=True)
    other = fsdp_pair(x)
    first = lax.axis_index("fsdp") == 0
    return jnp.concatenate([jnp.where(first, x, other), jnp.where(first, other, x)], axis=0)


def fsdp_pick(x, owner):
    count = lax.axis_size("fsdp")
    if count != 2:
        return lax.dynamic_index_in_dim(lax.all_gather(x, "fsdp", axis=0), owner, 0, keepdims=False)
    return jnp.where(lax.axis_index("fsdp") == owner, x, fsdp_pair(x))


def fsdp_scatter(x):
    count = lax.axis_size("fsdp")
    if count != 2:
        return lax.psum_scatter(x.astype(BF), "fsdp", scatter_dimension=0, tiled=True).astype(F32)
    half = x.shape[0] // 2
    at = lax.axis_index("fsdp")
    kept = lax.dynamic_slice_in_dim(x, at * half, half, 0)
    given = lax.dynamic_slice_in_dim(x, (1 - at) * half, half, 0).astype(BF)
    return kept.astype(F32) + fsdp_pair(given).astype(F32)


def fsdp_sum(x):
    if lax.axis_size("fsdp") != 2:
        return lax.psum(x, "fsdp")
    return x + fsdp_pair(x)


def turn(values, cosine, sine):
    half = values.shape[-1] // 2
    turned = jnp.concatenate([-values[:, half:], values[:, :half]], axis=-1)
    return values * cosine + turned * sine


def turn_back(gradient, cosine, sine):
    half = gradient.shape[-1] // 2
    scaled = gradient * sine
    return gradient * cosine + jnp.concatenate([scaled[:, half:], -scaled[:, :half]], axis=-1)


def spans_of(length):
    step = length // 8
    for i in range(8):
        start = i * step
        yield start, step, max(0, start - (3 * step if i % 2 == 0 else 2 * step))


def allowed_of(seg_col, seg_row, start, step, low):
    width = start + step - low
    query = start + lax.broadcasted_iota(jnp.int32, (step, width), 0)
    key = low + lax.broadcasted_iota(jnp.int32, (step, width), 1)
    return (key <= query) & (seg_col[start : start + step, :] == seg_row[:, low : start + step])


def attend_kernel(q_ref, kv_ref, kr_ref, cos_ref, sin_ref, segc_ref, segr_ref, heads_ref, lse_ref, qh_ref, kh_ref):
    cosine, sine = cos_ref[...], sin_ref[...]
    qh_ref[:, :NOPE] = q_ref[:, :NOPE]
    qh_ref[:, NOPE:] = turn(q_ref[:, NOPE:].astype(F32), cosine, sine).astype(BF)
    kh_ref[:, :NOPE] = kv_ref[:, :NOPE]
    kh_ref[:, NOPE:] = turn(kr_ref[...].astype(F32), cosine, sine).astype(BF)
    for start, step, low in spans_of(q_ref.shape[0]):
        scores = mm_nt(qh_ref[start : start + step, :], kh_ref[low : start + step, :]) * SCALE
        scores = jnp.where(allowed_of(segc_ref, segr_ref, start, step, low), scores, NEG)
        peak = jnp.max(scores, axis=-1, keepdims=True)
        raised = jnp.exp(scores - peak)
        total = jnp.sum(raised, axis=-1, keepdims=True)
        prob = (raised * (1.0 / total)).astype(BF)
        heads_ref[start : start + step, :] = mm(prob, kv_ref[low : start + step, NOPE:]).astype(BF)
        lse_ref[start : start + step, :] = peak + jnp.log(total)


def attend_back_kernel(
    qh_ref, kh_ref, kv_ref, lse_ref, do_ref, cos_ref, sin_ref, segc_ref, segr_ref, dq_ref, dkv_ref, dkr_ref, dk_acc, dv_acc
):
    dk_acc[...] = jnp.zeros_like(dk_acc)
    dv_acc[...] = jnp.zeros_like(dv_acc)
    for start, step, low in spans_of(qh_ref.shape[0]):
        end = start + step
        query = qh_ref[start:end, :]
        grad = do_ref[start:end, :]
        keys = kh_ref[low:end, :]
        scores = mm_nt(query, keys) * SCALE
        allowed = allowed_of(segc_ref, segr_ref, start, step, low)
        prob = jnp.where(allowed, jnp.exp(scores - lse_ref[start:end, :]), 0.0)
        dv_acc[low:end, :] += mm_tn(prob.astype(BF), grad)
        dprob = mm_nt(grad, kv_ref[low:end, NOPE:])
        delta = jnp.sum(prob * dprob, axis=-1, keepdims=True)
        dscore = (prob * (dprob - delta) * SCALE).astype(BF)
        dquery = mm(dscore, keys)
        dq_ref[start:end, :NOPE] = dquery[:, :NOPE].astype(BF)
        dq_ref[start:end, NOPE:] = turn_back(dquery[:, NOPE:], cos_ref[start:end, :], sin_ref[start:end, :]).astype(BF)
        dk_acc[low:end, :] += mm_tn(dscore, query)
    dkv_ref[:, :NOPE] = dk_acc[:, :NOPE].astype(BF)
    dkv_ref[:, NOPE:] = dv_acc[...].astype(BF)
    dkr_ref[...] = turn_back(dk_acc[:, NOPE:], cos_ref[...], sin_ref[...]).astype(BF)


def local_call(kernel, outs, scratch, name, *operands):
    vmem = pl.BlockSpec(memory_space=pltpu.VMEM)
    return pl.pallas_call(
        kernel,
        out_shape=[jax.ShapeDtypeStruct(shape, dtype) for shape, dtype in outs],
        in_specs=[vmem] * len(operands),
        out_specs=[vmem] * len(outs),
        scratch_shapes=scratch,
        compiler_params=pltpu.CompilerParams(vmem_limit_bytes=VMEM_LIMIT),
        cost_estimate=pl.CostEstimate(flops=0, bytes_accessed=70 * 2**20, transcendentals=0),
        name=name,
    )(*operands)


def columns_of(weight, at, width):
    return lax.dynamic_slice_in_dim(weight, at * width, width, 1).astype(BF)


def rows_of(weight, at, height):
    return lax.dynamic_slice_in_dim(weight, at * height, height, 0).astype(BF)


def per_device(
    tokens,
    segment_ids,
    routes,
    gate_weights,
    out_grad,
    attn_gain,
    q_weight,
    latent_weight,
    latent_gain,
    kv_weight,
    out_weight,
    ffn_gain,
    shared_gate,
    shared_up,
    shared_down,
    expert_gate,
    expert_up,
    expert_down,
):
    _, rows, width = tokens.shape
    devices = lax.axis_size("seq")
    at = lax.axis_index("seq")
    parts = lax.axis_size("fsdp")
    part = lax.axis_index("fsdp")
    length = rows * devices
    own_x = tokens[0]
    own_g = out_grad[0]

    gains = jnp.concatenate([attn_gain, ffn_gain, latent_gain]).astype(BF)[None, :]
    gains = fsdp_gather(gains).astype(F32)
    per = attn_gain.shape[0]
    gain_one = gains[:, :per].reshape(1, -1)
    gain_two = gains[:, per : 2 * per].reshape(1, -1)
    gain_lat = gains[:, 2 * per :].reshape(1, -1)
    w_query = fsdp_gather(columns_of(q_weight, at, QD))
    w_latent = fsdp_gather(latent_weight.astype(BF))
    w_expand = fsdp_gather(columns_of(kv_weight, at, NOPE + V_DIM))
    out_rows = out_weight.shape[0]
    head_owner = at * V_DIM // out_rows
    w_out = fsdp_pick(lax.dynamic_slice_in_dim(out_weight, at * V_DIM % out_rows, V_DIM, 0).astype(BF), head_owner)
    hidden = shared_down.shape[0] * parts
    share = shared_down.shape[0] // devices

    def shared_columns(weight):
        pieces = [
            lax.dynamic_slice_in_dim(weight, p * (hidden // parts) + at * share, share, 1) for p in range(parts)
        ]
        return fsdp_gather(jnp.concatenate(pieces, axis=1).astype(BF))

    w_sgate = shared_columns(shared_gate)
    w_sup = shared_columns(shared_up)
    w_sdown = fsdp_gather(rows_of(shared_down, at, share))
    w_egate = fsdp_gather(expert_gate[0].astype(BF))
    w_eup = fsdp_gather(expert_up[0].astype(BF))
    w_edown = fsdp_gather(expert_down[0].astype(BF))

    experts = jnp.arange(devices, dtype=jnp.int32)
    spread = jnp.sum(
        jnp.where(routes[0][:, :, None] == experts[None, None, :], gate_weights[0][:, :, None], 0.0), axis=1
    )
    share_of = lax.all_to_all(spread.T, "seq", 0, 0, tiled=True)

    x_all = ring_gather(own_x, 1).astype(F32)
    r1_all = norm_scale(x_all)
    act_one = (x_all * r1_all * gain_one).astype(BF)
    q_proj = mm(act_one, w_query).astype(BF)
    latent = mm(act_one, w_latent)
    comp_all = latent[:, :KV_RANK]
    r2_all = norm_scale(comp_all)
    cnorm = (comp_all * r2_all * gain_lat).astype(BF)
    kv = mm(cnorm, w_expand).astype(BF)
    key_rope = latent[:, KV_RANK:].astype(BF)
    cosine, sine = rope_tables(length)
    seg_col, seg_row = segment_ids.reshape(length, 1), segment_ids
    heads, lse, qh, kh = local_call(
        attend_kernel,
        [((length, V_DIM), BF), ((length, 1), F32), ((length, QD), BF), ((length, QD), BF)],
        [],
        "attend",
        q_proj,
        kv,
        key_rope,
        cosine,
        sine,
        seg_col,
        seg_row,
    )
    own_xf = own_x.astype(F32)
    x1 = own_xf + ring_scatter(heads, w_out.T, 2)
    r3 = norm_scale(x1)
    act_two = (x1 * r3 * gain_two).astype(BF)
    g_all = ring_gather(own_g, 1)
    act_all = ring_gather(act_two, 1)

    sg, su = mm(act_all, w_sgate), mm(act_all, w_sup)
    sig = jax.nn.sigmoid(sg)
    silu = sg * sig
    sh = (silu * su).astype(BF)
    ys = mm(sh, w_sdown)
    dsh = mm_nt(g_all, w_sdown)
    dsg = (dsh * su * sig * (1.0 + sg * (1.0 - sig))).astype(BF)
    dsu = (dsh * silu).astype(BF)
    grad_sdown = fsdp_scatter(mm_tn(sh, g_all))
    grad_sgate = fsdp_scatter(mm_tn(act_all, dsg))
    grad_sup = fsdp_scatter(mm_tn(act_all, dsu))
    dact_shared = mm_nt(dsg, w_sgate) + mm_nt(dsu, w_sup)

    most = min(MOST, rows)
    named = share_of > 0.0
    rank = jnp.cumsum(named.astype(jnp.int32), axis=1) - 1
    pick = named[:, None, :] & (rank[:, None, :] == jnp.arange(most, dtype=jnp.int32)[None, :, None])
    pick_b = pick.astype(BF)
    share_packed = jnp.sum(jnp.where(pick, share_of[:, None, :], 0.0), axis=-1).reshape(-1, 1)

    def packed(values):
        blocks = values.reshape(devices, rows, width)
        return jnp.einsum("bct,btd->bcd", pick_b, blocks, preferred_element_type=F32).reshape(-1, width)

    def unpacked(values):
        blocks = values.reshape(devices, most, width)
        return jnp.einsum("bct,bcd->btd", pick_b, blocks, preferred_element_type=F32).reshape(-1, width)

    xe = packed(act_all).astype(BF)
    dye = (share_packed * packed(g_all)).astype(BF)
    ge, ue = mm(xe, w_egate), mm(xe, w_eup)
    sig_e = jax.nn.sigmoid(ge)
    silu_e = ge * sig_e
    he = (silu_e * ue).astype(BF)
    ye = mm(he, w_edown).astype(BF)
    dhe = mm_nt(dye, w_edown)
    dge = (dhe * ue * sig_e * (1.0 + ge * (1.0 - sig_e))).astype(BF)
    due = (dhe * silu_e).astype(BF)
    dxe = (mm_nt(dge, w_egate) + mm_nt(due, w_eup)).astype(BF)
    grad_edown = fsdp_scatter(mm_tn(he, dye))
    grad_egate = fsdp_scatter(mm_tn(xe, dge))
    grad_eup = fsdp_scatter(mm_tn(xe, due))
    dact_part = (dact_shared + unpacked(dxe)).astype(BF)
    y_part = (ys + unpacked((share_packed * ye.astype(F32)).astype(BF))).astype(BF)

    dact_two = ring_scatter(dact_part, None, 3)
    own_gf = own_g.astype(F32)
    grad_gain_two = jnp.sum(dact_two * x1 * r3, axis=0)
    dx1 = own_gf + norm_back(x1, r3, dact_two * gain_two)
    dattn_all = ring_gather(dx1.astype(BF), 1)
    y_sum = ring_scatter(y_part, None, 3)
    output = (x1 + y_sum).astype(BF)

    dheads = mm_nt(dattn_all, w_out).astype(BF)
    dqp, dkv, dkr = local_call(
        attend_back_kernel,
        [((length, QD), BF), ((length, NOPE + V_DIM), BF), ((length, ROPE), BF)],
        [pltpu.VMEM((length, QD), F32), pltpu.VMEM((length, V_DIM), F32)],
        "attend_back",
        qh,
        kh,
        kv,
        lse,
        dheads,
        cosine,
        sine,
        seg_col,
        seg_row,
    )
    back = jnp.concatenate([dqp, dkv, dkr], axis=1)
    kv_dim = NOPE + V_DIM
    w_back = jnp.concatenate(
        [
            jnp.pad(w_query, ((0, 0), (0, kv_dim + ROPE))),
            jnp.pad(w_expand, ((0, 0), (QD, ROPE))),
            jnp.pad(jnp.eye(ROPE, dtype=BF), ((0, 128 - ROPE), (QD + kv_dim, 0))),
        ],
        axis=0,
    )
    summed = ring_scatter(back, w_back, 4)
    grad_out = fsdp_sum(mm_tn(heads, dattn_all).astype(BF))
    grad_query = fsdp_scatter(mm_tn(act_one, dqp))
    grad_expand = fsdp_scatter(mm_tn(cnorm, dkv))

    r1 = norm_scale(own_xf)
    own_act = (own_xf * r1 * gain_one).astype(BF)
    own_comp = mm(own_act, w_latent)[:, :KV_RANK]
    r2 = norm_scale(own_comp)
    dcn = summed[:, width : width + KV_RANK]
    grad_gain_lat = jnp.sum(dcn * own_comp * r2, axis=0)
    dcomp = norm_back(own_comp, r2, dcn * gain_lat)
    dlatent = jnp.concatenate([dcomp, summed[:, width + KV_RANK : width + KV_RANK + ROPE]], axis=-1).astype(BF)
    dact_one = summed[:, :width] + mm_nt(dlatent, w_latent)
    grad_gain_one = jnp.sum(dact_one * own_xf * r1, axis=0)
    input_grad = dx1 + norm_back(own_xf, r1, dact_one * gain_one)

    dlatent_all = lax.all_gather(dlatent, "seq", axis=0, tiled=True)
    slab = width // parts // devices
    act_cols = jnp.concatenate(
        [lax.dynamic_slice_in_dim(act_one, p * (width // parts) + at * slab, slab, 1) for p in range(parts)], axis=1
    )
    grad_latent = fsdp_scatter(mm_tn(act_cols, dlatent_all)).astype(BF)

    def over_seq(x):
        return lax.all_gather(x.astype(BF), "seq", axis=0)

    def wide(x):
        stacked = over_seq(x)
        return jnp.swapaxes(stacked, 0, 1).reshape(x.shape[0], -1).astype(F32)

    def shared_wide(x):
        stacked = over_seq(x).reshape(devices, x.shape[0], parts, share)
        return jnp.transpose(stacked, (1, 2, 0, 3)).reshape(x.shape[0], -1).astype(F32)

    out_all = over_seq(grad_out).reshape(devices * V_DIM, width)
    out_grad_own = lax.dynamic_slice_in_dim(out_all, part * out_rows, out_rows, 0).astype(F32)
    small = jnp.concatenate([grad_gain_one, grad_gain_two, grad_gain_lat])
    small = fsdp_sum(jnp.sum(lax.all_gather(small, "seq", axis=0), axis=0))
    gain_rows = width // parts
    own_gains = [
        lax.dynamic_slice_in_dim(small, part * gain_rows, gain_rows),
        lax.dynamic_slice_in_dim(small, width + part * gain_rows, gain_rows),
        lax.dynamic_slice_in_dim(small, 2 * width + part * (KV_RANK // parts), KV_RANK // parts),
    ]
    return (
        output[None],
        input_grad[None],
        own_gains[0],
        wide(grad_query),
        over_seq(grad_latent).reshape(-1, grad_latent.shape[1]).astype(F32),
        own_gains[2],
        wide(grad_expand),
        out_grad_own,
        own_gains[1],
        shared_wide(grad_sgate),
        shared_wide(grad_sup),
        over_seq(grad_sdown).reshape(-1, width).astype(F32),
        grad_egate[None],
        grad_eup[None],
        grad_edown[None],
    )


def solution(mesh):
    token_spec = P("fsdp", "seq", None)
    row_spec = P("fsdp", None)
    gain_spec = P("fsdp")
    expert_spec = P("seq", "fsdp", None)
    dense = (gain_spec, row_spec, row_spec, gain_spec, row_spec, row_spec, gain_spec, row_spec, row_spec, row_spec)
    weights = dense + (expert_spec,) * 3
    return jax.shard_map(
        per_device,
        mesh=mesh,
        in_specs=(token_spec, row_spec, token_spec, token_spec, token_spec) + weights,
        out_specs=(token_spec, token_spec) + weights,
        check_vma=False,
    )
```

time: 2810 us -> 1280 us (0.46)
  waiting for transfers between devices: 1910 us -> 121 us
  Pallas kernels: 0 us -> 472 us
  other arithmetic: 235 us -> 156 us
  matrix products: 332 us -> 280 us
  starting transfers between devices: 64.5 us -> 30.4 us
    all_gather x10 -> x8, waiting for transfers between devices: 548 us -> 36.8 us  [the longest x1 36.7 us: per_device(): dlatent_all = lax.all_gather(dlatent, 'seq', axis=0, tiled=True)]
    pallas_call x0 -> x10, Pallas kernels: none -> 472 us  [the longest x4 262 us: ring_scatter(): pl.pallas_call(functools.partial(scatter_kernel, n, cut, w is not None),...]
    reduce_scatter x10 -> x0, waiting for transfers between devices: 465 us -> none  [the longest x1 147 us: per_device(): lax.psum_scatter(grad_query.astype(jnp.bfloat16), 'fsdp', scatter_dimensi...]
    psum x1 -> x0, waiting for transfers between devices: 462 us -> none  [per_device(): lax.psum(owned_grads[1].astype(jnp.bfloat16), 'seq').astype(jnp.float32)]
    all_to_all x10 -> x1, waiting for transfers between devices: 436 us -> 0.01 us  [per_device(): share_of = lax.all_to_all(spread.T, 'seq', 0, 0, tiled=True)]
    ppermute x0 -> x22, waiting for transfers between devices: none -> 84.4 us  [fsdp_pair(): return lax.ppermute(x, 'fsdp', [(0, 1), (1, 0)])]
    unnamed x9 -> x12, other arithmetic: 58.7 us -> 2.06 us
    all_to_all x10 -> x1, starting transfers between devices: 63.6 us -> 8.01 us  [per_device(): share_of = lax.all_to_all(spread.T, 'seq', 0, 0, tiled=True)]
  transfers between devices with their start and end apart: 31 -> 31, of which waited for: 20 -> 11; matrix products, arithmetic and copies ran while one was open for 25% -> 38% of each run, Pallas kernels for 0% -> 23%
where the time goes in v1:
time: 1280 us; the launch traced here: 1260 us
  Pallas kernels  472 us (37%)
  matrix products  280 us (22%)
  local copies, waits for them, and re-layouts  162 us (13%)
  other arithmetic  156 us (12%)
  waiting for transfers between devices  121 us (9%)
  starting transfers between devices  30.4 us (2%)
  blocking collectives  20.6 us (2%)
  between operations  16 us (1%)
    pallas_call x4, Pallas kernels, ring_scatter(): pl.pallas_call(functools.partial(scatter_kernel, n, cut, w is not None),...  262 us
    pallas_call x4, Pallas kernels, ring_gather(): pl.pallas_call(functools.partial(gather_kernel, n, pieces), out_shape=jax...  189 us
    dot_general x10, matrix products, mm(): return jnp.dot(a, b, preferred_element_type=F32)  93.1 us
    unnamed x187, local copies, waits for them, and re-layouts  90.2 us
    dot_general x8, matrix products, mm_nt(): lax.dot_general(a, b, (((1,), (1,)), ((), ())), preferred_element_type=F32)  89.3 us
    ppermute x22, waiting for transfers between devices, fsdp_pair(): return lax.ppermute(x, 'fsdp', [(0, 1), (1, 0)])  84.4 us
    dot_general x10, matrix products, mm_tn(): lax.dot_general(a, b, (((0,), (0,)), ((), ())), preferred_element_type=F32)  69.8 us
    all_gather x1, waiting for transfers between devices, per_device(): dlatent_all = lax.all_gather(dlatent, 'seq', axis=0, tiled=True)  36.7 us
  transfers between devices with their start and end apart: 31, of which 11 were waited for; matrix products, arithmetic and copies ran while one was open for 38% of the time, Pallas kernels for 23%

profile of v1, /device:TPU:9, one launch (start us, length us, event | category | flops | bytes accessed | tf_op | source)
XLA Modules:
  0.0 1258.4 jit_solution(16786840724952579173)
XLA Ops:
  22.1 8.0 all-to-all-start
  30.1 46.0 %ring_gather.4 = bf16[16,128,2048]{2,1,0:T(8,128)(2,1)} custom-call(bf16[128,2048]{1,0:T(8,128)(2,1)} %bitcast.209), custom_call_target="tpu_custom_call" | custom-call | bytes 184549376 | tf_op jit(solution)/shard_map/ring_gather/pallas_call | solution.py:136
  76.1 5.2 multiply_reduce_fusion
  97.1 45.3 %ring_gather.6 = bf16[16,128,2048]{2,1,0:T(8,128)(2,1)} custom-call(bf16[128,2048]{1,0:T(8,128)(2,1)} %bitcast.210), custom_call_target="tpu_custom_call" | custom-call | bytes 184549376 | tf_op jit(solution)/shard_map/ring_gather/pallas_call | solution.py:136
  142.9 8.8 fusion.3
  152.0 10.0 fusion.36
  162.5 8.0 fusion.4
  175.9 8.0 convolution_bitcast_fusion
  186.6 8.9 collective-permute-done.5
  207.4 6.9 fusion.14.refs_1_
  216.7 8.5 fusion.19
  232.6 9.5 attend.1
  242.1 55.9 %ring_scatter.4 = f32[128,2048]{1,0:T(8,128)} custom-call(bf16[2048,128]{1,0:T(8,128)(2,1)} %get-tuple-element.22.refs_0_, bf16[2048,128]{1,0:T(8,128)(2,1)} %fusion.60.refs_1_), custom_call_target="tpu_custom_call" | custom-call | bytes 184549376 | tf_op jit(solution)/shard_map/ring_scatter/pallas_call | solution.py:231
  301.5 47.4 %ring_gather.5 = bf16[16,128,2048]{2,1,0:T(8,128)(2,1)} custom-call(bf16[128,2048]{1,0:T(8,128)(2,1)} %multiply_convert_fusion.8.x_ref), custom_call_target="tpu_custom_call" | custom-call | bytes 184549376 | tf_op jit(solution)/shard_map/ring_gather/pallas_call | solution.py:136
  349.0 7.6 fusion.42
  358.4 9.3 multiply_convert_fusion.6
  367.7 9.8 fusion.41
  383.4 16.2 %fusion.9 = f32[1536,1408]{1,0:T(8,128)} fusion(bf16[1536,2048]{1,0:T(8,128)(2,1)} %fusion.4, bf16[704,2048]{1,0:T(8,128)(2,1)} %get-tuple-element.124, bf16[704,2048]{1,0:T(8,128)(2,1)S(1)} %get-tuple-element.123), kind=kOutput, calls=%fused_computation.39 | convolution fusion | flops 8869904384 | bytes 20709376 | tf_op jit(solution)/shard_map/dot_general | solution.py:50
  402.3 12.2 fusion.11
  419.5 22.3 %multiply_convert_fusion.2 = (bf16[1536,1408]{1,0:T(8,128)(2,1)}, bf16[1536,1408]{1,0:T(8,128)(2,1)}, bf16[1536,1408]{1,0:T(8,128)(2,1)}) fusion(f32[1536,1408]{1,0:T(8,128)} %fusion.9, f32[1536,1408]{1,0:T(8,128)} %fusion.11, bf16[1536,2048]{1,0:T(8,128)(2,1)} %bitcast.198, bf16[1024,1408]{1,0:T(8,128)(2,1)} %get-tuple-element.126, ...), kind=kOutput, calls=%fused_computation.14 | convolution fusion | flops 8902344704 | bytes 42336256 | tf_op jit(solution)/shard_map/dot_general | solution.py:42
  441.8 15.5 %fusion.10 = f32[1536,2048]{1,0:T(8,128)} fusion(bf16[1536,1408]{1,0:T(8,128)(2,1)} %get-tuple-element.115, bf16[1024,1408]{1,0:T(8,128)(2,1)} %copy-done.24, bf16[1024,1408]{1,0:T(8,128)(2,1)S(1)} %copy-done.23), kind=kOutput, calls=%fused_computation.40 | convolution fusion | flops 8869904384 | bytes 22675456 | tf_op jit(solution)/shard_map/dot_general | solution.py:50
  457.3 15.3 %add_convert_fusion = bf16[1536,2048]{1,0:T(8,128)(2,1)S(1)} fusion(f32[1536,2048]{1,0:T(8,128)} %fusion.10, bf16[1536,1408]{1,0:T(8,128)(2,1)} %get-tuple-element.114, bf16[1024,1408]{1,0:T(8,128)(2,1)} %get-tuple-element.126, bf16[1024,1408]{1,0:T(8,128)(2,1)} %get-tuple-element.125), kind=kOutput, calls=%fused_computation.11 | convolution fusion | flops 8876195840 | bytes 28966912 | tf_op jit(solution)/shard_map/dot_general | solution.py:50
  472.6 8.3 fusion.34
  480.8 16.2 %fusion = bf16[2048,2048]{1,0:T(8,128)(2,1)} fusion(f32[16,128,2048]{2,1,0:T(8,128)} %fusion.34, f32[2048,2048]{1,0:T(8,128)} %fusion.41, bf16[2048,176]{0,1:T(8,128)(2,1)} %get-tuple-element.129, bf16[1024,176]{1,0:T(8,128)(2,1)} %get-tuple-element.137, bf16[1024,176]{1,0:T(8,128)(2,1)} %get-tuple-element.136), kind=kOutput, calls=%fused_computation.1 | convolution fusion | flops 1490419712 | bytes 43384832 | tf_op jit(solution)/shard_map/dot_general | solution.py:50
  497.1 49.9 %ring_scatter.6 = f32[128,2048]{1,0:T(8,128)} custom-call(bf16[16,128,2048]{2,1,0:T(8,128)(2,1)} %bitcast.186), custom_call_target="tpu_custom_call" | custom-call | bytes 184549376 | tf_op jit(solution)/shard_map/ring_scatter/pallas_call | solution.py:231
  551.0 49.9 %ring_gather.7 = bf16[16,128,2048]{2,1,0:T(8,128)(2,1)} custom-call(bf16[128,2048]{1,0:T(8,128)(2,1)} %fusion.78.x_ref), custom_call_target="tpu_custom_call" | custom-call | bytes 184549376 | tf_op jit(solution)/shard_map/ring_gather/pallas_call | solution.py:136
  600.9 6.5 convolution_convert_fusion.5.do_ref
  607.4 11.9 attend_back.1
  623.4 64.5 %ring_scatter.7 = f32[128,2688]{1,0:T(8,128)} custom-call(bf16[2048,512]{1,0:T(8,128)(2,1)} %pad_maximum_fusion.10.refs_0_, bf16[2688,512]{1,0:T(8,128)(2,1)} %fusion.14.refs_1_), custom_call_target="tpu_custom_call" | custom-call | bytes 242221056 | tf_op jit(solution)/shard_map/ring_scatter/pallas_call | solution.py:231
  703.1 36.7 %all-gather.18.cloned.1.call-done = bf16[2048,576]{1,0:T(8,128)(2,1)} async-done(((bf16[128,576]{1,0:T(8,128)(2,1)}), bf16[2048,576]{1,0:T(8,128)(2,1)}) %all-gather.18.cloned.1.call-update) | async-done | bytes 2359312 | tf_op jit(solution)/shard_map/all_gather | solution.py:566
  749.3 5.3 fusion.87
  755.9 7.8 collective-permute-done.16
  765.6 5.3 fusion.88
  772.2 6.7 collective-permute-done.17
  779.9 5.3 fusion.83
  787.6 5.9 collective-permute-done.18
  795.8 5.2 fusion.82
  802.2 5.5 collective-permute-done.12
  814.5 7.4 collective-permute-done.15
  823.0 12.8 %fusion.86 = f32[1408,2048]{1,0:T(8,128)S(1)} fusion(bf16[1536,1408]{1,0:T(8,128)(2,1)} %get-tuple-element.116, bf16[1536,2048]{1,0:T(8,128)(2,1)} %fusion.4), kind=kOutput, calls=%fused_computation.222 | convolution fusion | flops 8858370048 | bytes 22151168 | tf_op jit(solution)/shard_map/dot_general | solution.py:46
  843.2 12.2 multiply_convert_fusion
  855.4 8.2 fusion.38
  863.6 12.3 fusion.84
  876.1 12.8 %fusion.85 = f32[2048,1408]{1,0:T(8,128)} fusion(bf16[1536,2048]{1,0:T(8,128)(2,1)S(1)} %bitcast.202, bf16[1536,1408]{1,0:T(8,128)(2,1)S(1)} %bitcast.231), kind=kOutput, calls=%fused_computation.221 | convolution fusion | flops 8858370048 | bytes 22151168 | tf_op jit(solution)/shard_map/dot_general | solution.py:46
  891.7 11.6 fusion.1
  903.3 91.3 %ring_scatter.5 = f32[128,2048]{1,0:T(8,128)} custom-call(bf16[16,128,2048]{2,1,0:T(8,128)(2,1)} %bitcast.185), custom_call_target="tpu_custom_call" | custom-call | bytes 184549376 | tf_op jit(solution)/shard_map/ring_scatter/pallas_call | solution.py:231
  994.7 5.1 dynamic-slice_convert_fusion.1
  1002.9 20.6 %all-gather.8 = f32[16,1,4608]{2,1,0:T(1,128)S(1)} all-gather(f32[1,1,4608]{2,1,0:T(1,128)S(1)} %reshape.266), channel_id=2, replica_groups=mesh['seq'=16,'fsdp'=2] {'seq'}, dimensions={0}, use_global_device_ids=true | all-gather | bytes 313344 | tf_op jit(solution)/shard_map/all_gather | solution.py:587
  1027.7 35.5 %collective-permute-done.11 = f32[4608]{0:T(1024)S(1)} collective-permute-done((f32[4608]{0:T(1024)S(1)}, f32[4608]{0:T(1024)S(1)}, u32[]{:S(2)}, u32[]{:S(2)}) %collective-permute-start.11) | collective-permute-done | bytes 18464 | tf_op jit(solution)/shard_map/ppermute | solution.py:248
  1064.5 7.6 add_bitcast_fusion
  1072.1 6.7 add_bitcast_fusion.2
  1091.4 8.4 convert_element_type.379
  1099.8 19.7 %copy.132 = f32[22,8,16,1024]{3,2,1,0:T(8,128)} copy(f32[22,8,16,1024]{3,1,2,0:T(8,128)} %bitcast.179) | data formatting | bytes 23068672
  1119.4 15.5 %copy.117 = f32[16,1024,2,88]{1,3,0,2:T(8,128)} copy(f32[16,1024,2,88]{1,0,3,2:T(8,128)} %bitcast.180) | data formatting | bytes 23068672 | tf_op jit(solution)/shard_map/convert_element_type | solution.py:582
  1135.0 12.0 copy.121
  1147.0 8.4 convert_element_type.380
  1155.3 19.6 %copy.133 = f32[22,8,16,1024]{3,2,1,0:T(8,128)} copy(f32[22,8,16,1024]{3,1,2,0:T(8,128)} %bitcast.182) | data formatting | bytes 23068672
  1174.9 15.6 %copy.118 = f32[16,1024,2,88]{1,3,0,2:T(8,128)} copy(f32[16,1024,2,88]{1,0,3,2:T(8,128)} %bitcast.183) | data formatting | bytes 23068672 | tf_op jit(solution)/shard_map/convert_element_type | solution.py:582
  1190.5 11.9 copy.122
  1202.5 8.7 convert_element_type.376
  1211.1 9.0 convert_element_type.377
  1220.1 11.8 copy.139
  1231.9 12.6 %copy.119 = f32[1024,3072]{1,0:T(8,128)} copy(f32[1024,3072]{0,1:T(8,128)} %bitcast.178) | data formatting | bytes 25165824
  1244.5 6.7 dynamic-slice_convert_fusion.3
  (345 shorter events, 162.8 us)
Async XLA Ops:
  9.3 133.2 %collective-permute-start = (bf16[1,2304]{1,0:T(2,128)(2,1)S(1)}, bf16[1,2304]{1,0:T(2,128)(2,1)S(1)}, u32[]{:S(2)}, u32[]{:S(2)}) collective-permute-start(bf16[1,2304]{1,0:T(2,128)(2,1)S(1)} %constant_dynamic-update-slice_fusion), channel_id=1, source_target_pairs={{0,1},{1,0},{2,3},{3,2},{4,5},{5,4},{6,7},{7,6},{8,9},{9,8},{10,11... | collective-permute-start | bytes 13832 | tf_op jit(solution)/shard_map/ppermute | solution.py:248
  13.0 185.1 %collective-permute-start.1 = (bf16[1024,192]{1,0:T(8,128)(2,1)}, bf16[1024,192]{1,0:T(8,128)(2,1)}, u32[]{:S(2)}, u32[]{:S(2)}) collective-permute-start(bf16[1024,192]{1,0:T(8,128)(2,1)} %dynamic-slice_convert_fusion.4), channel_id=1, source_target_pairs={{0,1},{1,0},{2,3},{3,2},{4,5},{5,4},{6,7},{7,6},{8,9},{9,8},{10,11... | collective-permute-start | bytes 1179656 | tf_op jit(solution)/shard_map/ppermute | solution.py:248
  14.2 156.3 %collective-permute-start.3 = (bf16[256,256]{1,0:T(8,128)(2,1)S(1)}, bf16[256,256]{1,0:T(8,128)(2,1)S(1)}, u32[]{:S(2)}, u32[]{:S(2)}) collective-permute-start(bf16[256,256]{1,0:T(8,128)(2,1)S(1)} %dynamic-slice_convert_fusion.16), channel_id=1, source_target_pairs={{0,1},{1,0},{2,3},{3,2},{4,5},{5,4},{6,7},{7,6},{8,9},{9,8},{10,11... | collective-permute-start | bytes 393224 | tf_op jit(solution)/shard_map/ppermute | solution.py:248
  18.3 196.9 %collective-permute-start.2 = (bf16[1024,576]{0,1:T(8,128)(2,1)}, bf16[1024,576]{0,1:T(8,128)(2,1)}, u32[]{:S(2)}, u32[]{:S(2)}) collective-permute-start(bf16[1024,576]{0,1:T(8,128)(2,1)} %convert_element_type.285), channel_id=1, source_target_pairs={{0,1},{1,0},{2,3},{3,2},{4,5},{5,4},{6,7},{7,6},{8,9},{9,8},{10,11... | collective-permute-start | bytes 3538952 | tf_op jit(solution)/shard_map/ppermute | solution.py:248
  20.2 194.2 %copy-start.26 = (bf16[128,2048]{0,1:T(8,128)(2,1)}, bf16[128,2048]{0,1:T(8,128)(2,1)S(1)}, u32[]{:S(2)}) copy-start(bf16[128,2048]{0,1:T(8,128)(2,1)S(1)} %copy.126) | copy-start | bytes 1572868
  20.2 194.2 %collective-permute-start.4 = (bf16[128,2048]{0,1:T(8,128)(2,1)S(1)}, bf16[128,2048]{0,1:T(8,128)(2,1)}, u32[]{:S(2)}, u32[]{:S(2)}) collective-permute-start(bf16[128,2048]{0,1:T(8,128)(2,1)S(1)} %copy.126), channel_id=1, source_target_pairs={{0,1},{1,0},{2,3},{3,2},{4,5},{5,4},{6,7},{7,6},{8,9},{9,8},{10,11... | collective-permute-start | bytes 1572872 | tf_op jit(solution)/shard_map/ppermute | solution.py:248
  22.1 129.7 %all-to-all-start = ((f32[16,1,128]{2,1,0:T(1,128)}), f32[16,1,128]{2,1,0:T(1,128)S(1)}, u32[]{:S(2)}, u32[]{:S(2)}) async-start(f32[16,1,128]{2,1,0:T(1,128)} %bitcast.8), calls=%async_computation | async-start | bytes 16384 | tf_op jit(solution)/shard_map/all_to_all | solution.py:436
  30.1 709.8 %all-gather.18.cloned.1.call-start = ((), (), s32[]{:S(2)}) async-start(), calls=%async_computation.1 | async-start | bytes 2785280 | tf_op jit(solution)/shard_map/all_gather | solution.py:566
  142.5 31.8 %collective-permute-start.7 = (bf16[88,2048]{1,0:T(8,128)(2,1)S(1)}, bf16[88,2048]{1,0:T(8,128)(2,1)}, u32[]{:S(2)}, u32[]{:S(2)}) collective-permute-start(bf16[88,2048]{1,0:T(8,128)(2,1)S(1)} %dynamic-slice_convert_fusion.9), channel_id=1, source_target_pairs={{0,1},{1,0},{2,3},{3,2},{4,5},{5,4},{6,7},{7,6},{8,9},{9,8},{10,11... | collective-permute-start | bytes 1081352 | tf_op jit(solution)/shard_map/ppermute | solution.py:248
  142.9 234.6 %copy-start.51 = (f32[1,8,2,128]{3,1,2,0:T(8,128)}, f32[1,8,2,128]{3,1,2,0:T(8,128)S(1)}, u32[]{:S(2)}) copy-start(f32[1,8,2,128]{3,1,2,0:T(8,128)S(1)} %copy.141) | copy-start | bytes 24580
  151.7 76.8 %copy-start.56 = (f32[1,2,2,128]{3,1,2,0:T(2,128)}, f32[1,2,2,128]{3,1,2,0:T(2,128)S(1)}, u32[]{:S(2)}) copy-start(f32[1,2,2,128]{3,1,2,0:T(2,128)S(1)} %copy.130) | copy-start | bytes 6148
  151.7 147.9 %copy-start.46 = (f32[1,8,2,128]{3,1,2,0:T(8,128)}, f32[1,8,2,128]{3,1,2,0:T(8,128)S(1)}, u32[]{:S(2)}) copy-start(f32[1,8,2,128]{3,1,2,0:T(8,128)S(1)} %copy.140) | copy-start | bytes 24580
  171.2 13.1 %collective-permute-start.6 = (bf16[1024,176]{1,0:T(8,128)(2,1)S(1)}, bf16[1024,176]{1,0:T(8,128)(2,1)S(1)}, u32[]{:S(2)}, u32[]{:S(2)}) collective-permute-start(bf16[1024,176]{1,0:T(8,128)(2,1)S(1)} %pad_maximum_fusion.22), channel_id=1, source_target_pairs={{0,1},{1,0},{2,3},{3,2},{4,5},{5,4},{6,7},{7,6},{8,9},{9,8},{10,11... | collective-permute-start | bytes 1081352 | tf_op jit(solution)/shard_map/ppermute | solution.py:248
  174.3 21.2 %collective-permute-start.5 = (bf16[1024,176]{1,0:T(8,128)(2,1)}, bf16[1024,176]{1,0:T(8,128)(2,1)S(1)}, u32[]{:S(2)}, u32[]{:S(2)}) collective-permute-start(bf16[1024,176]{1,0:T(8,128)(2,1)} %pad_maximum_fusion.21), channel_id=1, source_target_pairs={{0,1},{1,0},{2,3},{3,2},{4,5},{5,4},{6,7},{7,6},{8,9},{9,8},{10,11... | collective-permute-start | bytes 1081352 | tf_op jit(solution)/shard_map/ppermute | solution.py:248
  175.9 24.4 %slice-start.12 = ((s8[8388608]{0:T(1024)(128)(4,1)}), s8[4194304]{0:T(1024)(128)(4,1)S(1)}, s32[]{:S(2)}) async-start(s8[8388608]{0:T(1024)(128)(4,1)} %bitcast.205), calls=%async_computation.21 | async-start | bytes 8388608
  175.9 24.3 %slice-start.13 = ((s8[8388608]{0:T(1024)(128)(4,1)}), s8[4194304]{0:T(1024)(128)(4,1)S(1)}, s32[]{:S(2)}) async-start(s8[8388608]{0:T(1024)(128)(4,1)} %bitcast.205), calls=%async_computation.22 | async-start | bytes 8388608
  184.2 194.9 %collective-permute-start.10 = (bf16[704,2048]{1,0:T(8,128)(2,1)}, bf16[704,2048]{1,0:T(8,128)(2,1)}, u32[]{:S(2)}, u32[]{:S(2)}) collective-permute-start(bf16[704,2048]{1,0:T(8,128)(2,1)} %convert_bitcast_fusion.1), channel_id=1, source_target_pairs={{0,1},{1,0},{2,3},{3,2},{4,5},{5,4},{6,7},{7,6},{8,9},{9,8},{10,11... | collective-permute-start | bytes 8650760 | tf_op jit(solution)/shard_map/ppermute | solution.py:248
  186.6 162.3 %copy-start.10 = (bf16[1024,176]{1,0:T(8,128)(2,1)}, bf16[1024,176]{1,0:T(8,128)(2,1)S(1)}, u32[]{:S(2)}) copy-start(bf16[1024,176]{1,0:T(8,128)(2,1)S(1)} %get-tuple-element.138) | copy-start | bytes 1081348
  195.5 204.1 %collective-permute-start.9 = (bf16[1024,1408]{1,0:T(8,128)(2,1)}, bf16[1024,1408]{1,0:T(8,128)(2,1)}, u32[]{:S(2)}, u32[]{:S(2)}) collective-permute-start(bf16[1024,1408]{1,0:T(8,128)(2,1)} %convert_bitcast_fusion.2), channel_id=1, source_target_pairs={{0,1},{1,0},{2,3},{3,2},{4,5},{5,4},{6,7},{7,6},{8,9},{9,8},{10,11... | collective-permute-start | bytes 8650760 | tf_op jit(solution)/shard_map/ppermute | solution.py:248
  198.0 216.4 %collective-permute-start.8 = (bf16[1024,1408]{1,0:T(8,128)(2,1)}, bf16[1024,1408]{1,0:T(8,128)(2,1)}, u32[]{:S(2)}, u32[]{:S(2)}) collective-permute-start(bf16[1024,1408]{1,0:T(8,128)(2,1)} %convert_bitcast_fusion.3), channel_id=1, source_target_pairs={{0,1},{1,0},{2,3},{3,2},{4,5},{5,4},{6,7},{7,6},{8,9},{9,8},{10,11... | collective-permute-start | bytes 8650760 | tf_op jit(solution)/shard_map/ppermute | solution.py:248
  232.6 65.5 %copy-start.8 = (bf16[1,128,2048]{2,1,0:T(8,128)(2,1)S(1)}, bf16[1,128,2048]{2,1,0:T(8,128)(2,1)}, u32[]{:S(2)}) copy-start(bf16[1,128,2048]{2,1,0:T(8,128)(2,1)} %param.20) | copy-start | bytes 1572868
  299.6 49.4 %copy-start.58 = (f32[128]{0:T(128)}, f32[128]{0:T(128)S(1)}, u32[]{:S(2)}) copy-start(f32[128]{0:T(128)S(1)} %get-tuple-element.155) | copy-start | bytes 1540
  299.6 77.9 %copy-start.64 = (f32[128]{0:T(128)}, f32[128]{0:T(128)S(1)}, u32[]{:S(2)}) copy-start(f32[128]{0:T(128)S(1)} %get-tuple-element.154) | copy-start | bytes 1540
  301.5 47.5 %copy-start.11 = (bf16[1024,176]{1,0:T(8,128)(2,1)S(1)}, bf16[1024,176]{1,0:T(8,128)(2,1)}, u32[]{:S(2)}) copy-start(bf16[1024,176]{1,0:T(8,128)(2,1)} %get-tuple-element.139) | copy-start | bytes 1081348
  356.6 22.5 %slice-start = ((s8[5767168]{0:T(1024)(128)(4,1)}), s8[4194304]{0:T(1024)(128)(4,1)S(1)}, s32[]{:S(2)}) async-start(s8[5767168]{0:T(1024)(128)(4,1)} %bitcast.187), calls=%async_computation.9 | async-start | bytes 8388608
  358.4 43.9 %copy-start.3 = (bf16[16,96,2048]{2,1,0:T(8,128)(2,1)}, bf16[16,96,2048]{2,1,0:T(8,128)(2,1)S(1)}, u32[]{:S(2)}) copy-start(bf16[16,96,2048]{2,1,0:T(8,128)(2,1)S(1)} %convolution_convert_fusion.1) | copy-start | bytes 18874372
  358.4 20.7 %slice-start.1 = ((s8[5767168]{0:T(1024)(128)(4,1)}), s8[1572864]{0:T(1024)(128)(4,1)S(1)}, s32[]{:S(2)}) async-start(s8[5767168]{0:T(1024)(128)(4,1)} %bitcast.187), calls=%async_computation.10 | async-start | bytes 3145728
  379.1 20.4 %slice-start.4 = ((s8[5767168]{0:T(1024)(128)(4,1)}), s8[4194304]{0:T(1024)(128)(4,1)S(1)}, s32[]{:S(2)}) async-start(s8[5767168]{0:T(1024)(128)(4,1)} %bitcast.191), calls=%async_computation.13 | async-start | bytes 8388608
  383.4 16.2 %slice-start.5 = ((s8[5767168]{0:T(1024)(128)(4,1)}), s8[1572864]{0:T(1024)(128)(4,1)S(1)}, s32[]{:S(2)}) async-start(s8[5767168]{0:T(1024)(128)(4,1)} %bitcast.191), calls=%async_computation.14 | async-start | bytes 3145728
  419.5 22.3 %copy-start.23 = (bf16[1024,1408]{1,0:T(8,128)(2,1)S(1)}, bf16[1024,1408]{1,0:T(8,128)(2,1)}, u32[]{:S(2)}) copy-start(bf16[1024,1408]{1,0:T(8,128)(2,1)} %copy-done.22) | copy-start | bytes 8650756
  497.1 49.9 %copy-start.2 = (f32[128,2048]{1,0:T(8,128)S(1)}, f32[128,2048]{1,0:T(8,128)}, u32[]{:S(2)}) copy-start(f32[128,2048]{1,0:T(8,128)} %copy-done.1) | copy-start | bytes 3145732
  497.1 49.9 %copy-start.47 = (f32[1,8,2,128]{3,1,2,0:T(8,128)S(1)}, f32[1,8,2,128]{3,1,2,0:T(8,128)}, u32[]{:S(2)}) copy-start(f32[1,8,2,128]{3,1,2,0:T(8,128)} %copy-done.46) | copy-start | bytes 24580
  497.1 49.9 %copy-start.59 = (f32[128]{0:T(128)S(1)}, f32[128]{0:T(128)}, u32[]{:S(2)}) copy-start(f32[128]{0:T(128)} %copy-done.58) | copy-start | bytes 1540
  497.1 51.4 %copy-start.12 = (bf16[1,128,2048]{2,1,0:T(8,128)(2,1)S(1)}, bf16[1,128,2048]{2,1,0:T(8,128)(2,1)}, u32[]{:S(2)}) copy-start(bf16[1,128,2048]{2,1,0:T(8,128)(2,1)} %param.24) | copy-start | bytes 1572868
  551.0 49.9 %copy-start.27 = (bf16[128,2048]{0,1:T(8,128)(2,1)S(1)}, bf16[128,2048]{0,1:T(8,128)(2,1)}, u32[]{:S(2)}) copy-start(bf16[128,2048]{0,1:T(8,128)(2,1)} %copy-done.26) | copy-start | bytes 1572868
  619.3 69.4 %copy-start.34 = (f32[128,512]{1,0:T(8,128)S(1)}, f32[128,512]{1,0:T(8,128)}, u32[]{:S(2)}) copy-start(f32[128,512]{1,0:T(8,128)} %get-tuple-element.152) | copy-start | bytes 786436
  619.3 69.4 %copy-start.57 = (f32[1,2,2,128]{3,1,2,0:T(2,128)S(1)}, f32[1,2,2,128]{3,1,2,0:T(2,128)}, u32[]{:S(2)}) copy-start(f32[1,2,2,128]{3,1,2,0:T(2,128)} %copy-done.56) | copy-start | bytes 6148
  623.4 68.3 %copy-start.36 = (bf16[2048,256]{1,0:T(8,128)(2,1)S(1)}, bf16[2048,256]{1,0:T(8,128)(2,1)}, u32[]{:S(2)}) copy-start(bf16[2048,256]{1,0:T(8,128)(2,1)} %get-tuple-element.27) | copy-start | bytes 3145732
  623.4 68.3 %copy-start.61 = (f32[2048]{0:T(1024)S(1)}, f32[2048]{0:T(1024)}, u32[]{:S(2)}) copy-start(f32[2048]{0:T(1024)} %copy-done.60) | copy-start | bytes 24580
  690.9 48.9 %copy-start.39 = (bf16[128,512]{1,0:T(8,128)(2,1)}, bf16[128,512]{1,0:T(8,128)(2,1)S(1)}, u32[]{:S(2)}) copy-start(bf16[128,512]{1,0:T(8,128)(2,1)S(1)} %subtract_convert_fusion) | copy-start | bytes 393220
  691.7 392.0 %all-gather.24.cloned.1.call-start = ((), (), s32[]{:S(2)}) async-start(), calls=%async_computation.4 | async-start | bytes 2228224 | tf_op jit(solution)/shard_map/all_gather | solution.py:574
  695.5 4.3 collective-permute-start.14
  701.5 386.8 %all-gather.22.cloned.1.call-start = ((), (), s32[]{:S(2)}) async-start(), calls=%async_computation.3 | async-start | bytes 1392640 | tf_op jit(solution)/shard_map/all_gather | solution.py:574
  743.1 5.3 collective-permute-start.13
  749.3 342.1 %all-gather.28.cloned.1.call-start = ((), (), s32[]{:S(2)}) async-start(), calls=%async_computation.6 | async-start | bytes 6127616 | tf_op jit(solution)/shard_map/all_gather | solution.py:574
  754.7 9.0 collective-permute-start.16
  765.5 381.4 %all-gather.30.cloned.1.call-start = ((), (), s32[]{:S(2)}) async-start(), calls=%async_computation.7 | async-start | bytes 6127616 | tf_op jit(solution)/shard_map/all_gather | solution.py:574
  771.0 8.0 collective-permute-start.17
  779.8 422.6 %all-gather.32.cloned.1.call-start = ((), (), s32[]{:S(2)}) async-start(), calls=%async_computation.8 | async-start | bytes 6127616 | tf_op jit(solution)/shard_map/all_gather | solution.py:574
  786.4 7.2 collective-permute-start.18
  795.5 415.6 %all-gather.20.cloned.1.call-start = ((), (), s32[]{:S(2)}) async-start(), calls=%async_computation.2 | async-start | bytes 6684672 | tf_op jit(solution)/shard_map/all_gather | solution.py:574
  801.1 6.7 collective-permute-start.12
  808.6 435.9 %all-gather.26.cloned.1.call-start = ((), (), s32[]{:S(2)}) async-start(), calls=%async_computation.5 | async-start | bytes 8912896 | tf_op jit(solution)/shard_map/all_gather | solution.py:574
  813.4 8.6 collective-permute-start.15
  822.9 20.2 %copy-start.20 = (bf16[704,2048]{1,0:T(8,128)(2,1)S(1)}, bf16[704,2048]{1,0:T(8,128)(2,1)}, u32[]{:S(2)}) copy-start(bf16[704,2048]{1,0:T(8,128)(2,1)} %copy-done.19) | copy-start | bytes 8650756
  822.9 20.2 %copy-start.21 = (bf16[704,2048]{1,0:T(8,128)(2,1)S(1)}, bf16[704,2048]{1,0:T(8,128)(2,1)}, u32[]{:S(2)}) copy-start(bf16[704,2048]{1,0:T(8,128)(2,1)} %get-tuple-element.124) | copy-start | bytes 8650756
  840.2 23.4 %slice-start.10 = ((s8[6291456]{0:T(1024)(128)(4,1)}), s8[4194304]{0:T(1024)(128)(4,1)S(1)}, s32[]{:S(2)}) async-start(s8[6291456]{0:T(1024)(128)(4,1)} %bitcast.199), calls=%async_computation.19 | async-start | bytes 8388608
  842.2 21.4 %slice-start.11 = ((s8[6291456]{0:T(1024)(128)(4,1)}), s8[2097152]{0:T(1024)(128)(4,1)S(1)}, s32[]{:S(2)}) async-start(s8[6291456]{0:T(1024)(128)(4,1)} %bitcast.199), calls=%async_computation.20 | async-start | bytes 4194304
  842.2 222.3 %collective-permute-start.21 = (bf16[704,2048]{1,0:T(8,128)(2,1)}, bf16[704,2048]{1,0:T(8,128)(2,1)}, u32[]{:S(2)}, u32[]{:S(2)}) collective-permute-start(bf16[704,2048]{1,0:T(8,128)(2,1)} %dynamic-slice_convert_fusion), channel_id=1, source_target_pairs={{0,1},{1,0},{2,3},{3,2},{4,5},{5,4},{6,7},{7,6},{8,9},{9,8},{10,11... | collective-permute-start | bytes 8650760 | tf_op jit(solution)/shard_map/ppermute | solution.py:248
  855.4 20.7 %slice-start.17 = ((s8[4325376]{0:T(1024)(128)(4,1)}), s8[4194304]{0:T(1024)(128)(4,1)S(1)}, s32[]{:S(2)}) async-start(s8[4325376]{0:T(1024)(128)(4,1)} %bitcast.230), calls=%async_computation.26 | async-start | bytes 8388608
  890.8 181.3 %collective-permute-start.19 = (bf16[1024,1408]{1,0:T(8,128)(2,1)}, bf16[1024,1408]{1,0:T(8,128)(2,1)}, u32[]{:S(2)}, u32[]{:S(2)}) collective-permute-start(bf16[1024,1408]{1,0:T(8,128)(2,1)} %dynamic-slice_convert_fusion.2), channel_id=1, source_target_pairs={{0,1},{1,0},{2,3},{3,2},{4,5},{5,4},{6,7},{7,6},{8,9},{9,8},{10,11... | collective-permute-start | bytes 8650760 | tf_op jit(solution)/shard_map/ppermute | solution.py:248
  999.8 24.6 %copy-start.4 = (f32[128,2048]{1,0:T(8,128)S(1)}, f32[128,2048]{1,0:T(8,128)}, u32[]{:S(2)}) copy-start(f32[128,2048]{1,0:T(8,128)} %ring_scatter.6) | copy-start | bytes 3145732
  999.8 79.0 %collective-permute-start.20 = (bf16[1024,1408]{1,0:T(8,128)(2,1)}, bf16[1024,1408]{1,0:T(8,128)(2,1)}, u32[]{:S(2)}, u32[]{:S(2)}) collective-permute-start(bf16[1024,1408]{1,0:T(8,128)(2,1)} %dynamic-slice_convert_fusion.1), channel_id=1, source_target_pairs={{0,1},{1,0},{2,3},{3,2},{4,5},{5,4},{6,7},{7,6},{8,9},{9,8},{10,11... | collective-permute-start | bytes 8650760 | tf_op jit(solution)/shard_map/ppermute | solution.py:248
  1023.7 39.5 %collective-permute-start.11 = (f32[4608]{0:T(1024)S(1)}, f32[4608]{0:T(1024)S(1)}, u32[]{:S(2)}, u32[]{:S(2)}) collective-permute-start(f32[4608]{0:T(1024)S(1)} %reduce_sum.139), channel_id=1, source_target_pairs={{0,1},{1,0},{2,3},{3,2},{4,5},{5,4},{6,7},{7,6},{8,9},{9,8},{10,11... | collective-permute-start | bytes 55304 | tf_op jit(solution)/shard_map/ppermute | solution.py:248
  (52 other events, 422.8 us)
Sparse Core Ops, SparseCore 0:
  691.8 47.9 all-gather.17
  742.0 39.2 all-gather.23
  783.6 37.5 all-gather.21
  823.3 58.8 all-gather.27
  884.2 68.7 all-gather.29
  955.2 71.5 all-gather.31
  1029.5 61.0 all-gather.19
  1092.8 72.9 all-gather.25

commit v2 on v1

v2 whole, which is shorter than its diff:
```python
import functools
import math

import jax
import jax.numpy as jnp
import numpy as np
from jax import lax
from jax.experimental import pallas as pl
from jax.experimental.pallas import tpu as pltpu
from jax.sharding import PartitionSpec as P

HEADS = 16
NOPE = 128
ROPE = 64
QD = NOPE + ROPE
KV_RANK = 512
V_DIM = 128
TOP = 6
MOST = 96

EPS = 1e-06
NEG = -1e30
THETA = 10000.0
SCALE = 1.0 / math.sqrt(QD)
KV_END = 2 * NOPE + V_DIM
QK_END = KV_END + ROPE
MESH = pl.DeviceIdType.MESH
BF = jnp.bfloat16
F32 = jnp.float32
VMEM_LIMIT = 60 * 2**20
COST = pl.CostEstimate(flops=0, bytes_accessed=2**20, transcendentals=0)


def norm_scale(values):
    return lax.rsqrt(jnp.mean(values * values, axis=-1, keepdims=True) + EPS)


def norm_back(values, inverse, gradient):
    return inverse * gradient - values * inverse * inverse * inverse * jnp.mean(
        gradient * values, axis=-1, keepdims=True
    )


def mm(a, b):
    return jnp.dot(a, b, preferred_element_type=F32)


def mm_tn(a, b):
    return lax.dot_general(a, b, (((0,), (0,)), ((), ())), preferred_element_type=F32)


def mm_nt(a, b):
    return lax.dot_general(a, b, (((1,), (1,)), ((), ())), preferred_element_type=F32)


def rope_tables(length):
    places = np.arange(length, dtype=np.float32)
    frequency = np.power(np.float32(THETA), np.arange(ROPE // 2, dtype=np.float32) * np.float32(-2.0 / ROPE))
    angles = places[:, None] * frequency[None, :].astype(np.float32)
    angles = np.concatenate([angles, angles], axis=-1)
    return jnp.asarray(np.cos(angles), F32), jnp.asarray(np.sin(angles), F32)


def ring_place():
    me = lax.axis_index("seq")
    core, chip = me % 2, me // 2
    z, y = chip // 2, chip % 2
    half = lax.axis_size("seq") // 4
    return me, core, jnp.where(y == 0, z, 2 * half - 1 - z), 2 * half


def ring_seq(r, core, n):
    low = r < n // 2
    return (jnp.where(low, r, n - 1 - r) * 2 + jnp.where(low, 0, 1)) * 2 + core


def greet(devices, across=False):
    barrier = pltpu.get_barrier_semaphore()
    for device in devices:
        pl.semaphore_signal(barrier, inc=1, device_id={"seq": device}, device_id_type=MESH)
    if across:
        other = 1 - lax.axis_index("fsdp")
        pl.semaphore_signal(barrier, inc=1, device_id={"fsdp": other}, device_id_type=MESH)
    pl.semaphore_wait(barrier, len(devices) + across)


def swap_copies(gives, takes, sems):
    other = 1 - lax.axis_index("fsdp")
    return [
        pltpu.make_async_remote_copy(
            give, take, sems.at[i, 0], sems.at[i, 1], device_id={"fsdp": other}, device_id_type=MESH
        )
        for i, (give, take) in enumerate(zip(gives, takes))
    ]


def remote(src, dst, send, recv, device):
    return pltpu.make_async_remote_copy(src, dst, send, recv, device_id={"seq": device}, device_id_type=MESH)


def gather_kernel(n, cuts, actives, swaps, shared, *refs):
    count = len(cuts)
    total = count + swaps
    x_refs, give_refs = refs[:count], refs[count:total]
    o_refs, take_refs = refs[total : total + count], refs[total + count : 2 * total]
    own_sem, local_sem, swap_sems, hand_sem = refs[2 * total : 2 * total + 4]
    sems = refs[2 * total + 4 :]
    me, core, r, _ = ring_place()
    targets = (ring_seq((r + 1) % n, core, n), ring_seq((r + n - 1) % n, core, n))
    sibling = ring_seq(r, 1 - core, n)
    greet((*targets, sibling), swaps > 0)

    def half_of(ref, c):
        height = ref.shape[0] // 2
        return ref.at[pl.ds(pl.multiple_of(c * height, height), height), :]

    gives, takes = list(give_refs), list(take_refs)
    if shared is not None:
        gives[shared], takes[shared] = half_of(gives[shared], core), half_of(takes[shared], core)
    swapped = swap_copies(gives, takes, swap_sems)
    for copy in swapped:
        copy.start()

    def handed(c):
        half = half_of(take_refs[shared], c)
        return remote(half, half, hand_sem.at[0], hand_sem.at[1], sibling)

    def block(t, d, c):
        return ring_seq((r + (-t if d == 0 else t) + n) % n, c, n)

    def guarded(i, source, action):
        if actives[i] is None:
            action()
        else:
            pl.when(actives[i](source))(action)

    def parts_of(i):
        height = x_refs[i].shape[0] // (2 * cuts[i])
        for k in range(cuts[i]):
            for d in range(2):
                yield k, d, pl.ds((d * cuts[i] + k) * height, height)

    def onward(i, t, d, k, rows):
        at = o_refs[i].at[block(t, d, core), rows]
        source = x_refs[i].at[rows] if t == 0 else at
        return remote(source, at, sems[4 * i].at[t, d, k], sems[4 * i + 1].at[t, d, k], targets[d])

    def across(i, t, d, k, rows, c):
        at = o_refs[i].at[block(t, d, c), rows]
        return remote(at, at, sems[4 * i + 2].at[t - 1, d, k], sems[4 * i + 3].at[t - 1, d, k], sibling)

    def local(i):
        return pltpu.make_async_copy(x_refs[i], o_refs[i].at[me], local_sem.at[i])

    def own(i):
        return remote(x_refs[i], o_refs[i].at[me], own_sem.at[i, 0], own_sem.at[i, 1], sibling)

    for i in range(count):
        local(i).start()
        for k, d, rows in parts_of(i):
            guarded(i, me, lambda: onward(i, 0, d, k, rows).start())
        guarded(i, me, lambda: own(i).start())
    for t in range(n - 1):
        for i in range(count):
            for k, d, rows in parts_of(i):

                def step():
                    arriving = onward(i, t, d, k, rows)
                    arriving.wait_recv()
                    if t < n - 2:
                        onward(i, t + 1, d, k, rows).start()
                    across(i, t + 1, d, k, rows, core).start()

                guarded(i, block(t + 1, d, core), step)
    for i in range(count):
        local(i).wait()
        guarded(i, me, lambda: own(i).wait_send())
        guarded(i, sibling, lambda: own(i).wait_recv())
        for t in range(n - 1):
            for k, d, rows in parts_of(i):
                guarded(i, block(t, d, core), lambda: onward(i, t, d, k, rows).wait_send())
                guarded(i, block(t + 1, d, core), lambda: across(i, t + 1, d, k, rows, core).wait_send())
                guarded(i, block(t + 1, d, 1 - core), lambda: across(i, t + 1, d, k, rows, 1 - core).wait_recv())
    if shared is not None:
        swapped[shared].wait_recv()
        handed(core).start()
    for i, copy in enumerate(swapped):
        copy.wait_send()
        if i != shared:
            copy.wait_recv()
    if shared is not None:
        handed(core).wait_send()
        handed(1 - core).wait_recv()


def ring_gather_many(operands, collective_id, actives=None, swaps=(), shared=None):
    devices = lax.axis_size("seq")
    n = devices // 2
    cuts = [2 if x.shape[0] % 64 == 0 else 1 for x in operands]
    anywhere = pl.BlockSpec(memory_space=pl.ANY)
    sems = [pltpu.SemaphoreType.DMA((n - 1, 2, cut)) for cut in cuts for _ in range(4)]
    return pl.pallas_call(
        functools.partial(gather_kernel, n, cuts, actives or [None] * len(operands), len(swaps), shared),
        out_shape=[jax.ShapeDtypeStruct((devices, *x.shape), x.dtype) for x in operands]
        + [jax.ShapeDtypeStruct(x.shape, x.dtype) for x in swaps],
        in_specs=[anywhere] * (len(operands) + len(swaps)),
        out_specs=[anywhere] * (len(operands) + len(swaps)),
        scratch_shapes=[
            pltpu.SemaphoreType.DMA((len(operands), 2)),
            pltpu.SemaphoreType.DMA((len(operands),)),
            pltpu.SemaphoreType.DMA((max(1, len(swaps)), 2)),
            pltpu.SemaphoreType.DMA((2,)),
        ]
        + sems,
        compiler_params=pltpu.CompilerParams(collective_id=collective_id, has_side_effects=True),
        cost_estimate=COST,
        name="ring_gather",
    )(*operands, *swaps)


def ring_gather(x, collective_id, swaps=()):
    out, *taken = ring_gather_many([x], collective_id, None, swaps)
    return out.reshape(-1, x.shape[1]), taken


def scatter_kernel(n, cut, swaps, *refs):
    a_ref, w_ref = refs[:2]
    o_ref = refs[2 + swaps]
    stage, sibbuf, rbuf, sbuf, send, recv, fsend, frecv, swap_sems = refs[3 + 2 * swaps :]
    me, core, r, _ = ring_place()
    targets = (ring_seq((r + 1) % n, core, n), ring_seq((r + n - 1) % n, core, n))
    sibling = ring_seq(r, 1 - core, n)
    greet((*targets, sibling), swaps > 0)
    swapped = swap_copies(refs[2 : 2 + swaps], refs[3 + swaps : 3 + 2 * swaps], swap_sems)
    for copy in swapped:
        copy.start()
    height, columns = o_ref.shape
    spans = (pl.ds(0, cut), pl.ds(cut, columns - cut))

    def chip(t, d):
        return (r + (-t - 1 if d == 0 else t + 1) + n) % n

    def part(t, d, c):
        block = ring_seq(chip(t, d), c, n)
        rows = a_ref[pl.ds(block * height, height), :]
        return mm_nt(rows, w_ref[spans[d], :])

    def across(t, d):
        return remote(stage.at[t, :, spans[d]], sibbuf.at[t, :, spans[d]], fsend.at[t, d], frecv.at[t, d], sibling)

    def onward(t, d):
        return remote(sbuf.at[t, :, spans[d]], rbuf.at[t, :, spans[d]], send.at[t, d], recv.at[t, d], targets[d])

    def give(t, d):
        stage[t, :, spans[d]] = part(t, d, 1 - core).astype(BF)
        across(t, d).start()

    for d in range(2):
        give(0, d)
    for t in range(n):
        for d in range(2):
            if t < n - 1:
                give(t + 1, d)
            value = part(t, d, core)
            across(t, d).wait_recv()
            value = value + sibbuf[t, :, spans[d]].astype(F32)
            if t > 0:
                onward(t - 1, d).wait_recv()
                value = value + rbuf[t - 1, :, spans[d]].astype(F32)
            if t < n - 1:
                sbuf[t, :, spans[d]] = value.astype(BF)
                onward(t, d).start()
            else:
                o_ref[:, spans[d]] = value
    for t in range(n):
        for d in range(2):
            across(t, d).wait_send()
            if t < n - 1:
                onward(t, d).wait_send()
    for copy in swapped:
        copy.wait()


def ring_scatter(a, w, collective_id, swaps=()):
    devices = lax.axis_size("seq")
    n = devices // 2
    rows = a.shape[0] // devices
    columns = w.shape[0]
    cut = columns // 256 * 128
    vmem = pl.BlockSpec(memory_space=pltpu.VMEM)
    anywhere = [pl.BlockSpec(memory_space=pl.ANY)] * len(swaps)
    out, *taken = pl.pallas_call(
        functools.partial(scatter_kernel, n, cut, len(swaps)),
        out_shape=[jax.ShapeDtypeStruct((rows, columns), F32)] + [jax.ShapeDtypeStruct(x.shape, x.dtype) for x in swaps],
        in_specs=[vmem, vmem] + anywhere,
        out_specs=[vmem] + anywhere,
        scratch_shapes=[
            pltpu.VMEM((n, rows, columns), BF),
            pltpu.VMEM((n, rows, columns), BF),
            pltpu.VMEM((n - 1, rows, columns), BF),
            pltpu.VMEM((n - 1, rows, columns), BF),
        ]
        + [pltpu.SemaphoreType.DMA((n - 1, 2))] * 2
        + [pltpu.SemaphoreType.DMA((n, 2))] * 2
        + [pltpu.SemaphoreType.DMA((max(1, len(swaps)), 2))],
        compiler_params=pltpu.CompilerParams(
            collective_id=collective_id, has_side_effects=True, vmem_limit_bytes=VMEM_LIMIT
        ),
        cost_estimate=COST,
        name="ring_scatter",
    )(a, w, *swaps)
    return out, taken


def fsdp_gather(x, other=None):
    count = lax.axis_size("fsdp")
    if count != 2:
        return lax.all_gather(x, "fsdp", axis=0, tiled=True)
    first = lax.axis_index("fsdp") == 0
    return jnp.concatenate([jnp.where(first, x, other), jnp.where(first, other, x)], axis=0)


def fsdp_pick(x, owner, other):
    count = lax.axis_size("fsdp")
    if count != 2:
        return lax.dynamic_index_in_dim(lax.all_gather(x, "fsdp", axis=0), owner, 0, keepdims=False)
    return jnp.where(lax.axis_index("fsdp") == owner, x, other)


def fsdp_given(x):
    half = x.shape[0] // 2
    return lax.dynamic_slice_in_dim(x, (1 - lax.axis_index("fsdp")) * half, half, 0)


def fsdp_scatter(x, taken=None):
    if taken is None:
        return lax.psum_scatter(x.astype(BF), "fsdp", scatter_dimension=0, tiled=True).astype(F32)
    half = x.shape[0] // 2
    kept = lax.dynamic_slice_in_dim(x, lax.axis_index("fsdp") * half, half, 0)
    return kept.astype(F32) + taken.astype(F32)


def fsdp_sum(x, taken=None):
    return lax.psum(x, "fsdp") if taken is None else x + taken


def turn(values, cosine, sine):
    half = values.shape[-1] // 2
    turned = jnp.concatenate([-values[:, half:], values[:, :half]], axis=-1)
    return values * cosine + turned * sine


def turn_back(gradient, cosine, sine):
    half = gradient.shape[-1] // 2
    scaled = gradient * sine
    return gradient * cosine + jnp.concatenate([scaled[:, half:], -scaled[:, :half]], axis=-1)


def spans_of(length):
    step = length // 8
    for i in range(8):
        start = i * step
        yield start, step, max(0, start - (3 * step if i % 2 == 0 else 2 * step))


def allowed_of(seg_col, seg_row, start, step, low):
    width = start + step - low
    query = start + lax.broadcasted_iota(jnp.int32, (step, width), 0)
    key = low + lax.broadcasted_iota(jnp.int32, (step, width), 1)
    return (key <= query) & (seg_col[start : start + step, :] == seg_row[:, low : start + step])


def attend_block(start, step, low, qh_ref, kh_ref, v_ref, segc_ref, segr_ref, heads_ref, lse_ref):
    end = start + step
    scores = mm_nt(qh_ref[start:end, :], kh_ref[low:end, :]) * SCALE
    scores = jnp.where(allowed_of(segc_ref, segr_ref, start, step, low), scores, NEG)
    peak = jnp.max(scores, axis=-1, keepdims=True)
    raised = jnp.exp(scores - peak)
    total = jnp.sum(raised, axis=-1, keepdims=True)
    prob = (raised * (1.0 / total)).astype(BF)
    heads_ref[start:end, :] = mm(prob, v_ref[low:end, :]).astype(BF)
    lse_ref[start:end, :] = peak + jnp.log(total)


def weights_back(wb_ref, wq, we):
    width = wq.shape[0]
    rank = we.shape[0]
    wb_ref[:, :] = jnp.zeros(wb_ref.shape, BF)
    wb_ref[:width, :NOPE] = wq[:, :NOPE]
    wb_ref[:width, KV_END:QK_END] = wq[:, NOPE:]
    wb_ref[width : width + rank, NOPE:KV_END] = we[...]
    shape = (ROPE, 2 * ROPE)
    eye = lax.broadcasted_iota(jnp.int32, shape, 0) + ROPE == lax.broadcasted_iota(jnp.int32, shape, 1)
    wb_ref[width + rank : width + rank + ROPE, KV_END:] = eye.astype(F32).astype(BF)


def front_kernel(count, swaps, chunks, *refs):
    wq_parts, wl_parts, we_parts = refs[:count], refs[count : 2 * count], refs[2 * count : 3 * count]
    x_ref, gain_ref, lgain_ref, cos_ref, sin_ref, segc_ref, segr_ref = refs[3 * count : 3 * count + 7]
    refs = refs[3 * count + 7 :]
    gives, refs = refs[:swaps], refs[swaps:]
    act_ref, cn_ref, qh_ref, kh_ref, v_ref, heads_ref, lse_ref, wb_ref = refs[:8]
    takes, refs = refs[8 : 8 + swaps], refs[8 + swaps :]
    wq, wl, we, sems, swap_sems = refs
    i = pl.program_id(0)
    length = qh_ref.shape[0]
    step = length // chunks
    swapped = swap_copies(gives, takes, swap_sems) if swaps else []
    copies = [fill(p, w, sems.at[j]) for j, (p, w) in enumerate(((wq_parts, wq), (wl_parts, wl), (we_parts, we)))]
    start_first(copies)

    @pl.when(i == 0)
    def _():
        if swaps:
            greet((), True)
            for copy in swapped:
                copy.start()

    wait_first(copies)

    @pl.when(i < chunks)
    def _():
        rows = pl.ds(pl.multiple_of(i * step, step), step)
        x = x_ref[...].astype(F32)
        act_ref[...] = (x * norm_scale(x) * gain_ref[...]).astype(BF)
        cosine, sine = cos_ref[...], sin_ref[...]
        query = mm(act_ref[...], wq[...])
        qh_ref[rows, :NOPE] = query[:, :NOPE].astype(BF)
        qh_ref[rows, NOPE:] = turn(query[:, NOPE:].astype(BF).astype(F32), cosine, sine).astype(BF)
        latent = mm(act_ref[...], wl[...])
        comp = latent[:, :KV_RANK]
        cn_ref[...] = (comp * norm_scale(comp) * lgain_ref[...]).astype(BF)
        kh_ref[rows, NOPE:] = turn(latent[:, KV_RANK:].astype(BF).astype(F32), cosine, sine).astype(BF)
        kv = mm(cn_ref[...], we[...])
        kh_ref[rows, :NOPE] = kv[:, :NOPE].astype(BF)
        v_ref[rows, :] = kv[:, NOPE:].astype(BF)

    @pl.when(i == chunks)
    def _():
        for start, size, low in spans_of(length):
            attend_block(start, size, low, qh_ref, kh_ref, v_ref, segc_ref, segr_ref, heads_ref, lse_ref)
        weights_back(wb_ref, wq, we)
        for copy in swapped:
            copy.wait()


def front(pieces, x, gain, lgain, cosine, sine, seg_col, seg_row, swaps, collective_id):
    length, width = x.shape
    chunks = 4
    step = length // chunks
    count = len(pieces[0])
    vmem = pl.BlockSpec(memory_space=pltpu.VMEM)
    anywhere = pl.BlockSpec(memory_space=pl.ANY)

    def tile(columns):
        return pl.BlockSpec((step, columns), lambda i: (jnp.minimum(i, chunks - 1), 0))

    def held(rows, columns):
        return pl.BlockSpec((rows, columns), lambda i: (0, 0))

    full = lambda group: (group[0].shape[0] * count, group[0].shape[1])
    backs = (width + KV_RANK + 2 * ROPE, QK_END + ROPE)
    outs = [
        (tile(width), (length, width), BF),
        (tile(KV_RANK), (length, KV_RANK), BF),
        (held(length, QD), (length, QD), BF),
        (held(length, QD), (length, QD), BF),
        (held(length, V_DIM), (length, V_DIM), BF),
        (held(length, V_DIM), (length, V_DIM), BF),
        (held(length, 1), (length, 1), F32),
        (held(*backs), backs, BF),
    ]
    return pl.pallas_call(
        functools.partial(front_kernel, count, len(swaps), chunks),
        grid=(chunks + 1,),
        out_shape=[jax.ShapeDtypeStruct(shape, dtype) for _, shape, dtype in outs]
        + [jax.ShapeDtypeStruct(w.shape, w.dtype) for w in swaps],
        in_specs=[anywhere] * (3 * count) + [tile(width), vmem, vmem, tile(ROPE), tile(ROPE), vmem, vmem]
        + [anywhere] * len(swaps),
        out_specs=[spec for spec, _, _ in outs] + [anywhere] * len(swaps),
        scratch_shapes=[pltpu.VMEM(full(group), BF) for group in pieces]
        + [pltpu.SemaphoreType.DMA((3, count)), pltpu.SemaphoreType.DMA((max(1, len(swaps)), 2))],
        compiler_params=pltpu.CompilerParams(
            vmem_limit_bytes=VMEM_LIMIT, collective_id=collective_id, has_side_effects=len(swaps) > 0
        ),
        cost_estimate=COST,
        name="front",
    )(*sum(pieces, ()), x, gain, lgain, cosine, sine, seg_col, seg_row, *swaps)


def attend_back_kernel(
    qh_ref, kh_ref, v_ref, lse_ref, heads_ref, da_ref, wo_ref, cos_ref, sin_ref, segc_ref, segr_ref, back_ref, gout_ref, dk_acc, dv_acc
):
    dk_acc[...] = jnp.zeros_like(dk_acc)
    dv_acc[...] = jnp.zeros_like(dv_acc)
    for start, step, low in spans_of(qh_ref.shape[0]):
        end = start + step
        query = qh_ref[start:end, :]
        grad = mm_nt(da_ref[start:end, :], wo_ref[...]).astype(BF)
        keys = kh_ref[low:end, :]
        scores = mm_nt(query, keys) * SCALE
        allowed = allowed_of(segc_ref, segr_ref, start, step, low)
        prob = jnp.where(allowed, jnp.exp(scores - lse_ref[start:end, :]), 0.0)
        dv_acc[low:end, :] += mm_tn(prob.astype(BF), grad)
        dprob = mm_nt(grad, v_ref[low:end, :])
        delta = jnp.sum(prob * dprob, axis=-1, keepdims=True)
        dscore = (prob * (dprob - delta) * SCALE).astype(BF)
        dquery = mm(dscore, keys)
        back_ref[start:end, :NOPE] = dquery[:, :NOPE].astype(BF)
        turned = turn_back(dquery[:, NOPE:], cos_ref[start:end, :], sin_ref[start:end, :])
        back_ref[start:end, KV_END:QK_END] = turned.astype(BF)
        dk_acc[low:end, :] += mm_tn(dscore, query)
    back_ref[:, NOPE : 2 * NOPE] = dk_acc[:, :NOPE].astype(BF)
    back_ref[:, 2 * NOPE : KV_END] = dv_acc[...].astype(BF)
    back_ref[:, QK_END:] = turn_back(dk_acc[:, NOPE:], cos_ref[...], sin_ref[...]).astype(BF)
    gout_ref[...] = mm_tn(heads_ref[...], da_ref[...]).astype(BF)


def local_call(kernel, outs, scratch, name, *operands):
    vmem = pl.BlockSpec(memory_space=pltpu.VMEM)
    return pl.pallas_call(
        kernel,
        out_shape=[jax.ShapeDtypeStruct(shape, dtype) for shape, dtype in outs],
        in_specs=[vmem] * len(operands),
        out_specs=[vmem] * len(outs),
        scratch_shapes=scratch,
        compiler_params=pltpu.CompilerParams(vmem_limit_bytes=VMEM_LIMIT),
        cost_estimate=COST,
        name=name,
    )(*operands)


def fsdp_pieces(x, other):
    if lax.axis_size("fsdp") != 2:
        return (lax.all_gather(x, "fsdp", axis=0, tiled=True),)
    return (x, other)


def fill(pieces, dst, sems):
    if len(pieces) == 1:
        return [pltpu.make_async_copy(pieces[0], dst, sems.at[0])]
    part = lax.axis_index("fsdp")
    height = pieces[0].shape[0]
    starts = (part * height, (1 - part) * height)
    return [
        pltpu.make_async_copy(piece, dst.at[pl.ds(pl.multiple_of(start, height), height), :], sems.at[i])
        for i, (piece, start) in enumerate(zip(pieces, starts))
    ]


def picks(slot_ref, share_ref, b, most):
    slots = slot_ref[b]
    pick = slots == lax.broadcasted_iota(jnp.int32, (most, slots.shape[1]), 0)
    return pick.astype(BF), jnp.sum(jnp.where(pick, share_ref[b], 0.0), axis=-1, keepdims=True)


def hidden_spans(hidden):
    cut = -(-hidden // 256) * 128
    return ((0, cut), (cut, hidden))


def start_first(groups):
    @pl.when(pl.program_id(0) == 0)
    def _():
        for group in groups:
            for copy in group:
                copy.start()


def wait_first(groups):
    @pl.when(pl.program_id(0) == 0)
    def _():
        for group in groups:
            for copy in group:
                copy.wait()


def expert_in_kernel(count, most, swaps, *refs):
    wg_parts, wu_parts = refs[:count], refs[count : 2 * count]
    act_ref, slot_ref, share_ref, wsg_ref, wsu_ref = refs[2 * count : 2 * count + 5]
    gives, refs = refs[2 * count + 5 : 2 * count + 5 + swaps], refs[2 * count + 5 + swaps :]
    xe_ref, ge_ref, ue_ref, he_ref, sg_ref, su_ref, sh_ref = refs[:7]
    takes, (wg, wu, sems, swap_sems) = refs[7 : 7 + swaps], refs[7 + swaps :]
    swapped = swap_copies(gives, takes, swap_sems) if swaps else []
    if swaps:

        @pl.when(pl.program_id(0) == 0)
        def _():
            greet((), True)
            for copy in swapped:
                copy.start()

    copies = [fill(wg_parts, wg, sems.at[0]), fill(wu_parts, wu, sems.at[1])]
    start_first(copies)
    blocks, rows = slot_ref.shape[0], slot_ref.shape[2]
    for b in range(blocks):
        pick, _ = picks(slot_ref, share_ref, b, most)
        xe_ref[b * most : (b + 1) * most, :] = mm(pick, act_ref[b * rows : (b + 1) * rows, :]).astype(BF)
    act = act_ref[...]
    sg, su = mm(act, wsg_ref[...]), mm(act, wsu_ref[...])
    sg_ref[...] = sg
    su_ref[...] = su
    sh_ref[...] = (sg * jax.nn.sigmoid(sg) * su).astype(BF)
    wait_first(copies)
    for low, high in hidden_spans(wg.shape[1]):
        ge = mm(xe_ref[...], wg[:, low:high])
        ue = mm(xe_ref[...], wu[:, low:high])
        ge_ref[:, low:high] = ge
        ue_ref[:, low:high] = ue
        he_ref[:, low:high] = (ge * jax.nn.sigmoid(ge) * ue).astype(BF)
    if swaps:

        @pl.when(pl.program_id(0) == pl.num_programs(0) - 1)
        def _():
            for copy in swapped:
                copy.wait()


def expert_out_kernel(count, most, swaps, *refs):
    wd_parts = refs[:count]
    he_ref, slot_ref, share_ref, wsd_ref, sh_ref, y_ref, wd, sems, _ = refs[count:]
    copies = [fill(wd_parts, wd, sems.at[0])]
    start_first(copies)
    wait_first(copies)
    blocks, rows = slot_ref.shape[0], slot_ref.shape[2]
    z = mm(he_ref[...], wd[...]).astype(BF)
    for b in range(blocks):
        pick, share = picks(slot_ref, share_ref, b, most)
        ye = z[b * most : (b + 1) * most, :].astype(F32)
        ys = mm(sh_ref[b * rows : (b + 1) * rows, :], wsd_ref[...])
        y_ref[b * rows : (b + 1) * rows, :] = (ys + mm_tn(pick, (share * ye).astype(BF))).astype(BF)


def expert_back_kernel(count, most, swaps, *refs):
    wg_parts, wu_parts, wd_parts = refs[:count], refs[count : 2 * count], refs[2 * count : 3 * count]
    g_ref, slot_ref, share_ref, wsg_ref, wsu_ref, wsd_ref, ge_ref, ue_ref, sg_ref, su_ref = refs[3 * count : 3 * count + 10]
    dact_ref, dye_ref, dge_ref, due_ref, dsg_ref, dsu_ref = refs[3 * count + 10 : 3 * count + 16]
    wg, wu, wd, sems, _ = refs[3 * count + 16 :]
    copies = [fill(p, w, sems.at[i]) for i, (p, w) in enumerate(((wg_parts, wg), (wu_parts, wu), (wd_parts, wd)))]
    start_first(copies)
    blocks, rows = slot_ref.shape[0], slot_ref.shape[2]
    for b in range(blocks):
        pick, share = picks(slot_ref, share_ref, b, most)
        packed = mm(pick, g_ref[b * rows : (b + 1) * rows, :])
        dye_ref[b * most : (b + 1) * most, :] = (share * packed).astype(BF)
    dsh = mm_nt(g_ref[...], wsd_ref[...])
    sg, su = sg_ref[...], su_ref[...]
    sig = jax.nn.sigmoid(sg)
    dsg_ref[...] = (dsh * su * sig * (1.0 + sg * (1.0 - sig))).astype(BF)
    dsu_ref[...] = (dsh * sg * sig).astype(BF)
    wait_first(copies)
    for low, high in hidden_spans(wg.shape[1]):
        dhe = mm_nt(dye_ref[...], wd[low:high, :])
        ge, ue = ge_ref[:, low:high], ue_ref[:, low:high]
        sig = jax.nn.sigmoid(ge)
        dge_ref[:, low:high] = (dhe * ue * sig * (1.0 + ge * (1.0 - sig))).astype(BF)
        due_ref[:, low:high] = (dhe * ge * sig).astype(BF)
    dxe = (mm_nt(dge_ref[...], wg[...]) + mm_nt(due_ref[...], wu[...])).astype(BF)
    for b in range(blocks):
        pick, _ = picks(slot_ref, share_ref, b, most)
        block = slice(b * rows, (b + 1) * rows)
        shared = mm_nt(dsg_ref[block, :], wsg_ref[...]) + mm_nt(dsu_ref[block, :], wsu_ref[...])
        dact_ref[block, :] = (shared + mm_tn(pick, dxe[b * most : (b + 1) * most, :])).astype(BF)


def expert_call(kernel, name, pieces, most, steps, slot, share, whole, tiled, outs, swaps=(), collective_id=None):
    devices, rows = slot.shape[0], slot.shape[2]
    per = devices // steps
    anywhere = pl.BlockSpec(memory_space=pl.ANY)
    vmem = pl.BlockSpec(memory_space=pltpu.VMEM)

    def tile(total, columns):
        return pl.BlockSpec((total // steps, columns), lambda i: (i, 0))

    cut = pl.BlockSpec((per, 1, rows), lambda i: (i, 0, 0))
    count = len(pieces[0])
    full = lambda group: (group[0].shape[0] * count, group[0].shape[1])
    return pl.pallas_call(
        functools.partial(kernel, count, most, len(swaps)),
        grid=(steps,),
        out_shape=[jax.ShapeDtypeStruct((total, columns), dtype) for total, columns, dtype in outs]
        + [jax.ShapeDtypeStruct(x.shape, x.dtype) for x in swaps],
        in_specs=[anywhere] * (len(pieces) * count) + [tile(*tiled[0].shape), cut, cut] + [vmem] * len(whole)
        + [tile(*t.shape) for t in tiled[1:]]
        + [anywhere] * len(swaps),
        out_specs=[tile(total, columns) for total, columns, _ in outs] + [anywhere] * len(swaps),
        scratch_shapes=[pltpu.VMEM(full(group), BF) for group in pieces]
        + [pltpu.SemaphoreType.DMA((len(pieces), count)), pltpu.SemaphoreType.DMA((max(1, len(swaps)), 2))],
        compiler_params=pltpu.CompilerParams(
            vmem_limit_bytes=VMEM_LIMIT, collective_id=collective_id, has_side_effects=len(swaps) > 0
        ),
        cost_estimate=COST,
        name=name,
    )(*sum(pieces, ()), tiled[0], slot, share, *whole, *tiled[1:], *swaps)


def weight_grads_kernel(n, cut, *refs):
    xe_ref, dge_ref, due_ref, he_ref, dye_ref, act_ref, dsg_ref, dsu_ref, sh_ref, g_ref, part_ref = refs[:11]
    o_ref, gate_ref, up_ref, down_ref, sgate_ref, sup_ref, sdown_ref = refs[11:18]
    sibbuf, rbuf, sbuf, send, recv, fsend, frecv = refs[18:]
    t = pl.program_id(0)
    me, core, r, _ = ring_place()
    targets = (ring_seq((r + 1) % n, core, n), ring_seq((r + n - 1) % n, core, n))
    sibling = ring_seq(r, 1 - core, n)
    columns = o_ref.shape[1]
    spans = (pl.ds(0, cut), pl.ds(cut, columns - cut))

    def block(step, d, c):
        return ring_seq((r + (-step - 1 if d == 0 else step + 1) + n) % n, c, n)

    def across(step, d):
        source = part_ref.at[block(step, d, 1 - core), :, spans[d]]
        return remote(source, sibbuf.at[step, :, spans[d]], fsend.at[step, d], frecv.at[step, d], sibling)

    def onward(step, d):
        return remote(
            sbuf.at[step, :, spans[d]], rbuf.at[step, :, spans[d]], send.at[step, d], recv.at[step, d], targets[d]
        )

    @pl.when(t == 0)
    def _():
        greet((*targets, sibling))
        for step in range(n):
            for d in range(2):
                across(step, d).start()

    for d in range(2):
        across(t, d).wait_recv()

        def both():
            return part_ref[block(t, d, core), :, spans[d]].astype(F32) + sibbuf[t, :, spans[d]].astype(F32)

        @pl.when(t == 0)
        def _():
            sbuf[0, :, spans[d]] = both().astype(BF)
            onward(0, d).start()

        @pl.when((t > 0) & (t < n - 1))
        def _():
            onward(t - 1, d).wait_recv()
            sbuf[t, :, spans[d]] = (both() + rbuf[t - 1, :, spans[d]].astype(F32)).astype(BF)
            onward(t, d).start()

        @pl.when(t == n - 1)
        def _():
            onward(n - 2, d).wait_recv()
            o_ref[:, spans[d]] = both() + rbuf[n - 2, :, spans[d]].astype(F32)

    gate_ref[...] = mm_tn(xe_ref[...], dge_ref[...]).astype(BF)
    up_ref[...] = mm_tn(xe_ref[...], due_ref[...]).astype(BF)
    down_ref[...] = mm_tn(he_ref[...], dye_ref[...]).astype(BF)
    sgate_ref[...] = mm_tn(act_ref[...], dsg_ref[...]).astype(BF)
    sup_ref[...] = mm_tn(act_ref[...], dsu_ref[...]).astype(BF)
    sdown_ref[...] = mm_tn(sh_ref[...], g_ref[...]).astype(BF)

    @pl.when(t == n - 1)
    def _():
        for step in range(n):
            for d in range(2):
                across(step, d).wait_send()
                if step < n - 1:
                    onward(step, d).wait_send()


def weight_grads(xe, dge, due, he, dye, act, dsg, dsu, sh, g, part, collective_id):
    devices = lax.axis_size("seq")
    n = devices // 2
    length, columns = part.shape
    rows = length // devices
    cut = columns // 256 * 128

    def tile(x):
        return pl.BlockSpec((x.shape[0], x.shape[1] // n), lambda i: (0, i))

    def held(x):
        return pl.BlockSpec(memory_space=pltpu.VMEM)

    ff, units = dge.shape[1], dsg.shape[1]
    slab = columns // n
    down = lambda width: pl.BlockSpec((slab, width), lambda i: (i, 0))
    along = lambda height: pl.BlockSpec((height, slab), lambda i: (0, i))
    return pl.pallas_call(
        functools.partial(weight_grads_kernel, n, cut),
        grid=(n,),
        out_shape=[jax.ShapeDtypeStruct((rows, columns), F32)]
        + [
            jax.ShapeDtypeStruct(shape, BF)
            for shape in ((columns, ff), (columns, ff), (ff, columns), (columns, units), (columns, units), (units, columns))
        ],
        in_specs=[tile(xe), held(dge), held(due), held(he), tile(dye), tile(act), held(dsg), held(dsu), held(sh), tile(g)]
        + [held(part)],
        out_specs=[pl.BlockSpec((rows, columns), lambda i: (0, 0)), down(ff), down(ff), along(ff)]
        + [down(units), down(units), along(units)],
        scratch_shapes=[
            pltpu.VMEM((n, rows, columns), BF),
            pltpu.VMEM((n - 1, rows, columns), BF),
            pltpu.VMEM((n - 1, rows, columns), BF),
        ]
        + [pltpu.SemaphoreType.DMA((n - 1, 2))] * 2
        + [pltpu.SemaphoreType.DMA((n, 2))] * 2,
        compiler_params=pltpu.CompilerParams(
            collective_id=collective_id, has_side_effects=True, vmem_limit_bytes=VMEM_LIMIT
        ),
        cost_estimate=COST,
        name="weight_grads",
    )(xe, dge, due, he, dye, act, dsg, dsu, sh, g, part.reshape(devices, rows, columns))


def widen(stacked, parts, name):
    devices, rows, columns = stacked.shape
    share = columns // parts
    steps = 8

    def kernel(i_ref, o_ref):
        for p in range(parts):
            for d in range(devices):
                at = (p * devices + d) * share
                o_ref[:, at : at + share] = i_ref[d, :, p * share : (p + 1) * share].astype(F32)

    return pl.pallas_call(
        kernel,
        grid=(steps,),
        out_shape=jax.ShapeDtypeStruct((rows, devices * columns), F32),
        in_specs=[pl.BlockSpec((devices, rows // steps, columns), lambda i: (0, i, 0))],
        out_specs=pl.BlockSpec((rows // steps, devices * columns), lambda i: (i, 0)),
        compiler_params=pltpu.CompilerParams(vmem_limit_bytes=VMEM_LIMIT),
        cost_estimate=COST,
        name=name,
    )(stacked)


def columns_of(weight, at, width):
    return lax.dynamic_slice_in_dim(weight, at * width, width, 1).astype(BF)


def rows_of(weight, at, height):
    return lax.dynamic_slice_in_dim(weight, at * height, height, 0).astype(BF)


def per_device(
    tokens,
    segment_ids,
    routes,
    gate_weights,
    out_grad,
    attn_gain,
    q_weight,
    latent_weight,
    latent_gain,
    kv_weight,
    out_weight,
    ffn_gain,
    shared_gate,
    shared_up,
    shared_down,
    expert_gate,
    expert_up,
    expert_down,
):
    _, rows, width = tokens.shape
    devices = lax.axis_size("seq")
    at = lax.axis_index("seq")
    parts = lax.axis_size("fsdp")
    part = lax.axis_index("fsdp")
    length = rows * devices
    own_x = tokens[0]
    own_g = out_grad[0]

    per, per_latent = attn_gain.shape[0], latent_gain.shape[0]
    gains = jnp.concatenate([attn_gain, ffn_gain, latent_gain]).astype(BF)
    gains_size = gains.shape[0]
    gains_rows = -(-gains_size // 2048) * 16
    gains = jnp.pad(gains, (0, gains_rows * 128 - gains_size)).reshape(gains_rows, 128)
    out_rows = out_weight.shape[0]
    early_latent = 2
    early = (
        gains,
        columns_of(q_weight, at, QD),
        latent_weight.astype(BF),
        columns_of(kv_weight, at, NOPE + V_DIM),
        lax.dynamic_slice_in_dim(out_weight, at * V_DIM % out_rows, V_DIM, 0).astype(BF),
    )
    pair = parts == 2

    def crossing(*arrays):
        return arrays if pair else ()

    def crossed(taken, count):
        return taken if pair else [None] * count

    experts = jnp.arange(devices, dtype=jnp.int32)
    spread = jnp.sum(
        jnp.where(routes[0].T[None, :, :] == experts[:, None, None], gate_weights[0].T[None, :, :], 0.0), axis=1
    )
    x_all, spread_all, *others = ring_gather_many(
        [own_x, spread], 8, None, crossing(*early), early_latent if pair else None
    )
    x_all = x_all.reshape(length, width)
    share_of = lax.dynamic_index_in_dim(spread_all, at, 1, keepdims=False)
    others = crossed(others, len(early))
    gains = fsdp_gather(gains, others[0]).reshape(parts, -1)[:, :gains_size].astype(F32)
    gain_one = gains[:, :per].reshape(1, -1)
    gain_two = gains[:, per : 2 * per].reshape(1, -1)
    gain_lat = gains[:, 2 * per :].reshape(1, -1)
    w_latent = fsdp_gather(early[2], others[2])
    w_out = fsdp_pick(early[4], at * V_DIM // out_rows, others[4])

    hidden = shared_down.shape[0] * parts
    share = shared_down.shape[0] // devices

    def shared_columns(weight):
        pieces = [
            lax.dynamic_slice_in_dim(weight, p * (hidden // parts) + at * share, share, 1) for p in range(parts)
        ]
        return jnp.concatenate(pieces, axis=1).astype(BF)

    share_pad = -(-share // 32) * 32
    sgate, sup = shared_columns(shared_gate), shared_columns(shared_up)
    sdown = jnp.pad(rows_of(shared_down, at, share), ((0, share_pad - share), (0, 0)))
    egate, eup, edown = expert_gate[0].astype(BF), expert_up[0].astype(BF), expert_down[0].astype(BF)

    cosine, sine = rope_tables(length)
    seg_col, seg_row = segment_ids.reshape(length, 1), segment_ids
    act_one, cnorm, qh, kh, values, heads, lse, w_back, *taken = front(
        tuple(fsdp_pieces(early[i], others[i]) for i in (1, 2, 3)),
        x_all,
        gain_one,
        gain_lat,
        cosine,
        sine,
        seg_col,
        seg_row,
        crossing(sgate, sup, sdown),
        11 if pair else None,
    )
    sgate_other, sup_other, sdown_other = crossed(taken, 3)
    own_xf = own_x.astype(F32)
    attended, taken = ring_scatter(heads, w_out.T, 2, crossing(egate))
    (egate_other,) = crossed(taken, 1)
    x1 = own_xf + attended
    r3 = norm_scale(x1)
    act_two = (x1 * r3 * gain_two).astype(BF)
    act_all, taken = ring_gather(act_two, 9, crossing(eup))
    (eup_other,) = crossed(taken, 1)
    w_egate, w_eup = fsdp_pieces(egate, egate_other), fsdp_pieces(eup, eup_other)
    w_sgate, w_sup = fsdp_gather(sgate, sgate_other), fsdp_gather(sup, sup_other)
    late_g, act_all = lax.optimization_barrier((own_g, act_all))
    g_all = lax.all_gather(late_g, "seq", axis=0, tiled=True)

    most = min(MOST, rows)
    named = share_of > 0.0
    rank = jnp.cumsum(named.astype(jnp.int32), axis=1) - 1
    slot = jnp.where(named, rank, -1)[:, None, :]
    share_of = share_of[:, None, :]
    packed = devices * most
    ff = expert_gate.shape[2]
    units = parts * share
    steps = 4
    xe, ge, ue, he, sg, su, sh, *taken = expert_call(
        expert_in_kernel,
        "experts_in",
        (w_egate, w_eup),
        most,
        steps,
        slot,
        share_of,
        (w_sgate, w_sup),
        (act_all,),
        (
            (packed, width, BF),
            (packed, ff, F32),
            (packed, ff, F32),
            (packed, ff, BF),
            (length, units, F32),
            (length, units, F32),
            (length, units, BF),
        ),
        crossing(edown),
        10 if pair else None,
    )
    (edown_other,) = crossed(taken, 1)
    w_edown = fsdp_pieces(edown, edown_other)
    w_sdown = fsdp_gather(sdown[:share], sdown_other[:share] if pair else None)
    (y_part,) = expert_call(
        expert_out_kernel,
        "experts_out",
        (w_edown,),
        most,
        steps,
        slot,
        share_of,
        (w_sdown,),
        (he, sh),
        ((length, width, BF),),
    )
    y_sum = lax.psum_scatter(y_part, "seq", scatter_dimension=0, tiled=True).astype(F32)
    dact_part, dye, dge, due, dsg, dsu = expert_call(
        expert_back_kernel,
        "experts_back",
        (w_egate, w_eup, w_edown),
        most,
        steps,
        slot,
        share_of,
        (w_sgate, w_sup, w_sdown),
        (g_all, ge, ue, sg, su),
        (
            (length, width, BF),
            (packed, width, BF),
            (packed, ff, BF),
            (packed, ff, BF),
            (length, units, BF),
            (length, units, BF),
        ),
    )
    dact_two, grad_egate, grad_eup, grad_edown, grad_sgate, grad_sup, grad_sdown = weight_grads(
        xe, dge, due, he, dye, act_all, dsg, dsu, sh, g_all, dact_part, 3
    )
    own_gf = own_g.astype(F32)
    grad_gain_two = jnp.sum(dact_two * x1 * r3, axis=0)
    dx1 = own_gf + norm_back(x1, r3, dact_two * gain_two)
    sdown_given = jnp.pad(fsdp_given(grad_sdown), ((0, share_pad - share), (0, 0))) if pair else None
    dattn_all, taken = ring_gather(
        dx1.astype(BF), 1, crossing(fsdp_given(grad_sgate), fsdp_given(grad_sup), sdown_given) if pair else ()
    )
    sgate_taken, sup_taken, sdown_taken = crossed(taken, 3)
    grad_sgate = fsdp_scatter(grad_sgate, sgate_taken).astype(BF)
    grad_sup = fsdp_scatter(grad_sup, sup_taken).astype(BF)
    grad_sdown = fsdp_scatter(grad_sdown, sdown_taken[:share] if pair else None).astype(BF)
    output = (x1 + y_sum).astype(BF)

    back, grad_out = local_call(
        attend_back_kernel,
        [((length, QK_END + ROPE), BF), ((V_DIM, width), BF)],
        [pltpu.VMEM((length, QD), F32), pltpu.VMEM((length, V_DIM), F32)],
        "attend_back",
        qh,
        kh,
        values,
        lse,
        heads,
        dattn_all,
        w_out,
        cosine,
        sine,
        seg_col,
        seg_row,
    )
    grad_back = mm_tn(act_one, back).astype(BF)
    grad_query = jnp.concatenate([grad_back[:, :NOPE], grad_back[:, KV_END:QK_END]], 1)
    grad_expand = mm_tn(cnorm, back[:, NOPE:KV_END]).astype(BF)
    summed, taken = ring_scatter(back, w_back, 4, (fsdp_given(grad_edown),) if pair else ())
    grad_edown = fsdp_scatter(grad_edown, *taken)

    r1 = norm_scale(own_xf)
    own_act = (own_xf * r1 * gain_one).astype(BF)
    own_comp = mm(own_act, w_latent)[:, :KV_RANK]
    r2 = norm_scale(own_comp)
    dcn = summed[:, width : width + KV_RANK]
    grad_gain_lat = jnp.sum(dcn * own_comp * r2, axis=0)
    dcomp = norm_back(own_comp, r2, dcn * gain_lat)
    dlatent = jnp.concatenate([dcomp, summed[:, width + KV_RANK : width + KV_RANK + ROPE]], axis=-1).astype(BF)
    dact_one = summed[:, :width] + mm_nt(dlatent, w_latent)
    grad_gain_one = jnp.sum(dact_one * own_xf * r1, axis=0)
    input_grad = dx1 + norm_back(own_xf, r1, dact_one * gain_one)

    small = jnp.concatenate([grad_gain_one, grad_gain_two, grad_gain_lat])
    small = jnp.pad(small, (0, 64 * 128 - small.shape[0])).reshape(64, 128)

    def in_part(device):
        return device * V_DIM // out_rows == lax.axis_index("fsdp")

    gate_all, up_all, dlatent_all, *taken = ring_gather_many(
        [grad_sgate, grad_sup, dlatent],
        5,
        None,
        (fsdp_given(grad_query), fsdp_given(grad_expand), grad_out, small) if pair else (),
    )
    query_taken, expand_taken, out_taken, small_taken = crossed(taken, 4)
    grad_query = fsdp_scatter(grad_query, query_taken).astype(BF)
    grad_expand = fsdp_scatter(grad_expand, expand_taken).astype(BF)
    grad_out = fsdp_sum(grad_out, out_taken)
    small = fsdp_sum(small, small_taken)
    slab = width // parts // devices
    act_cols = jnp.concatenate(
        [lax.dynamic_slice_in_dim(act_one, p * (width // parts) + at * slab, slab, 1) for p in range(parts)], axis=1
    )
    grad_latent = mm_tn(act_cols, dlatent_all.reshape(length, -1)).astype(BF)
    sdown_pad = jnp.pad(grad_sdown, ((0, share_pad - share), (0, 0)))
    query_all, sdown_all, *taken = ring_gather_many(
        [grad_query, sdown_pad], 6, None, (fsdp_given(grad_latent), fsdp_given(grad_egate)) if pair else ()
    )
    latent_taken, egate_taken = crossed(taken, 2)
    grad_latent = fsdp_scatter(grad_latent, latent_taken).astype(BF)
    grad_egate = fsdp_scatter(grad_egate, egate_taken)
    latent_pad = -(-slab // 32) * 32
    out_all, expand_all, latent_all, small_all, *taken = ring_gather_many(
        [grad_out, grad_expand, jnp.pad(grad_latent, ((0, latent_pad - slab), (0, 0))), small],
        7,
        [in_part, None, None, None],
        (fsdp_given(grad_eup),) if pair else (),
    )
    (eup_taken,) = crossed(taken, 1)
    grad_eup = fsdp_scatter(grad_eup, eup_taken)
    latent_all = latent_all[:, :slab]
    out_grad_own = lax.dynamic_slice_in_dim(
        out_all.reshape(devices * V_DIM, width), part * out_rows, out_rows, 0
    ).astype(F32)
    small = jnp.sum(small_all, axis=0).reshape(-1)
    gain_rows = width // parts
    own_gains = [
        lax.dynamic_slice_in_dim(small, part * gain_rows, gain_rows),
        lax.dynamic_slice_in_dim(small, width + part * gain_rows, gain_rows),
        lax.dynamic_slice_in_dim(small, 2 * width + part * (KV_RANK // parts), KV_RANK // parts),
    ]
    return (
        output[None],
        input_grad[None],
        own_gains[0],
        widen(query_all, 1, "wide_q"),
        latent_all.reshape(-1, grad_latent.shape[1]).astype(F32),
        own_gains[2],
        widen(expand_all, 1, "wide_kv"),
        out_grad_own,
        own_gains[1],
        widen(gate_all, parts, "wide_gate"),
        widen(up_all, parts, "wide_up"),
        sdown_all[:, :share].reshape(-1, width).astype(F32),
        grad_egate[None],
        grad_eup[None],
        grad_edown[None],
    )


def solution(mesh):
    token_spec = P("fsdp", "seq", None)
    row_spec = P("fsdp", None)
    gain_spec = P("fsdp")
    expert_spec = P("seq", "fsdp", None)
    dense = (gain_spec, row_spec, row_spec, gain_spec, row_spec, row_spec, gain_spec, row_spec, row_spec, row_spec)
    weights = dense + (expert_spec,) * 3
    return jax.shard_map(
        per_device,
        mesh=mesh,
        in_specs=(token_spec, row_spec, token_spec, token_spec, token_spec) + weights,
        out_specs=(token_spec, token_spec) + weights,
        check_vma=False,
    )
```

time: 1280 us -> 1050 us (0.82); the launches traced: 1260 us -> 1040 us
  Pallas kernels: 472 us -> 876 us
  matrix products: 280 us -> 18.3 us
  waiting for transfers between devices: 121 us -> 0.04 us
  local copies, waits for them, and re-layouts: 162 us -> 53.9 us
  other arithmetic: 156 us -> 78.4 us
  starting transfers between devices: 30.4 us -> 0.08 us
  blocking collectives: 20.6 us -> 0 us
    pallas_call x8 -> x17, Pallas kernels: 450 us -> 857 us  [the longest x6 406 us: ring_gather_many(): pl.pallas_call(functools.partial(gather_kernel, n, cuts, actives or [None...]
    dot_general x10 -> x1, matrix products: 93.1 us -> 2.11 us  [mm(): return jnp.dot(a, b, preferred_element_type=F32)]
    dot_general x8 -> x1, matrix products: 89.3 us -> 4.77 us  [mm_nt(): lax.dot_general(a, b, (((1,), (1,)), ((), ())), preferred_element_type=F32)]
    ppermute x22 -> x0, waiting for transfers between devices: 84.4 us -> none  [fsdp_pair(): return lax.ppermute(x, 'fsdp', [(0, 1), (1, 0)])]
    unnamed x187 -> x117, local copies, waits for them, and re-layouts: 90.2 us -> 9.91 us
    dot_general x10 -> x3, matrix products: 69.8 us -> 11.5 us  [mm_tn(): lax.dot_general(a, b, (((0,), (0,)), ((), ())), preferred_element_type=F32)]
    convert_element_type x15 -> x1, local copies, waits for them, and re-layouts: 57.9 us -> 2.08 us  [per_device(): lax.dynamic_slice_in_dim(out_weight, at * V_DIM % out_rows, V_DIM, 0)]
    convert_element_type x19 -> x14, other arithmetic: 78.9 us -> 32.2 us  [the longest x1 7.44 us: per_device(): expert_up[0].astype(BF)]
  transfers between devices with their start and end apart: 31 -> 2, of which waited for: 11 -> 0; matrix products, arithmetic and copies ran while one was open for 38% -> 10% of each run, Pallas kernels for 23% -> 63%
where the time goes in v2:
time: 1050 us; the launch traced here: 1040 us
  Pallas kernels  876 us (83%)
  other arithmetic  78.4 us (7%)
  local copies, waits for them, and re-layouts  53.9 us (5%)
  matrix products  18.3 us (2%)
  between operations  15 us (1%)
    pallas_call x6, Pallas kernels, ring_gather_many(): pl.pallas_call(functools.partial(gather_kernel, n, cuts, actives or [None...  406 us
    pallas_call x3, Pallas kernels, expert_call(): pl.pallas_call(functools.partial(kernel, count, most, len(swaps)), grid=(...  158 us
    pallas_call x2, Pallas kernels, ring_scatter(): pl.pallas_call(functools.partial(scatter_kernel, n, cut, len(swaps)), out...  136 us
    pallas_call x1, Pallas kernels, weight_grads(): pl.pallas_call(functools.partial(weight_grads_kernel, n, cut), grid=(n,),...  79.6 us
    pallas_call x1, Pallas kernels, front(): pl.pallas_call(functools.partial(front_kernel, count, len(swaps), chunks)...  39.4 us
    pallas_call x4, Pallas kernels, widen(): pl.pallas_call(kernel, grid=(steps,), out_shape=jax.ShapeDtypeStruct((row...  38.1 us
  transfers between devices with their start and end apart: 2, of which 0 were waited for; matrix products, arithmetic and copies ran while one was open for 10% of the time, Pallas kernels for 63%

profile of v2, /device:TPU:9, one launch (start us, length us, event | category | flops | bytes accessed | tf_op | source)
XLA Modules:
  0.0 1041.5 jit_solution(13669381883646978020)
XLA Ops:
  10.7 2.7 copy.53.refs_4_.refs_2_
  13.4 2.4 dynamic-slice_convert_fusion.2.refs_3_.refs_0_
  16.4 1.6 dynamic-slice_convert_fusion.8.refs_5_.refs_4_
  18.0 2.1 dynamic-slice_convert_fusion.1.refs_6_
  20.7 50.0 %ring_gather.6 = (bf16[16,128,2048]{2,1,0:T(8,128)(2,1)}, f32[16,16,128]{2,1,0:T(8,128)}, bf16[32,128]{1,0:T(8,128)(2,1)}, bf16[1024,192]{1,0:T(8,128)(2,1)}, bf...) custom-call(bf16[128,2048]{1,0:T(8,128)(2,1)} %bitcast.108, ...), custom_call_target="tpu_custom_call" | custom-call | bytes 1048576 | tf_op jit(solution)/shard_map/ring_gather/pallas_call | solution.py:202
  72.8 1.3 copy.54.refs_11_.segc_ref
  74.1 1.8 dynamic-slice_convert_fusion.7
  75.9 1.9 dynamic-slice_convert_fusion.5
  77.8 1.5 broadcast_select_fusion.6.wo_ref
  79.3 1.0 copy.55.refs_1_
  80.3 1.0 pad_maximum_fusion.3.refs_13_
  81.3 1.0 pad_maximum_fusion.4.refs_14_
  82.4 1.1 dynamic-slice_convert_fusion.3
  84.3 7.4 convert_bitcast_fusion
  91.7 39.4 %front.1 = (bf16[2048,2048]{1,0:T(8,128)(2,1)}, bf16[2048,512]{1,0:T(8,128)(2,1)}, bf16[2048,192]{1,0:T(8,128)(2,1)}, bf16[2048,192]{1,0:T(8,128)(2,1)}, bf16[20...) custom-call(bf16[1024,192]{1,0:T(8,128)(2,1)} %dynamic-slice_convert, ...), custom_call_target="tpu_custom_call" | custom-call | bytes 1048576 | tf_op jit(solution)/shard_map/front/pallas_call | solution.py:473
  131.2 67.1 %ring_scatter.2 = (f32[128,2048]{1,0:T(8,128)}, bf16[1024,1408]{1,0:T(8,128)(2,1)}) custom-call(bf16[2048,128]{1,0:T(8,128)(2,1)} %get-tuple-element.89.refs_0_.heads_ref, bf16[2048,128]{1,0:T(8,128)(2,1)} %copy.55.refs_1_, bf16[1024,1408]{1,0:T(8,128)(2,1)} %get-tuple-element.240.refs_2_.refs_0_), custom_call_target="tpu_custom_call" | custom-call | bytes 1048576 | tf_op jit(solution)/shard_map/ring_scatter/pallas_call | solution.py:292
  198.3 1.5 multiply_reduce_fusion.2
  200.8 65.0 %ring_gather.7 = (bf16[16,128,2048]{2,1,0:T(8,128)(2,1)}, bf16[1024,1408]{1,0:T(8,128)(2,1)}) custom-call(bf16[128,2048]{1,0:T(8,128)(2,1)} %multiply_convert_fusion.refs_0_, bf16[1024,1408]{1,0:T(8,128)(2,1)} %get-tuple-element.239.refs_1_.refs_2_), custom_call_target="tpu_custom_call" | custom-call | bytes 1048576 | tf_op jit(solution)/shard_map/ring_gather/pallas_call | solution.py:202
  267.7 2.2 broadcast_select_fusion.3
  270.0 1.2 pad_maximum_fusion.refs_7_.refs_9_
  271.2 1.1 pad_maximum_fusion.1.refs_8_.refs_10_
  272.3 2.0 convert_bitcast_fusion.1.refs_9_.refs_0_.refs_4_
  274.3 68.9 %experts_in.1 = (bf16[1536,2048]{1,0:T(8,128)(2,1)}, f32[1536,1408]{1,0:T(8,128)}, f32[1536,1408]{1,0:T(8,128)}, bf16[1536,1408]{1,0:T(8,128)(2,1)}, f32[2048,17...) custom-call(bf16[1024,1408]{1,0:T(8,128)(2,1)} %get-tuple-element.240.refs_2_.refs_0_, ...), custom_call_target="tpu_custom_call" | custom-call | bytes 1048576 | tf_op jit(solution)/shard_map/experts_in/pallas_call | solution.py:678
  343.2 1.2 broadcast_select_fusion.8
  345.4 20.7 %experts_out.1 = bf16[2048,2048]{1,0:T(8,128)(2,1)} custom-call(bf16[704,2048]{1,0:T(8,128)(2,1)} %convert_bitcast_fusion.1.refs_9_.refs_0_.refs_4_, bf16[704,2048]{1,0:T(8,128)(2,1)} %get-tuple-element.99.refs_1_.refs_5_, bf16[1536,1408]{1,0:T(8,128)(2,1)} %get-tuple-element.100.refs_2_.refs_3_, ...), custom_call_target="tpu_custom_call" | custom-call | bytes 1048576 | tf_op jit(solution)/shard_map/experts_out/pallas_call | solution.py:678
  366.1 1.3 copy-done
  367.4 3.0 broadcast_select_fusion.1
  370.5 2.1 multiply_reduce_fusion.5
  372.6 2.6 constant_dynamic-slice_fusion.4
  375.2 68.0 %experts_back.1 = (bf16[2048,2048]{1,0:T(8,128)(2,1)}, bf16[1536,2048]{1,0:T(8,128)(2,1)}, bf16[1536,1408]{1,0:T(8,128)(2,1)}, bf16[1536,1408]{1,0:T(8,128)(2,1)...) custom-call(bf16[1024,1408]{1,0:T(8,128)(2,1)} %get-tuple-element.240.refs_2_.refs_0_, ...), custom_call_target="tpu_custom_call" | custom-call | bytes 1048576 | tf_op jit(solution)/shard_map/experts_back/pallas_call | solution.py:678
  443.3 79.6 %weight_grads.1 = (f32[128,2048]{1,0:T(8,128)}, bf16[2048,1408]{1,0:T(8,128)(2,1)}, bf16[2048,1408]{1,0:T(8,128)(2,1)}, bf16[1408,2048]{1,0:T(8,128)(2,1)}, bf16...) custom-call(bf16[1536,2048]{1,0:T(8,128)(2,1)} %get-tuple-element.103.refs_0_, ...), custom_call_target="tpu_custom_call" | custom-call | bytes 1048576 | tf_op jit(solution)/shard_map/weight_grads/pallas_call | solution.py:782
  522.9 1.1 constant_dynamic-slice_fusion.7
  524.8 1.9 constant_dynamic-slice_fusion.9.refs_1_
  526.7 1.9 constant_dynamic-slice_fusion.8.refs_2_
  528.9 1.2 fusion.45.refs_0_
  530.1 47.3 %ring_gather.8 = (bf16[16,128,2048]{2,1,0:T(8,128)(2,1)}, bf16[1024,176]{1,0:T(8,128)(2,1)}, bf16[1024,176]{1,0:T(8,128)(2,1)}, bf16[96,2048]{1,0:T(8,128)(2,1)}) custom-call(bf16[128,2048]{1,0:T(8,128)(2,1)} %fusion.45.refs_0_, bf16[1024,176]{1,0:T(8,128)(2,1)} %constant_dynamic-slice_fusion.9.refs_1_, ...), custom_call_target="tpu_custom_call" | custom-call | bytes 1048576 | tf_op jit(solution)/shard_map/ring_gather/pallas_call | solution.py:202
  577.3 18.9 %attend_back.1 = (bf16[2048,512]{1,0:T(8,128)(2,1)}, bf16[128,2048]{1,0:T(8,128)(2,1)}) custom-call(bf16[2048,192]{1,0:T(8,128)(2,1)} %get-tuple-element.116.qh_ref, bf16[2048,192]{1,0:T(8,128)(2,1)} %get-tuple-element.117.kh_ref, bf16[2048,128]{1,0:T(8,128)(2,1)} %get-tuple-element.118.v_ref, f32[2048,1]{1,0:T(8,128)} %get-tuple-element.119.lse_ref, ...), custom_call_target="tpu_custom_call" | custom-call | bytes 1048576 | tf_op jit(solution)/shard_map/attend_back/pallas_call | solution.py:521
  596.3 8.5 convolution_convert_fusion
  605.0 4.0 constant_dynamic-slice_fusion.6.refs_2_
  608.9 68.8 %ring_scatter.3 = (f32[128,2688]{1,0:T(8,128)}, bf16[704,2048]{1,0:T(8,128)(2,1)}) custom-call(bf16[2048,512]{1,0:T(8,128)(2,1)} %get-tuple-element.124.refs_0_, bf16[2688,512]{1,0:T(8,128)(2,1)} %get-tuple-element.125.refs_1_, bf16[704,2048]{1,0:T(8,128)(2,1)} %constant_dynamic-slice_fusion.6.refs_2_), custom_call_target="tpu_custom_call" | custom-call | bytes 1048576 | tf_op jit(solution)/shard_map/ring_scatter/pallas_call | solution.py:292
  678.6 1.1 multiply_reduce_fusion.3
  679.7 1.1 subtract_convert_fusion
  680.8 4.8 fusion.22
  691.1 99.9 %ring_gather.9 = (bf16[16,1024,176]{2,1,0:T(8,128)(2,1)}, bf16[16,1024,176]{2,1,0:T(8,128)(2,1)}, bf16[16,128,576]{2,1,0:T(8,128)(2,1)}, bf16[1024,192]{1,0:T(8,...) custom-call(bf16[1024,176]{1,0:T(8,128)(2,1)} %add_convert_fusion.2.refs_0_, ...), custom_call_target="tpu_custom_call" | custom-call | bytes 1048576 | tf_op jit(solution)/shard_map/ring_gather/pallas_call | solution.py:202
  791.1 2.3 add.215.refs_0_
  793.4 1.2 add_convert_fusion.4
  795.4 2.2 convolution_convert_fusion.2
  799.2 3.6 constant_dynamic-slice_fusion.1.refs_3_
  802.8 75.5 %ring_gather.10 = (bf16[16,1024,192]{2,1,0:T(8,128)(2,1)}, bf16[16,96,2048]{2,1,0:T(8,128)(2,1)}, bf16[64,576]{1,0:T(8,128)(2,1)}, bf16[1024,1408]{1,0:T(8,128)(2,1)}) custom-call(bf16[1024,192]{1,0:T(8,128)(2,1)} %add_convert_fusion.refs_0_, bf16[96,2048]{1,0:T(8,128)(2,1)} %pad.22.refs_1_, bf16[64,576]{1,0:T(8,128)(2,1)} %constant_dynamic-slice_fusion.2.refs_2_, ...), custom_call_target="tpu_custom_call" | custom-call | bytes 1048576 | tf_op jit(solution)/shard_map/ring_gather/pallas_call | solution.py:202
  878.3 10.2 wide_q.1
  890.5 3.6 constant_dynamic-slice_fusion.refs_4_
  894.1 68.4 %ring_gather.11 = (bf16[16,128,2048]{2,1,0:T(8,128)(2,1)}, bf16[16,256,256]{2,1,0:T(8,128)(2,1)}, bf16[16,64,576]{2,1,0:T(8,128)(2,1)}, f32[16,64,128]{2,1,0:T(8,128)}, bf16[1024,1408]{1,0:T(8,128)(2,1)}) custom-call(bf16[128,2048]{1,0:T(8,128)(2,1)} %add.215.refs_0_, bf16[256,256]{1,0:T(8,128)(2,1)} %add_convert_fusion.5.refs_1_, ...), custom_call_target="tpu_custom_call" | custom-call | bytes 1048576 | tf_op jit(solution)/shard_map/ring_gather/pallas_call | solution.py:202
  962.5 3.0 bitcast_convert_fusion.1
  965.5 3.1 copy.62
  968.6 6.0 wide_kv.1
  974.6 10.9 %wide_gate.1 = f32[1024,2816]{1,0:T(8,128)} custom-call(bf16[16,1024,176]{2,1,0:T(8,128)(2,1)} %get-tuple-element.147.i_ref), custom_call_target="tpu_custom_call" | custom-call | bytes 1048576 | tf_op jit(solution)/shard_map/wide_gate/pallas_call | solution.py:820
  985.5 11.0 %wide_up.1 = f32[1024,2816]{1,0:T(8,128)} custom-call(bf16[16,1024,176]{2,1,0:T(8,128)(2,1)} %get-tuple-element.148.i_ref), custom_call_target="tpu_custom_call" | custom-call | bytes 1048576 | tf_op jit(solution)/shard_map/wide_up/pallas_call | solution.py:820
  996.5 6.2 slice.57
  1004.0 6.8 dynamic-slice_convert_fusion
  1010.9 5.6 add_bitcast_fusion
  1016.5 5.2 add_bitcast_fusion.2
  1021.7 3.1 add_bitcast_fusion.1
  1024.9 6.4 bitcast_convert_fusion
  1031.3 3.1 fusion.18
  (168 shorter events, 24.6 us)
Async XLA Ops:
  7.2 368.1 %all-gather.2.cloned.1.call-start = ((), (), s32[]{:S(2)}) async-start(), calls=%async_computation.2 | async-start | bytes 8912896 | tf_op jit(solution)/shard_map/all_gather | solution.py:948
  13.4 59.4 %copy-start.31 = (s32[1,2048]{1,0:T(1,128)S(1)}, s32[1,2048]{1,0:T(1,128)}, u32[]{:S(2)}) copy-start(s32[1,2048]{1,0:T(1,128)} %segr_ref.1) | copy-start | bytes 24580
  70.7 7.1 copy-start.23
  75.9 6.5 copy-start.12
  77.7 6.5 copy-start.13
  77.8 6.5 copy-start.14
  79.3 12.4 %copy-start.7 = (bf16[128,2048]{1,0:T(8,128)(2,1)}, bf16[128,2048]{1,0:T(8,128)(2,1)S(1)}, u32[]{:S(2)}) copy-start(bf16[128,2048]{1,0:T(8,128)(2,1)S(1)} %broadcast_select_fusion.6.wo_ref) | copy-start | bytes 1572868
  131.2 67.2 %copy-start.2 = (bf16[1,128,2048]{2,1,0:T(8,128)(2,1)S(1)}, bf16[1,128,2048]{2,1,0:T(8,128)(2,1)}, u32[]{:S(2)}) copy-start(bf16[1,128,2048]{2,1,0:T(8,128)(2,1)} %param.20) | copy-start | bytes 1572868
  199.9 329.0 %copy-start.39 = (f32[128]{0:T(128)}, f32[128]{0:T(128)S(1)}, u32[]{:S(2)}) copy-start(f32[128]{0:T(128)S(1)} %add_rsqrt_fusion.2) | copy-start | bytes 1540
  200.8 71.5 %slice-start.2 = ((s8[5767168]{0:T(1024)(128)(4,1)}), s8[1572864]{0:T(1024)(128)(4,1)S(1)}, s32[]{:S(2)}) async-start(s8[5767168]{0:T(1024)(128)(4,1)} %bitcast.104), calls=%async_computation.5 | async-start | bytes 3145728
  265.9 765.4 %reduce-scatter.2.cloned.1.call-start = ((), (), s32[]{:S(2)}) async-start(), calls=%async_computation.1 | async-start | bytes 8912896 | tf_op jit(solution)/shard_map/reduce_scatter | solution.py:996
  266.8 4.3 copy-start.28
  267.7 4.6 slice-start.3
  274.3 68.9 %copy-start.24 = (bf16[96,2048]{1,0:T(8,128)(2,1)S(1)}, bf16[96,2048]{1,0:T(8,128)(2,1)}, u32[]{:S(2)}) copy-start(bf16[96,2048]{1,0:T(8,128)(2,1)} %get-tuple-element.101) | copy-start | bytes 1179652
  366.1 1.3 copy-start
  370.5 310.3 %copy-start.43 = (f32[128]{0:T(128)}, f32[128]{0:T(128)S(1)}, u32[]{:S(2)}) copy-start(f32[128]{0:T(128)S(1)} %add_rsqrt_fusion.1) | copy-start | bytes 1540
  370.5 310.3 %copy-start.32 = (f32[1,8,2,128]{3,1,2,0:T(8,128)}, f32[1,8,2,128]{3,1,2,0:T(8,128)S(1)}, u32[]{:S(2)}) copy-start(f32[1,8,2,128]{3,1,2,0:T(8,128)S(1)} %copy.77) | copy-start | bytes 24580
  522.9 5.7 copy-start.1
  522.9 6.0 copy-start.5
  528.9 67.4 %copy-start.41 = (f32[128]{0:T(128)}, f32[128]{0:T(128)S(1)}, u32[]{:S(2)}) copy-start(f32[128]{0:T(128)S(1)} %broadcast_multiply_fusion.2) | copy-start | bytes 1540
  605.0 83.4 %copy-start.3 = (bf16[2048,64]{1,0:T(8,128)(2,1)}, bf16[2048,64]{1,0:T(8,128)(2,1)S(1)}, u32[]{:S(2)}) copy-start(bf16[2048,64]{1,0:T(8,128)(2,1)S(1)} %slice.65) | copy-start | bytes 786436
  679.7 5.9 copy-start.37
  680.8 5.4 copy-start.15
  680.8 5.4 copy-start.45
  685.6 2.8 copy-start.35
  686.2 3.1 copy-start.18
  686.2 3.1 copy-start.22
  687.0 4.2 copy-start.26
  687.0 3.2 copy-start.17
  687.0 3.2 copy-start.21
  690.2 103.2 %copy-start.25 = (bf16[96,2048]{1,0:T(8,128)(2,1)S(1)}, bf16[96,2048]{1,0:T(8,128)(2,1)}, u32[]{:S(2)}) copy-start(bf16[96,2048]{1,0:T(8,128)(2,1)} %get-tuple-element.137) | copy-start | bytes 1179652
  791.1 4.3 copy-start.11
  791.1 4.2 copy-start.16
  793.4 4.8 copy-start.4
  793.4 4.8 copy-start.19
  878.3 10.2 copy-start.34
  878.3 10.2 copy-start.36
  878.3 10.2 copy-start.38
  878.3 10.8 %copy-start.30 = (bf16[64,576]{1,0:T(8,128)(2,1)S(1)}, bf16[64,576]{1,0:T(8,128)(2,1)}, u32[]{:S(2)}) copy-start(bf16[64,576]{1,0:T(8,128)(2,1)} %get-tuple-element.139) | copy-start | bytes 221188
  878.3 11.5 %copy-start.27 = (bf16[512,256]{1,0:T(8,128)(2,1)S(1)}, bf16[512,256]{1,0:T(8,128)(2,1)}, u32[]{:S(2)}) copy-start(bf16[512,256]{1,0:T(8,128)(2,1)} %copy-done.26) | copy-start | bytes 786436
  878.3 11.5 %copy-start.29 = (bf16[256,256]{1,0:T(8,128)(2,1)S(1)}, bf16[256,256]{1,0:T(8,128)(2,1)}, u32[]{:S(2)}) copy-start(bf16[256,256]{1,0:T(8,128)(2,1)} %get-tuple-element.134) | copy-start | bytes 393220
  996.5 6.2 copy-start.20
  996.5 7.5 copy-start.46
  1004.0 6.8 copy-start.8
  1004.0 17.7 %slice-start.4 = ((s8[5767168]{0:T(1024)(128)(4,1)}), s8[1572864]{0:T(1024)(128)(4,1)S(1)}, s32[]{:S(2)}) async-start(s8[5767168]{0:T(1024)(128)(4,1)} %bitcast.106), calls=%async_computation.7 | async-start | bytes 3145728
  1010.9 5.6 copy-start.9
  1010.9 10.9 %slice-start.5 = ((s8[5767168]{0:T(1024)(128)(4,1)}), s8[4194304]{0:T(1024)(128)(4,1)S(1)}, s32[]{:S(2)}) async-start(s8[5767168]{0:T(1024)(128)(4,1)} %bitcast.106), calls=%async_computation.8 | async-start | bytes 8388608
  1016.5 5.3 copy-start.10
  1016.5 8.4 slice-start
  1021.7 3.1 slice-start.1
  1024.8 6.4 copy-start.6
  1024.8 6.4 copy-start.33
  1024.8 6.4 copy-start.40
  1024.9 6.4 copy-start.42
  1024.9 6.4 copy-start.44
Sparse Core Ops, SparseCore 0:
  266.0 75.0 all-gather.1
  366.2 115.9 reduce-scatter.1

commit v3 on v2

--- a/solution.py
+++ b/solution.py
@@ -84,11 +84,29 @@
     pl.semaphore_wait(barrier, len(devices) + across)
 
 
+def given(x):
+    return (x, True)
+
+
+def swap_arrays(swaps):
+    return [x[0] if isinstance(x, tuple) else x for x in swaps]
+
+
+def swap_shapes(swaps):
+    shapes = [(x[0].shape[0] // 2, x[0].shape[1]) if isinstance(x, tuple) else x.shape for x in swaps]
+    return [jax.ShapeDtypeStruct(shape, x.dtype) for shape, x in zip(shapes, swap_arrays(swaps))]
+
+
 def swap_copies(gives, takes, sems):
     other = 1 - lax.axis_index("fsdp")
+
+    def source(give, take):
+        height = take.shape[0]
+        return give if give.shape[0] == height else give.at[pl.ds(pl.multiple_of(other * height, height), height), :]
+
     return [
         pltpu.make_async_remote_copy(
-            give, take, sems.at[i, 0], sems.at[i, 1], device_id={"fsdp": other}, device_id_type=MESH
+            source(give, take), take, sems.at[i, 0], sems.at[i, 1], device_id={"fsdp": other}, device_id_type=MESH
         )
         for i, (give, take) in enumerate(zip(gives, takes))
     ]
@@ -98,13 +116,58 @@
     return pltpu.make_async_remote_copy(src, dst, send, recv, device_id={"seq": device}, device_id_type=MESH)
 
 
-def gather_kernel(n, cuts, actives, swaps, shared, *refs):
+def cast_pieces(rows):
+    return next(pieces for pieces in (8, 4, 2, 1) if rows % (16 * pieces) == 0 or pieces == 1)
+
+
+def cast_scratch(casts):
+    shapes = []
+    for x in casts:
+        height = x.shape[0] // cast_pieces(x.shape[0])
+        shapes += [
+            pltpu.VMEM((2, height, x.shape[1]), F32),
+            pltpu.VMEM((2, height, x.shape[1]), BF),
+            pltpu.SemaphoreType.DMA((2,)),
+            pltpu.SemaphoreType.DMA((2,)),
+        ]
+    return shapes
+
+
+def cast_steps(sources, targets, scratch):
+    for i, (source, target) in enumerate(zip(sources, targets)):
+        wide, narrow, in_sem, out_sem = scratch[4 * i : 4 * i + 4]
+        pieces = cast_pieces(source.shape[0])
+        height = source.shape[0] // pieces
+
+        def load(c):
+            return pltpu.make_async_copy(source.at[pl.ds(c * height, height), :], wide.at[c % 2], in_sem.at[c % 2])
+
+        def save(c):
+            return pltpu.make_async_copy(narrow.at[c % 2], target.at[pl.ds(c * height, height), :], out_sem.at[c % 2])
+
+        load(0).start()
+        for c in range(pieces):
+            if c + 1 < pieces:
+                load(c + 1).start()
+            load(c).wait()
+            if c >= 2:
+                save(c - 2).wait()
+            narrow[c % 2] = wide[c % 2].astype(BF)
+            save(c).start()
+            yield
+        for c in range(max(0, pieces - 2), pieces):
+            save(c).wait()
+
+
+def gather_kernel(n, cuts, actives, swaps, shared, casts, *refs):
     count = len(cuts)
     total = count + swaps
-    x_refs, give_refs = refs[:count], refs[count:total]
-    o_refs, take_refs = refs[total : total + count], refs[total + count : 2 * total]
-    own_sem, local_sem, swap_sems, hand_sem = refs[2 * total : 2 * total + 4]
-    sems = refs[2 * total + 4 :]
+    x_refs, give_refs, wide_refs = refs[:count], refs[count:total], refs[total : total + casts]
+    refs = refs[total + casts :]
+    o_refs, take_refs, narrow_refs = refs[:count], refs[count:total], refs[total : total + casts]
+    own_sem, local_sem, swap_sems, hand_sem = refs[total + casts : total + casts + 4]
+    sems = refs[total + casts + 4 :]
+    casting = cast_steps(wide_refs, narrow_refs, sems[4 * count :])
     me, core, r, _ = ring_place()
     targets = (ring_seq((r + 1) % n, core, n), ring_seq((r + n - 1) % n, core, n))
     sibling = ring_seq(r, 1 - core, n)
@@ -172,6 +235,10 @@
                     across(i, t + 1, d, k, rows, core).start()
 
                 guarded(i, block(t + 1, d, core), step)
+        for _ in range(4):
+            next(casting, None)
+    for _ in casting:
+        pass
     for i in range(count):
         local(i).wait()
         guarded(i, me, lambda: own(i).wait_send())
@@ -193,29 +260,33 @@
         handed(1 - core).wait_recv()
 
 
-def ring_gather_many(operands, collective_id, actives=None, swaps=(), shared=None):
+def ring_gather_many(operands, collective_id, actives=None, swaps=(), shared=None, casts=()):
     devices = lax.axis_size("seq")
     n = devices // 2
     cuts = [2 if x.shape[0] % 64 == 0 else 1 for x in operands]
     anywhere = pl.BlockSpec(memory_space=pl.ANY)
     sems = [pltpu.SemaphoreType.DMA((n - 1, 2, cut)) for cut in cuts for _ in range(4)]
     return pl.pallas_call(
-        functools.partial(gather_kernel, n, cuts, actives or [None] * len(operands), len(swaps), shared),
+        functools.partial(gather_kernel, n, cuts, actives or [None] * len(operands), len(swaps), shared, len(casts)),
         out_shape=[jax.ShapeDtypeStruct((devices, *x.shape), x.dtype) for x in operands]
-        + [jax.ShapeDtypeStruct(x.shape, x.dtype) for x in swaps],
-        in_specs=[anywhere] * (len(operands) + len(swaps)),
-        out_specs=[anywhere] * (len(operands) + len(swaps)),
+        + swap_shapes(swaps)
+        + [jax.ShapeDtypeStruct(x.shape, BF) for x in casts],
+        in_specs=[anywhere] * (len(operands) + len(swaps) + len(casts)),
+        out_specs=[anywhere] * (len(operands) + len(swaps) + len(casts)),
         scratch_shapes=[
             pltpu.SemaphoreType.DMA((len(operands), 2)),
             pltpu.SemaphoreType.DMA((len(operands),)),
             pltpu.SemaphoreType.DMA((max(1, len(swaps)), 2)),
             pltpu.SemaphoreType.DMA((2,)),
         ]
-        + sems,
-        compiler_params=pltpu.CompilerParams(collective_id=collective_id, has_side_effects=True),
+        + sems
+        + cast_scratch(casts),
+        compiler_params=pltpu.CompilerParams(
+            collective_id=collective_id, has_side_effects=True, **({"vmem_limit_bytes": VMEM_LIMIT} if casts else {})
+        ),
         cost_estimate=COST,
         name="ring_gather",
-    )(*operands, *swaps)
+    )(*operands, *swap_arrays(swaps), *casts)
 
 
 def ring_gather(x, collective_id, swaps=()):
@@ -291,7 +362,7 @@
     anywhere = [pl.BlockSpec(memory_space=pl.ANY)] * len(swaps)
     out, *taken = pl.pallas_call(
         functools.partial(scatter_kernel, n, cut, len(swaps)),
-        out_shape=[jax.ShapeDtypeStruct((rows, columns), F32)] + [jax.ShapeDtypeStruct(x.shape, x.dtype) for x in swaps],
+        out_shape=[jax.ShapeDtypeStruct((rows, columns), F32)] + swap_shapes(swaps),
         in_specs=[vmem, vmem] + anywhere,
         out_specs=[vmem] + anywhere,
         scratch_shapes=[
@@ -308,7 +379,7 @@
         ),
         cost_estimate=COST,
         name="ring_scatter",
-    )(a, w, *swaps)
+    )(a, w, *swap_arrays(swaps))
     return out, taken
 
 
@@ -325,11 +396,6 @@
     if count != 2:
         return lax.dynamic_index_in_dim(lax.all_gather(x, "fsdp", axis=0), owner, 0, keepdims=False)
     return jnp.where(lax.axis_index("fsdp") == owner, x, other)
-
-
-def fsdp_given(x):
-    half = x.shape[0] // 2
-    return lax.dynamic_slice_in_dim(x, (1 - lax.axis_index("fsdp")) * half, half, 0)
 
 
 def fsdp_scatter(x, taken=None):
@@ -577,9 +643,9 @@
 
 def expert_in_kernel(count, most, swaps, *refs):
     wg_parts, wu_parts = refs[:count], refs[count : 2 * count]
-    act_ref, slot_ref, share_ref, wsg_ref, wsu_ref = refs[2 * count : 2 * count + 5]
-    gives, refs = refs[2 * count + 5 : 2 * count + 5 + swaps], refs[2 * count + 5 + swaps :]
-    xe_ref, ge_ref, ue_ref, he_ref, sg_ref, su_ref, sh_ref = refs[:7]
+    act_ref, slot_ref, share_ref, wsgu_ref, wsd_ref, g_ref = refs[2 * count : 2 * count + 6]
+    gives, refs = refs[2 * count + 6 : 2 * count + 6 + swaps], refs[2 * count + 6 + swaps :]
+    xe_ref, ge_ref, ue_ref, he_ref, sh_ref, dye_ref, dsgu_ref = refs[:7]
     takes, (wg, wu, sems, swap_sems) = refs[7 : 7 + swaps], refs[7 + swaps :]
     swapped = swap_copies(gives, takes, swap_sems) if swaps else []
     if swaps:
@@ -594,13 +660,18 @@
     start_first(copies)
     blocks, rows = slot_ref.shape[0], slot_ref.shape[2]
     for b in range(blocks):
-        pick, _ = picks(slot_ref, share_ref, b, most)
-        xe_ref[b * most : (b + 1) * most, :] = mm(pick, act_ref[b * rows : (b + 1) * rows, :]).astype(BF)
-    act = act_ref[...]
-    sg, su = mm(act, wsg_ref[...]), mm(act, wsu_ref[...])
-    sg_ref[...] = sg
-    su_ref[...] = su
-    sh_ref[...] = (sg * jax.nn.sigmoid(sg) * su).astype(BF)
+        pick, share = picks(slot_ref, share_ref, b, most)
+        block, packed = slice(b * rows, (b + 1) * rows), slice(b * most, (b + 1) * most)
+        xe_ref[packed, :] = mm(pick, act_ref[block, :]).astype(BF)
+        dye_ref[packed, :] = (share * mm(pick, g_ref[block, :])).astype(BF)
+    sgu = mm(act_ref[...], wsgu_ref[...])
+    units = sh_ref.shape[1]
+    sg, su = sgu[:, :units], sgu[:, units:]
+    sig = jax.nn.sigmoid(sg)
+    sh_ref[...] = (sg * sig * su).astype(BF)
+    dsh = mm_nt(g_ref[...], wsd_ref[...])
+    dsgu_ref[:, :units] = (dsh * su * sig * (1.0 + sg * (1.0 - sig))).astype(BF)
+    dsgu_ref[:, units:] = (dsh * sg * sig).astype(BF)
     wait_first(copies)
     for low, high in hidden_spans(wg.shape[1]):
         ge = mm(xe_ref[...], wg[:, low:high])
@@ -631,23 +702,15 @@
         y_ref[b * rows : (b + 1) * rows, :] = (ys + mm_tn(pick, (share * ye).astype(BF))).astype(BF)
 
 
-def expert_back_kernel(count, most, swaps, *refs):
+def expert_back_kernel(n, cut, count, most, swaps, *refs):
     wg_parts, wu_parts, wd_parts = refs[:count], refs[count : 2 * count], refs[2 * count : 3 * count]
-    g_ref, slot_ref, share_ref, wsg_ref, wsu_ref, wsd_ref, ge_ref, ue_ref, sg_ref, su_ref = refs[3 * count : 3 * count + 10]
-    dact_ref, dye_ref, dge_ref, due_ref, dsg_ref, dsu_ref = refs[3 * count + 10 : 3 * count + 16]
-    wg, wu, wd, sems, _ = refs[3 * count + 16 :]
+    dye_ref, slot_ref, share_ref, wsgu_ref, part_ref, ge_ref, ue_ref, dsgu_ref = refs[3 * count : 3 * count + 8]
+    dact_ref, dge_ref, due_ref, y_ref = refs[3 * count + 8 : 3 * count + 12]
+    wg, wu, wd, sems, _, *buffers = refs[3 * count + 12 :]
     copies = [fill(p, w, sems.at[i]) for i, (p, w) in enumerate(((wg_parts, wg), (wu_parts, wu), (wd_parts, wd)))]
     start_first(copies)
+    finish = scatter_in_grid(pl.program_id(0), n, cut, part_ref, y_ref, buffers)
     blocks, rows = slot_ref.shape[0], slot_ref.shape[2]
-    for b in range(blocks):
-        pick, share = picks(slot_ref, share_ref, b, most)
-        packed = mm(pick, g_ref[b * rows : (b + 1) * rows, :])
-        dye_ref[b * most : (b + 1) * most, :] = (share * packed).astype(BF)
-    dsh = mm_nt(g_ref[...], wsd_ref[...])
-    sg, su = sg_ref[...], su_ref[...]
-    sig = jax.nn.sigmoid(sg)
-    dsg_ref[...] = (dsh * su * sig * (1.0 + sg * (1.0 - sig))).astype(BF)
-    dsu_ref[...] = (dsh * sg * sig).astype(BF)
     wait_first(copies)
     for low, high in hidden_spans(wg.shape[1]):
         dhe = mm_nt(dye_ref[...], wd[low:high, :])
@@ -659,11 +722,12 @@
     for b in range(blocks):
         pick, _ = picks(slot_ref, share_ref, b, most)
         block = slice(b * rows, (b + 1) * rows)
-        shared = mm_nt(dsg_ref[block, :], wsg_ref[...]) + mm_nt(dsu_ref[block, :], wsu_ref[...])
+        shared = mm_nt(dsgu_ref[block, :], wsgu_ref[...])
         dact_ref[block, :] = (shared + mm_tn(pick, dxe[b * most : (b + 1) * most, :])).astype(BF)
-
-
-def expert_call(kernel, name, pieces, most, steps, slot, share, whole, tiled, outs, swaps=(), collective_id=None):
+    finish()
+
+
+def expert_call(kernel, name, pieces, most, steps, slot, share, whole, tiled, outs, swaps=(), collective_id=None, summed=None):
     devices, rows = slot.shape[0], slot.shape[2]
     per = devices // steps
     anywhere = pl.BlockSpec(memory_space=pl.ANY)
@@ -675,30 +739,56 @@
     cut = pl.BlockSpec((per, 1, rows), lambda i: (i, 0, 0))
     count = len(pieces[0])
     full = lambda group: (group[0].shape[0] * count, group[0].shape[1])
+    buffers, kept = [], []
+    if summed is not None:
+        buffers = scatter_buffers(devices // 2, *summed)
+        kept = [(pl.BlockSpec(summed, lambda i: (0, 0)), jax.ShapeDtypeStruct(summed, F32))]
     return pl.pallas_call(
         functools.partial(kernel, count, most, len(swaps)),
         grid=(steps,),
         out_shape=[jax.ShapeDtypeStruct((total, columns), dtype) for total, columns, dtype in outs]
+        + [shape for _, shape in kept]
         + [jax.ShapeDtypeStruct(x.shape, x.dtype) for x in swaps],
         in_specs=[anywhere] * (len(pieces) * count) + [tile(*tiled[0].shape), cut, cut] + [vmem] * len(whole)
         + [tile(*t.shape) for t in tiled[1:]]
         + [anywhere] * len(swaps),
-        out_specs=[tile(total, columns) for total, columns, _ in outs] + [anywhere] * len(swaps),
+        out_specs=[tile(total, columns) for total, columns, _ in outs]
+        + [spec for spec, _ in kept]
+        + [anywhere] * len(swaps),
         scratch_shapes=[pltpu.VMEM(full(group), BF) for group in pieces]
-        + [pltpu.SemaphoreType.DMA((len(pieces), count)), pltpu.SemaphoreType.DMA((max(1, len(swaps)), 2))],
+        + [pltpu.SemaphoreType.DMA((len(pieces), count)), pltpu.SemaphoreType.DMA((max(1, len(swaps)), 2))]
+        + buffers,
         compiler_params=pltpu.CompilerParams(
-            vmem_limit_bytes=VMEM_LIMIT, collective_id=collective_id, has_side_effects=len(swaps) > 0
+            vmem_limit_bytes=VMEM_LIMIT, collective_id=collective_id, has_side_effects=collective_id is not None
         ),
         cost_estimate=COST,
         name=name,
     )(*sum(pieces, ()), tiled[0], slot, share, *whole, *tiled[1:], *swaps)
 
 
-def weight_grads_kernel(n, cut, *refs):
-    xe_ref, dge_ref, due_ref, he_ref, dye_ref, act_ref, dsg_ref, dsu_ref, sh_ref, g_ref, part_ref = refs[:11]
-    o_ref, gate_ref, up_ref, down_ref, sgate_ref, sup_ref, sdown_ref = refs[11:18]
-    sibbuf, rbuf, sbuf, send, recv, fsend, frecv = refs[18:]
-    t = pl.program_id(0)
+def trim(stacked, share):
+    devices, room, width = stacked.shape
+    if share % 8:
+        return stacked[:, :share].reshape(-1, width).astype(F32)
+
+    def kernel(i_ref, o_ref):
+        for d in range(i_ref.shape[0]):
+            o_ref[d * share : (d + 1) * share, :] = i_ref[d, :share, :].astype(F32)
+
+    return pl.pallas_call(
+        kernel,
+        grid=(4,),
+        out_shape=jax.ShapeDtypeStruct((devices * share, width), F32),
+        in_specs=[pl.BlockSpec((devices // 4, room, width), lambda i: (i, 0, 0))],
+        out_specs=pl.BlockSpec((devices // 4 * share, width), lambda i: (i, 0)),
+        compiler_params=pltpu.CompilerParams(vmem_limit_bytes=VMEM_LIMIT),
+        cost_estimate=COST,
+        name="trim",
+    )(stacked)
+
+
+def scatter_in_grid(t, n, cut, part_ref, o_ref, buffers):
+    sibbuf, rbuf, sbuf, send, recv, fsend, frecv = buffers
     me, core, r, _ = ring_place()
     targets = (ring_seq((r + 1) % n, core, n), ring_seq((r + n - 1) % n, core, n))
     sibling = ring_seq(r, 1 - core, n)
@@ -746,23 +836,46 @@
             onward(n - 2, d).wait_recv()
             o_ref[:, spans[d]] = both() + rbuf[n - 2, :, spans[d]].astype(F32)
 
+    def finish():
+        @pl.when(t == n - 1)
+        def _():
+            for step in range(n):
+                for d in range(2):
+                    across(step, d).wait_send()
+                    if step < n - 1:
+                        onward(step, d).wait_send()
+
+    return finish
+
+
+def scatter_buffers(n, rows, columns):
+    return (
+        [pltpu.VMEM((n, rows, columns), BF), pltpu.VMEM((n - 1, rows, columns), BF), pltpu.VMEM((n - 1, rows, columns), BF)]
+        + [pltpu.SemaphoreType.DMA((n - 1, 2))] * 2
+        + [pltpu.SemaphoreType.DMA((n, 2))] * 2
+    )
+
+
+def weight_grads_kernel(n, cut, parts, *refs):
+    xe_ref, dge_ref, due_ref, he_ref, dye_ref, act_ref, dsgu_ref, sh_ref, g_ref, part_ref = refs[:10]
+    o_ref, gate_ref, up_ref, down_ref, sgu_ref, sdown_ref = refs[10:16]
+    finish = scatter_in_grid(pl.program_id(0), n, cut, part_ref, o_ref, refs[16:])
     gate_ref[...] = mm_tn(xe_ref[...], dge_ref[...]).astype(BF)
     up_ref[...] = mm_tn(xe_ref[...], due_ref[...]).astype(BF)
     down_ref[...] = mm_tn(he_ref[...], dye_ref[...]).astype(BF)
-    sgate_ref[...] = mm_tn(act_ref[...], dsg_ref[...]).astype(BF)
-    sup_ref[...] = mm_tn(act_ref[...], dsu_ref[...]).astype(BF)
-    sdown_ref[...] = mm_tn(sh_ref[...], g_ref[...]).astype(BF)
-
-    @pl.when(t == n - 1)
-    def _():
-        for step in range(n):
-            for d in range(2):
-                across(step, d).wait_send()
-                if step < n - 1:
-                    onward(step, d).wait_send()
-
-
-def weight_grads(xe, dge, due, he, dye, act, dsg, dsu, sh, g, part, collective_id):
+    sgu_ref[...] = mm_tn(act_ref[...], dsgu_ref[...]).astype(BF)
+    sdown = mm_tn(sh_ref[...], g_ref[...]).astype(BF)
+    share = sdown.shape[0] // parts
+    room = sdown_ref.shape[0] // parts
+    for p in range(parts):
+        sdown_ref[p * room : p * room + share, :] = sdown[p * share : (p + 1) * share, :]
+        if room > share:
+            sdown_ref[p * room + share : (p + 1) * room, :] = jnp.zeros((room - share, sdown.shape[1]), BF)
+
+    finish()
+
+
+def weight_grads(xe, dge, due, he, dye, act, dsgu, sh, g, part, parts, room, collective_id):
     devices = lax.axis_size("seq")
     n = devices // 2
     length, columns = part.shape
@@ -775,54 +888,50 @@
     def held(x):
         return pl.BlockSpec(memory_space=pltpu.VMEM)
 
-    ff, units = dge.shape[1], dsg.shape[1]
+    ff, units = dge.shape[1], dsgu.shape[1]
     slab = columns // n
     down = lambda width: pl.BlockSpec((slab, width), lambda i: (i, 0))
     along = lambda height: pl.BlockSpec((height, slab), lambda i: (0, i))
     return pl.pallas_call(
-        functools.partial(weight_grads_kernel, n, cut),
+        functools.partial(weight_grads_kernel, n, cut, parts),
         grid=(n,),
         out_shape=[jax.ShapeDtypeStruct((rows, columns), F32)]
         + [
             jax.ShapeDtypeStruct(shape, BF)
-            for shape in ((columns, ff), (columns, ff), (ff, columns), (columns, units), (columns, units), (units, columns))
+            for shape in ((columns, ff), (columns, ff), (ff, columns), (columns, units), (parts * room, columns))
         ],
-        in_specs=[tile(xe), held(dge), held(due), held(he), tile(dye), tile(act), held(dsg), held(dsu), held(sh), tile(g)]
+        in_specs=[tile(xe), held(dge), held(due), held(he), tile(dye), tile(act), held(dsgu), held(sh), tile(g)]
         + [held(part)],
         out_specs=[pl.BlockSpec((rows, columns), lambda i: (0, 0)), down(ff), down(ff), along(ff)]
-        + [down(units), down(units), along(units)],
-        scratch_shapes=[
-            pltpu.VMEM((n, rows, columns), BF),
-            pltpu.VMEM((n - 1, rows, columns), BF),
-            pltpu.VMEM((n - 1, rows, columns), BF),
-        ]
-        + [pltpu.SemaphoreType.DMA((n - 1, 2))] * 2
-        + [pltpu.SemaphoreType.DMA((n, 2))] * 2,
+        + [down(units), along(parts * room)],
+        scratch_shapes=scatter_buffers(n, rows, columns),
         compiler_params=pltpu.CompilerParams(
             collective_id=collective_id, has_side_effects=True, vmem_limit_bytes=VMEM_LIMIT
         ),
         cost_estimate=COST,
         name="weight_grads",
-    )(xe, dge, due, he, dye, act, dsg, dsu, sh, g, part.reshape(devices, rows, columns))
-
-
-def widen(stacked, parts, name):
+    )(xe, dge, due, he, dye, act, dsgu, sh, g, part.reshape(devices, rows, columns))
+
+
+def widen(stacked, count, parts, name):
     devices, rows, columns = stacked.shape
-    share = columns // parts
+    share = columns // parts // count
+    width = devices * columns // count
     steps = 8
 
-    def kernel(i_ref, o_ref):
-        for p in range(parts):
-            for d in range(devices):
-                at = (p * devices + d) * share
-                o_ref[:, at : at + share] = i_ref[d, :, p * share : (p + 1) * share].astype(F32)
+    def kernel(i_ref, *o_refs):
+        for j, o_ref in enumerate(o_refs):
+            for p in range(parts):
+                for d in range(devices):
+                    at, source = (p * devices + d) * share, (j * parts + p) * share
+                    o_ref[:, at : at + share] = i_ref[d, :, source : source + share].astype(F32)
 
     return pl.pallas_call(
         kernel,
         grid=(steps,),
-        out_shape=jax.ShapeDtypeStruct((rows, devices * columns), F32),
+        out_shape=[jax.ShapeDtypeStruct((rows, width), F32)] * count,
         in_specs=[pl.BlockSpec((devices, rows // steps, columns), lambda i: (0, i, 0))],
-        out_specs=pl.BlockSpec((rows // steps, devices * columns), lambda i: (i, 0)),
+        out_specs=[pl.BlockSpec((rows // steps, width), lambda i: (i, 0))] * count,
         compiler_params=pltpu.CompilerParams(vmem_limit_bytes=VMEM_LIMIT),
         cost_estimate=COST,
         name=name,
@@ -893,9 +1002,16 @@
         jnp.where(routes[0].T[None, :, :] == experts[:, None, None], gate_weights[0].T[None, :, :], 0.0), axis=1
     )
     x_all, spread_all, *others = ring_gather_many(
-        [own_x, spread], 8, None, crossing(*early), early_latent if pair else None
-    )
-    x_all = x_all.reshape(length, width)
+        [own_x, spread],
+        8,
+        None,
+        crossing(*early),
+        early_latent if pair else None,
+        (expert_gate[0], expert_up[0], expert_down[0]),
+    )
+    others, (egate, eup, edown) = others[:-3], others[-3:]
+    late_g, x_all = lax.optimization_barrier((own_g, x_all.reshape(length, width)))
+    g_all = lax.all_gather(late_g, "seq", axis=0, tiled=True)
     share_of = lax.dynamic_index_in_dim(spread_all, at, 1, keepdims=False)
     others = crossed(others, len(early))
     gains = fsdp_gather(gains, others[0]).reshape(parts, -1)[:, :gains_size].astype(F32)
@@ -912,12 +1028,11 @@
         pieces = [
             lax.dynamic_slice_in_dim(weight, p * (hidden // parts) + at * share, share, 1) for p in range(parts)
         ]
-        return jnp.concatenate(pieces, axis=1).astype(BF)
+        return pieces
 
     share_pad = -(-share // 32) * 32
-    sgate, sup = shared_columns(shared_gate), shared_columns(shared_up)
+    sgu = jnp.concatenate(shared_columns(shared_gate) + shared_columns(shared_up), axis=1).astype(BF)
     sdown = jnp.pad(rows_of(shared_down, at, share), ((0, share_pad - share), (0, 0)))
-    egate, eup, edown = expert_gate[0].astype(BF), expert_up[0].astype(BF), expert_down[0].astype(BF)
 
     cosine, sine = rope_tables(length)
     seg_col, seg_row = segment_ids.reshape(length, 1), segment_ids
@@ -930,10 +1045,10 @@
         sine,
         seg_col,
         seg_row,
-        crossing(sgate, sup, sdown),
+        crossing(sgu, sdown),
         11 if pair else None,
     )
-    sgate_other, sup_other, sdown_other = crossed(taken, 3)
+    sgu_other, sdown_other = crossed(taken, 2)
     own_xf = own_x.astype(F32)
     attended, taken = ring_scatter(heads, w_out.T, 2, crossing(egate))
     (egate_other,) = crossed(taken, 1)
@@ -943,9 +1058,8 @@
     act_all, taken = ring_gather(act_two, 9, crossing(eup))
     (eup_other,) = crossed(taken, 1)
     w_egate, w_eup = fsdp_pieces(egate, egate_other), fsdp_pieces(eup, eup_other)
-    w_sgate, w_sup = fsdp_gather(sgate, sgate_other), fsdp_gather(sup, sup_other)
-    late_g, act_all = lax.optimization_barrier((own_g, act_all))
-    g_all = lax.all_gather(late_g, "seq", axis=0, tiled=True)
+    w_sgu = fsdp_gather(sgu, sgu_other)
+    w_sdown = fsdp_gather(sdown[:share], sdown_other[:share] if pair else None)
 
     most = min(MOST, rows)
     named = share_of > 0.0
@@ -956,7 +1070,7 @@
     ff = expert_gate.shape[2]
     units = parts * share
     steps = 4
-    xe, ge, ue, he, sg, su, sh, *taken = expert_call(
+    xe, ge, ue, he, sh, dye, dsgu, *taken = expert_call(
         expert_in_kernel,
         "experts_in",
         (w_egate, w_eup),
@@ -964,23 +1078,22 @@
         steps,
         slot,
         share_of,
-        (w_sgate, w_sup),
-        (act_all,),
+        (w_sgu, w_sdown),
+        (act_all, g_all),
         (
             (packed, width, BF),
             (packed, ff, F32),
             (packed, ff, F32),
             (packed, ff, BF),
-            (length, units, F32),
-            (length, units, F32),
             (length, units, BF),
+            (packed, width, BF),
+            (length, 2 * units, BF),
         ),
         crossing(edown),
         10 if pair else None,
     )
     (edown_other,) = crossed(taken, 1)
     w_edown = fsdp_pieces(edown, edown_other)
-    w_sdown = fsdp_gather(sdown[:share], sdown_other[:share] if pair else None)
     (y_part,) = expert_call(
         expert_out_kernel,
         "experts_out",
@@ -993,40 +1106,31 @@
         (he, sh),
         ((length, width, BF),),
     )
-    y_sum = lax.psum_scatter(y_part, "seq", scatter_dimension=0, tiled=True).astype(F32)
-    dact_part, dye, dge, due, dsg, dsu = expert_call(
-        expert_back_kernel,
+    dact_part, dge, due, y_sum = expert_call(
+        functools.partial(expert_back_kernel, devices // 2, width // 256 * 128),
         "experts_back",
         (w_egate, w_eup, w_edown),
         most,
-        steps,
+        devices // 2,
         slot,
         share_of,
-        (w_sgate, w_sup, w_sdown),
-        (g_all, ge, ue, sg, su),
-        (
-            (length, width, BF),
-            (packed, width, BF),
-            (packed, ff, BF),
-            (packed, ff, BF),
-            (length, units, BF),
-            (length, units, BF),
-        ),
-    )
-    dact_two, grad_egate, grad_eup, grad_edown, grad_sgate, grad_sup, grad_sdown = weight_grads(
-        xe, dge, due, he, dye, act_all, dsg, dsu, sh, g_all, dact_part, 3
+        (w_sgu, y_part.reshape(devices, rows, width)),
+        (dye, ge, ue, dsgu),
+        ((length, width, BF), (packed, ff, BF), (packed, ff, BF)),
+        (),
+        12,
+        (rows, width),
+    )
+    dact_two, grad_egate, grad_eup, grad_edown, grad_sgu, grad_sdown = weight_grads(
+        xe, dge, due, he, dye, act_all, dsgu, sh, g_all, dact_part, parts, share_pad, 3
     )
     own_gf = own_g.astype(F32)
     grad_gain_two = jnp.sum(dact_two * x1 * r3, axis=0)
     dx1 = own_gf + norm_back(x1, r3, dact_two * gain_two)
-    sdown_given = jnp.pad(fsdp_given(grad_sdown), ((0, share_pad - share), (0, 0))) if pair else None
-    dattn_all, taken = ring_gather(
-        dx1.astype(BF), 1, crossing(fsdp_given(grad_sgate), fsdp_given(grad_sup), sdown_given) if pair else ()
-    )
-    sgate_taken, sup_taken, sdown_taken = crossed(taken, 3)
-    grad_sgate = fsdp_scatter(grad_sgate, sgate_taken).astype(BF)
-    grad_sup = fsdp_scatter(grad_sup, sup_taken).astype(BF)
-    grad_sdown = fsdp_scatter(grad_sdown, sdown_taken[:share] if pair else None).astype(BF)
+    dattn_all, taken = ring_gather(dx1.astype(BF), 1, (given(grad_sgu), given(grad_sdown)) if pair else ())
+    sgu_taken, sdown_taken = crossed(taken, 2)
+    grad_sgu = fsdp_scatter(grad_sgu, sgu_taken).astype(BF)
+    grad_sdown = fsdp_scatter(grad_sdown, sdown_taken).astype(BF)
     output = (x1 + y_sum).astype(BF)
 
     back, grad_out = local_call(
@@ -1049,7 +1153,7 @@
     grad_back = mm_tn(act_one, back).astype(BF)
     grad_query = jnp.concatenate([grad_back[:, :NOPE], grad_back[:, KV_END:QK_END]], 1)
     grad_expand = mm_tn(cnorm, back[:, NOPE:KV_END]).astype(BF)
-    summed, taken = ring_scatter(back, w_back, 4, (fsdp_given(grad_edown),) if pair else ())
+    summed, taken = ring_scatter(back, w_back, 4, (given(grad_edown),) if pair else ())
     grad_edown = fsdp_scatter(grad_edown, *taken)
 
     r1 = norm_scale(own_xf)
@@ -1070,35 +1174,35 @@
     def in_part(device):
         return device * V_DIM // out_rows == lax.axis_index("fsdp")
 
-    gate_all, up_all, dlatent_all, *taken = ring_gather_many(
-        [grad_sgate, grad_sup, dlatent],
+    sgu_all, sdown_all, dlatent_all, *taken = ring_gather_many(
+        [grad_sgu, grad_sdown, dlatent],
         5,
         None,
-        (fsdp_given(grad_query), fsdp_given(grad_expand), grad_out, small) if pair else (),
-    )
-    query_taken, expand_taken, out_taken, small_taken = crossed(taken, 4)
+        (given(grad_query), given(grad_expand), grad_out, small, given(grad_egate)) if pair else (),
+    )
+    query_taken, expand_taken, out_taken, small_taken, egate_taken = crossed(taken, 5)
     grad_query = fsdp_scatter(grad_query, query_taken).astype(BF)
     grad_expand = fsdp_scatter(grad_expand, expand_taken).astype(BF)
     grad_out = fsdp_sum(grad_out, out_taken)
     small = fsdp_sum(small, small_taken)
+    grad_egate = fsdp_scatter(grad_egate, egate_taken)
     slab = width // parts // devices
     act_cols = jnp.concatenate(
         [lax.dynamic_slice_in_dim(act_one, p * (width // parts) + at * slab, slab, 1) for p in range(parts)], axis=1
     )
     grad_latent = mm_tn(act_cols, dlatent_all.reshape(length, -1)).astype(BF)
-    sdown_pad = jnp.pad(grad_sdown, ((0, share_pad - share), (0, 0)))
-    query_all, sdown_all, *taken = ring_gather_many(
-        [grad_query, sdown_pad], 6, None, (fsdp_given(grad_latent), fsdp_given(grad_egate)) if pair else ()
-    )
-    latent_taken, egate_taken = crossed(taken, 2)
+    latent_taken = None
+    if pair:
+        latent_taken = lax.ppermute(
+            lax.dynamic_slice_in_dim(grad_latent, (1 - part) * slab, slab, 0), "fsdp", [(0, 1), (1, 0)]
+        )
     grad_latent = fsdp_scatter(grad_latent, latent_taken).astype(BF)
-    grad_egate = fsdp_scatter(grad_egate, egate_taken)
     latent_pad = -(-slab // 32) * 32
-    out_all, expand_all, latent_all, small_all, *taken = ring_gather_many(
-        [grad_out, grad_expand, jnp.pad(grad_latent, ((0, latent_pad - slab), (0, 0))), small],
+    query_all, expand_all, out_all, latent_all, small_all, *taken = ring_gather_many(
+        [grad_query, grad_expand, grad_out, jnp.pad(grad_latent, ((0, latent_pad - slab), (0, 0))), small],
         7,
-        [in_part, None, None, None],
-        (fsdp_given(grad_eup),) if pair else (),
+        [None, None, in_part, None, None],
+        (given(grad_eup),) if pair else (),
     )
     (eup_taken,) = crossed(taken, 1)
     grad_eup = fsdp_scatter(grad_eup, eup_taken)
@@ -1107,6 +1211,7 @@
         out_all.reshape(devices * V_DIM, width), part * out_rows, out_rows, 0
     ).astype(F32)
     small = jnp.sum(small_all, axis=0).reshape(-1)
+    wide_gate, wide_up = widen(sgu_all, 2, parts, "wide_shared")
     gain_rows = width // parts
     own_gains = [
         lax.dynamic_slice_in_dim(small, part * gain_rows, gain_rows),
@@ -1117,15 +1222,15 @@
         output[None],
         input_grad[None],
         own_gains[0],
-        widen(query_all, 1, "wide_q"),
+        widen(query_all, 1, 1, "wide_q")[0],
         latent_all.reshape(-1, grad_latent.shape[1]).astype(F32),
         own_gains[2],
-        widen(expand_all, 1, "wide_kv"),
+        widen(expand_all, 1, 1, "wide_kv")[0],
         out_grad_own,
         own_gains[1],
-        widen(gate_all, parts, "wide_gate"),
-        widen(up_all, parts, "wide_up"),
-        sdown_all[:, :share].reshape(-1, width).astype(F32),
+        wide_gate,
+        wide_up,
+        trim(sdown_all, share),
         grad_egate[None],
         grad_eup[None],
         grad_edown[None],

time: 1050 us -> 954 us (0.909)
  Pallas kernels: 876 us -> 835 us
  local copies, waits for them, and re-layouts: 53.9 us -> 25.3 us
  other arithmetic: 78.4 us -> 54.2 us
    pallas_call x6 -> x5, Pallas kernels: 406 us -> 374 us  [ring_gather_many(): pl.pallas_call(functools.partial(gather_kernel, n, cuts, actives or [None...]
    dynamic_slice x8 -> x1, local copies, waits for them, and re-layouts: 17.4 us -> 0.02 us  [per_device(): lax.dynamic_slice_in_dim(grad_latent, (1 - part) * slab, slab, 0)]
    convert_element_type x6 -> x2, other arithmetic: 18.9 us -> 1.92 us  [the longest x1 1.08 us: per_device(): grad_sgu = fsdp_scatter(grad_sgu, sgu_taken).astype(BF)]
    pallas_call x5, Pallas kernels: 118 us -> 107 us  [the longest x1 66.9 us: weight_grads(): pl.pallas_call(functools.partial(weight_grads_kernel, n, cut, parts), gri...]
  transfers between devices with their start and end apart: 2 -> 2, of which waited for: 0 -> 0; matrix products, arithmetic and copies ran while one was open for 10% -> 4% of each run, Pallas kernels for 63% -> 20%
where the time goes in v3:
time: 954 us; the launch traced here: 948 us
  Pallas kernels  835 us (88%)
  other arithmetic  54.2 us (6%)
  local copies, waits for them, and re-layouts  25.3 us (3%)
  matrix products  18.3 us (2%)
  between operations  15 us (2%)
    pallas_call x5, Pallas kernels, ring_gather_many(): pl.pallas_call(functools.partial(gather_kernel, n, cuts, actives or [None...  374 us
    pallas_call x3, Pallas kernels, expert_call(): pl.pallas_call(functools.partial(kernel, count, most, len(swaps)), grid=(...  166 us
    pallas_call x2, Pallas kernels, ring_scatter(): pl.pallas_call(functools.partial(scatter_kernel, n, cut, len(swaps)), out...  136 us
    pallas_call x1, Pallas kernels, weight_grads(): pl.pallas_call(functools.partial(weight_grads_kernel, n, cut, parts), gri...  66.9 us
    pallas_call x1, Pallas kernels, front(): pl.pallas_call(functools.partial(front_kernel, count, len(swaps), chunks)...  34.2 us
    pallas_call x3, Pallas kernels, widen(): pl.pallas_call(kernel, grid=(steps,), out_shape=[jax.ShapeDtypeStruct((ro...  31.9 us
  transfers between devices with their start and end apart: 2, of which 0 were waited for; matrix products, arithmetic and copies ran while one was open for 4% of the time, Pallas kernels for 20%

profile of v3, /device:TPU:9, one launch (start us, length us, event | category | flops | bytes accessed | tf_op | source)
XLA Modules:
  0.0 948.4 jit_solution(15133935934009936597)
XLA Ops:
  7.2 0.7 copy.77
  9.3 0.7 convert.30
  10.0 0.7 convert.29
  10.7 2.7 copy.53.refs_4_.refs_2_
  13.4 2.4 dynamic-slice_convert_fusion.2.refs_3_.refs_0_
  16.4 1.6 dynamic-slice_convert_fusion.8.refs_5_.refs_4_
  18.0 2.1 dynamic-slice_convert_fusion.1.refs_6_
  20.7 50.1 %ring_gather.5 = (bf16[16,128,2048]{2,1,0:T(8,128)(2,1)}, f32[16,16,128]{2,1,0:T(8,128)}, bf16[32,128]{1,0:T(8,128)(2,1)}, bf16[1024,192]{1,0:T(8,128)(2,1)}, bf...) custom-call(bf16[128,2048]{1,0:T(8,128)(2,1)} %bitcast.103, ...), custom_call_target="tpu_custom_call" | custom-call | bytes 1048576 | tf_op jit(solution)/shard_map/ring_gather/pallas_call | solution.py:269
  70.9 0.7 broadcast_select_fusion.8
  72.9 1.3 copy.54.refs_11_.segc_ref
  74.2 1.3 broadcast_select_fusion.4.wo_ref
  75.5 1.0 copy.55.refs_1_
  76.5 0.9 broadcast_compare_fusion
  77.7 1.2 dynamic-slice_convert_fusion.3
  78.9 0.8 pad.13.refs_14_
  79.7 2.5 dynamic-slice_convert_fusion.5
  82.3 1.4 pad_maximum_fusion.2.refs_13_
  83.7 34.2 %front.1 = (bf16[2048,2048]{1,0:T(8,128)(2,1)}, bf16[2048,512]{1,0:T(8,128)(2,1)}, bf16[2048,192]{1,0:T(8,128)(2,1)}, bf16[2048,192]{1,0:T(8,128)(2,1)}, bf16[20...) custom-call(bf16[1024,192]{1,0:T(8,128)(2,1)} %dynamic-slice_convert, ...), custom_call_target="tpu_custom_call" | custom-call | bytes 1048576 | tf_op jit(solution)/shard_map/front/pallas_call | solution.py:539
  117.9 67.5 %ring_scatter.2 = (f32[128,2048]{1,0:T(8,128)}, bf16[1024,1408]{1,0:T(8,128)(2,1)}) custom-call(bf16[2048,128]{1,0:T(8,128)(2,1)} %get-tuple-element.88.refs_0_.heads_ref, bf16[2048,128]{1,0:T(8,128)(2,1)} %copy.55.refs_1_, bf16[1024,1408]{1,0:T(8,128)(2,1)} %get-tuple-element.90.refs_2_.refs_0_), custom_call_target="tpu_custom_call" | custom-call | bytes 1048576 | tf_op jit(solution)/shard_map/ring_scatter/pallas_call | solution.py:363
  185.4 1.5 multiply_reduce_fusion.2
  187.0 0.9 multiply_convert_fusion.refs_0_
  187.9 67.5 %ring_gather.6 = (bf16[16,128,2048]{2,1,0:T(8,128)(2,1)}, bf16[1024,1408]{1,0:T(8,128)(2,1)}) custom-call(bf16[128,2048]{1,0:T(8,128)(2,1)} %multiply_convert_fusion.refs_0_, bf16[1024,1408]{1,0:T(8,128)(2,1)} %get-tuple-element.93.refs_1_.refs_2_), custom_call_target="tpu_custom_call" | custom-call | bytes 1048576 | tf_op jit(solution)/shard_map/ring_gather/pallas_call | solution.py:269
  255.5 1.6 broadcast_select_fusion.1
  257.1 1.5 multiply_reduce_fusion.5
  259.3 1.2 broadcast_select_fusion.6
  260.6 0.9 pad_maximum_fusion.3.refs_8_.refs_5_
  261.5 2.5 constant_dynamic-slice_fusion.2
  264.7 1.3 pad_maximum_fusion.refs_7_.refs_9_
  266.0 69.4 %experts_in.1 = (bf16[1536,2048]{1,0:T(8,128)(2,1)}, f32[1536,1408]{1,0:T(8,128)}, f32[1536,1408]{1,0:T(8,128)}, bf16[1536,1408]{1,0:T(8,128)(2,1)}, bf16[2048,1...) custom-call(bf16[1024,1408]{1,0:T(8,128)(2,1)} %get-tuple-element.90.refs_2_, ...), custom_call_target="tpu_custom_call" | custom-call | bytes 1048576 | tf_op jit(solution)/shard_map/experts_in/pallas_call | solution.py:746
  335.5 20.6 %experts_out.1 = bf16[2048,2048]{1,0:T(8,128)(2,1)} custom-call(bf16[704,2048]{1,0:T(8,128)(2,1)} %get-tuple-element.95.refs_10_.refs_0_.refs_4_, bf16[704,2048]{1,0:T(8,128)(2,1)} %get-tuple-element.101.refs_1_.refs_5_, bf16[1536,1408]{1,0:T(8,128)(2,1)} %get-tuple-element.103.refs_2_.refs_3_, s32[16,1,128]{2,1,0:T(1,128)} %broadcast_select_fusion.9.refs_5_.refs_3_.refs_7_, ...), custom_call_target="tpu_custom_call" | custom-call | bytes 1048576 | tf_op jit(solution)/shard_map/experts_out/pallas_call | solution.py:746
  356.1 75.6 %experts_back.1 = (bf16[2048,2048]{1,0:T(8,128)(2,1)}, bf16[1536,1408]{1,0:T(8,128)(2,1)}, bf16[1536,1408]{1,0:T(8,128)(2,1)}, f32[128,2048]{1,0:T(8,128)}) custom-call(bf16[1024,1408]{1,0:T(8,128)(2,1)} %get-tuple-element.90.refs_2_.refs_0_, bf16[1024,1408]{1,0:T(8,128)(2,1)} %get-tuple-element.92.refs_1_, ...), custom_call_target="tpu_custom_call" | custom-call | bytes 1048576 | tf_op jit(solution)/shard_map/experts_back/pallas_call | solution.py:746
  431.7 66.9 %weight_grads.1 = (f32[128,2048]{1,0:T(8,128)}, bf16[2048,1408]{1,0:T(8,128)(2,1)}, bf16[2048,1408]{1,0:T(8,128)(2,1)}, bf16[1408,2048]{1,0:T(8,128)(2,1)}, bf16...) custom-call(bf16[1536,2048]{1,0:T(8,128)(2,1)} %get-tuple-element.109.refs_0_, ...), custom_call_target="tpu_custom_call" | custom-call | bytes 1048576 | tf_op jit(solution)/shard_map/weight_grads/pallas_call | solution.py:895
  498.6 1.5 multiply_reduce_fusion
  500.2 2.4 fusion.44.refs_0_
  502.6 48.1 %ring_gather.7 = (bf16[16,128,2048]{2,1,0:T(8,128)(2,1)}, bf16[1024,352]{1,0:T(8,128)(2,1)}, bf16[96,2048]{1,0:T(8,128)(2,1)}) custom-call(bf16[128,2048]{1,0:T(8,128)(2,1)} %fusion.44.refs_0_, bf16[2048,352]{1,0:T(8,128)(2,1)} %get-tuple-element.118.refs_1_, bf16[192,2048]{1,0:T(8,128)(2,1)} %get-tuple-element.119.refs_2_), custom_call_target="tpu_custom_call" | custom-call | bytes 1048576 | tf_op jit(solution)/shard_map/ring_gather/pallas_call | solution.py:269
  550.7 18.7 %attend_back.1 = (bf16[2048,512]{1,0:T(8,128)(2,1)}, bf16[128,2048]{1,0:T(8,128)(2,1)}) custom-call(bf16[2048,192]{1,0:T(8,128)(2,1)} %get-tuple-element.114.qh_ref, bf16[2048,192]{1,0:T(8,128)(2,1)} %get-tuple-element.115.kh_ref, bf16[2048,128]{1,0:T(8,128)(2,1)} %get-tuple-element.116.v_ref, f32[2048,1]{1,0:T(8,128)} %get-tuple-element.117.lse_ref, ...), custom_call_target="tpu_custom_call" | custom-call | bytes 1048576 | tf_op jit(solution)/shard_map/attend_back/pallas_call | solution.py:587
  569.4 68.4 %ring_scatter.3 = (f32[128,2688]{1,0:T(8,128)}, bf16[704,2048]{1,0:T(8,128)(2,1)}) custom-call(bf16[2048,512]{1,0:T(8,128)(2,1)} %get-tuple-element.121.refs_0_, bf16[2688,512]{1,0:T(8,128)(2,1)} %get-tuple-element.122.refs_1_, bf16[1408,2048]{1,0:T(8,128)(2,1)} %get-tuple-element.123.refs_2_), custom_call_target="tpu_custom_call" | custom-call | bytes 1048576 | tf_op jit(solution)/shard_map/ring_scatter/pallas_call | solution.py:363
  637.9 0.8 slice.73
  638.7 1.1 multiply_reduce_fusion.3
  639.8 1.1 subtract_convert_fusion
  640.9 3.8 fusion.22
  645.4 8.6 convolution_convert_fusion
  654.3 1.5 convolution_convert_fusion.1.refs_4_
  655.8 1.1 add_convert_fusion.refs_0_
  656.9 0.8 add_convert_fusion.3.refs_1_
  657.7 1.2 pad_maximum_fusion.1.refs_3_
  659.5 109.8 %ring_gather.8 = (bf16[16,1024,352]{2,1,0:T(8,128)(2,1)}, bf16[16,96,2048]{2,1,0:T(8,128)(2,1)}, bf16[16,128,576]{2,1,0:T(8,128)(2,1)}, bf16[1024,192]{1,0:T(8,1...) custom-call(bf16[1024,352]{1,0:T(8,128)(2,1)} %add_convert_fusion.re, ...), custom_call_target="tpu_custom_call" | custom-call | bytes 1048576 | tf_op jit(solution)/shard_map/ring_gather/pallas_call | solution.py:269
  769.3 2.1 add_convert_fusion.1.refs_0_
  771.5 2.9 convolution_convert_fusion.2
  774.4 0.8 collective-permute-start
  775.2 5.1 add_bitcast_fusion.2
  780.3 0.7 add_convert_fusion.4.refs_1_
  781.0 3.7 add_bitcast_fusion
  784.8 1.8 fusion.18
  787.3 0.9 add.189.refs_2_
  788.2 15.6 %wide_shared.1 = (f32[1024,2816]{1,0:T(8,128)}, f32[1024,2816]{1,0:T(8,128)}) custom-call(bf16[16,1024,352]{2,1,0:T(8,128)(2,1)} %get-tuple-element.142.i_ref), custom_call_target="tpu_custom_call" | custom-call | bytes 1048576 | tf_op jit(solution)/shard_map/wide_shared/pallas_call | solution.py:929
  803.8 7.9 trim.1
  812.4 98.0 %ring_gather.9 = (bf16[16,1024,192]{2,1,0:T(8,128)(2,1)}, bf16[16,256,256]{2,1,0:T(8,128)(2,1)}, bf16[16,128,2048]{2,1,0:T(8,128)(2,1)}, bf16[16,64,576]{2,1,0:T...) custom-call(bf16[1024,192]{1,0:T(8,128)(2,1)} %add_convert_fusion.1.refs_0_, ...), custom_call_target="tpu_custom_call" | custom-call | bytes 1048576 | tf_op jit(solution)/shard_map/ring_gather/pallas_call | solution.py:269
  910.4 10.1 %wide_q.1 = f32[1024,3072]{1,0:T(8,128)} custom-call(bf16[16,1024,192]{2,1,0:T(8,128)(2,1)} %get-tuple-element.138.i_ref), custom_call_target="tpu_custom_call" | custom-call | bytes 1048576 | tf_op jit(solution)/shard_map/wide_q/pallas_call | solution.py:929
  920.5 1.5 bitcast_convert_fusion
  922.0 2.0 copy.62
  924.0 6.1 wide_kv.1
  930.1 6.8 dynamic-slice_convert_fusion
  936.9 3.1 add_bitcast_fusion.1
  (125 shorter events, 9.8 us)
Async XLA Ops:
  7.2 258.9 %all-gather.2.cloned.1.call-start = ((), (), s32[]{:S(2)}) async-start(), calls=%async_computation | async-start | bytes 8912896 | tf_op jit(solution)/shard_map/all_gather | solution.py:1014
  20.7 52.1 %copy-start.35 = (s32[1,2048]{1,0:T(1,128)S(1)}, s32[1,2048]{1,0:T(1,128)}, u32[]{:S(2)}) copy-start(s32[1,2048]{1,0:T(1,128)} %segr_ref.1) | copy-start | bytes 24580
  75.5 8.1 copy-start.4
  77.4 181.3 %copy-start.33 = (f32[16,1,128]{2,1,0:T(1,128)}, f32[16,1,128]{2,1,0:T(1,128)S(1)}, u32[]{:S(2)}) copy-start(f32[16,1,128]{2,1,0:T(1,128)S(1)} %get-tuple-element.201.refs_6_.refs_4_.refs_8_) | copy-start | bytes 24580
  82.3 1.4 copy-start.9
  82.3 1.4 copy-start.11
  82.3 1.4 copy-start.13
  82.3 1.4 copy-start.15
  117.9 67.5 %copy-start.2 = (bf16[1,128,2048]{2,1,0:T(8,128)(2,1)S(1)}, bf16[1,128,2048]{2,1,0:T(8,128)(2,1)}, u32[]{:S(2)}) copy-start(bf16[1,128,2048]{2,1,0:T(8,128)(2,1)} %param.20) | copy-start | bytes 1572868
  186.9 68.6 %copy-start = (bf16[1024,576]{1,0:T(8,128)(2,1)S(1)}, bf16[1024,576]{1,0:T(8,128)(2,1)}, u32[]{:S(2)}) copy-start(bf16[1024,576]{1,0:T(8,128)(2,1)} %copy.53.refs_4_.refs_2_) | copy-start | bytes 3538948
  257.1 3.5 copy-start.20
  257.1 3.5 copy-start.22
  257.1 2.2 copy-start.32
  258.7 5.4 copy-start.10
  258.7 5.4 copy-start.12
  258.7 5.4 copy-start.14
  258.7 5.4 copy-start.16
  258.7 5.4 copy-start.27
  431.7 68.4 %copy-start.3 = (bf16[1,128,2048]{2,1,0:T(8,128)(2,1)S(1)}, bf16[1,128,2048]{2,1,0:T(8,128)(2,1)}, u32[]{:S(2)}) copy-start(bf16[1,128,2048]{2,1,0:T(8,128)(2,1)} %param.24) | copy-start | bytes 1572868
  569.4 69.3 %copy-start.25 = (f32[128,512]{1,0:T(8,128)S(1)}, f32[128,512]{1,0:T(8,128)}, u32[]{:S(2)}) copy-start(f32[128,512]{1,0:T(8,128)} %get-tuple-element.229) | copy-start | bytes 786436
  569.4 71.5 %copy-start.21 = (bf16[1024,576]{1,0:T(8,128)(2,1)S(1)}, bf16[1024,576]{1,0:T(8,128)(2,1)}, u32[]{:S(2)}) copy-start(bf16[1024,576]{1,0:T(8,128)(2,1)} %copy-done.20) | copy-start | bytes 3538948
  640.9 4.5 copy-start.18
  645.4 8.8 copy-start.37
  654.2 1.5 copy-start.5
  654.2 1.6 copy-start.26
  654.2 2.6 copy-start.19
  654.2 2.6 copy-start.31
  769.3 5.9 copy-start.7
  771.5 9.5 %slice-start.2 = ((s8[5767168]{0:T(1024)(128)(4,1)}), s8[4194304]{0:T(1024)(128)(4,1)S(1)}, s32[]{:S(2)}) async-start(s8[5767168]{0:T(1024)(128)(4,1)} %bitcast.95), calls=%async_computation.3 | async-start | bytes 8388608
  774.4 37.3 %collective-permute-start = (bf16[64,576]{1,0:T(8,128)(2,1)S(1)}, bf16[64,576]{1,0:T(8,128)(2,1)S(1)}, u32[]{:S(2)}, u32[]{:S(2)}) collective-permute-start(bf16[64,576]{1,0:T(8,128)(2,1)S(1)} %constant_dynamic-slice_fusion), channel_id=1, source_target_pairs={{0,1},{1,0},{2,3},{3,2},{4,5},{5,4},{6,7},{7,6},{8,9},{9,8},{10,11... | collective-permute-start | bytes 221192 | tf_op jit(solution)/shard_map/ppermute | solution.py:1196
  775.2 5.1 copy-start.28
  775.2 5.1 copy-start.34
  775.2 5.8 slice-start.3
  775.2 5.8 copy-start.6
  781.0 3.8 copy-start.1
  781.0 3.8 copy-start.23
  781.0 3.8 copy-start.24
  784.8 1.9 copy-start.36
  784.8 2.5 copy-start.17
  784.8 2.5 copy-start.29
  924.0 12.9 %slice-start = ((s8[5767168]{0:T(1024)(128)(4,1)}), s8[1572864]{0:T(1024)(128)(4,1)S(1)}, s32[]{:S(2)}) async-start(s8[5767168]{0:T(1024)(128)(4,1)} %bitcast.93), calls=%async_computation.1 | async-start | bytes 3145728
  930.1 6.8 slice-start.1
  930.1 6.8 copy-start.8
  936.9 3.1 copy-start.30
Sparse Core Ops, SparseCore 0:
  71.0 81.2 all-gather.1

commit v4 on v3

--- a/solution.py
+++ b/solution.py
@@ -159,6 +159,83 @@
             save(c).wait()
 
 
+def neighbours(n):
+    _, core, r, _ = ring_place()
+    return ring_seq((r + 1) % n, core, n), ring_seq((r + n - 1) % n, core, n), ring_seq(r, 1 - core, n)
+
+
+def gather_steps(n, cuts, actives, x_refs, o_refs, own_sem, local_sem, sems):
+    count = len(cuts)
+    me, core, r, _ = ring_place()
+    *targets, sibling = neighbours(n)
+
+    def block(t, d, c):
+        return ring_seq((r + (-t if d == 0 else t) + n) % n, c, n)
+
+    def guarded(i, source, action):
+        if actives[i] is None:
+            action()
+        else:
+            pl.when(actives[i](source))(action)
+
+    def parts_of(i):
+        height = x_refs[i].shape[0] // (2 * cuts[i])
+        for k in range(cuts[i]):
+            for d in range(2):
+                yield k, d, pl.ds((d * cuts[i] + k) * height, height)
+
+    def onward(i, t, d, k, rows):
+        at = o_refs[i].at[block(t, d, core), rows]
+        source = x_refs[i].at[rows] if t == 0 else at
+        return remote(source, at, sems[4 * i].at[t, d, k], sems[4 * i + 1].at[t, d, k], targets[d])
+
+    def across(i, t, d, k, rows, c):
+        at = o_refs[i].at[block(t, d, c), rows]
+        return remote(at, at, sems[4 * i + 2].at[t - 1, d, k], sems[4 * i + 3].at[t - 1, d, k], sibling)
+
+    def local(i):
+        return pltpu.make_async_copy(x_refs[i], o_refs[i].at[me], local_sem.at[i])
+
+    def own(i):
+        return remote(x_refs[i], o_refs[i].at[me], own_sem.at[i, 0], own_sem.at[i, 1], sibling)
+
+    for i in range(count):
+        local(i).start()
+        for k, d, rows in parts_of(i):
+            guarded(i, me, lambda: onward(i, 0, d, k, rows).start())
+        guarded(i, me, lambda: own(i).start())
+    yield
+    for t in range(n - 1):
+        for i in range(count):
+            for k, d, rows in parts_of(i):
+
+                def step():
+                    onward(i, t, d, k, rows).wait_recv()
+                    if t < n - 2:
+                        onward(i, t + 1, d, k, rows).start()
+                    across(i, t + 1, d, k, rows, core).start()
+
+                guarded(i, block(t + 1, d, core), step)
+        yield
+    for i in range(count):
+        local(i).wait()
+        guarded(i, me, lambda: own(i).wait_send())
+        guarded(i, sibling, lambda: own(i).wait_recv())
+        for t in range(n - 1):
+            for k, d, rows in parts_of(i):
+                guarded(i, block(t, d, core), lambda: onward(i, t, d, k, rows).wait_send())
+                guarded(i, block(t + 1, d, core), lambda: across(i, t + 1, d, k, rows, core).wait_send())
+                guarded(i, block(t + 1, d, 1 - core), lambda: across(i, t + 1, d, k, rows, 1 - core).wait_recv())
+
+
+def gather_cut(height):
+    return 2 if height % 64 == 0 else 1
+
+
+def gather_sems(n, cuts):
+    return [pltpu.SemaphoreType.DMA((n - 1, 2, cut)) for cut in cuts for _ in range(4)]
+
+
 def gather_kernel(n, cuts, actives, swaps, shared, casts, *refs):
     count = len(cuts)
     total = count + swaps
@@ -168,10 +245,9 @@
     own_sem, local_sem, swap_sems, hand_sem = refs[total + casts : total + casts + 4]
     sems = refs[total + casts + 4 :]
     casting = cast_steps(wide_refs, narrow_refs, sems[4 * count :])
-    me, core, r, _ = ring_place()
-    targets = (ring_seq((r + 1) % n, core, n), ring_seq((r + n - 1) % n, core, n))
-    sibling = ring_seq(r, 1 - core, n)
-    greet((*targets, sibling), swaps > 0)
+    _, core, _, _ = ring_place()
+    greet(neighbours(n), swaps > 0)
+    sibling = neighbours(n)[2]
 
     def half_of(ref, c):
         height = ref.shape[0] // 2
@@ -188,66 +264,16 @@
         half = half_of(take_refs[shared], c)
         return remote(half, half, hand_sem.at[0], hand_sem.at[1], sibling)
 
-    def block(t, d, c):
-        return ring_seq((r + (-t if d == 0 else t) + n) % n, c, n)
-
-    def guarded(i, source, action):
-        if actives[i] is None:
-            action()
-        else:
-            pl.when(actives[i](source))(action)
-
-    def parts_of(i):
-        height = x_refs[i].shape[0] // (2 * cuts[i])
-        for k in range(cuts[i]):
-            for d in range(2):
-                yield k, d, pl.ds((d * cuts[i] + k) * height, height)
-
-    def onward(i, t, d, k, rows):
-        at = o_refs[i].at[block(t, d, core), rows]
-        source = x_refs[i].at[rows] if t == 0 else at
-        return remote(source, at, sems[4 * i].at[t, d, k], sems[4 * i + 1].at[t, d, k], targets[d])
-
-    def across(i, t, d, k, rows, c):
-        at = o_refs[i].at[block(t, d, c), rows]
-        return remote(at, at, sems[4 * i + 2].at[t - 1, d, k], sems[4 * i + 3].at[t - 1, d, k], sibling)
-
-    def local(i):
-        return pltpu.make_async_copy(x_refs[i], o_refs[i].at[me], local_sem.at[i])
-
-    def own(i):
-        return remote(x_refs[i], o_refs[i].at[me], own_sem.at[i, 0], own_sem.at[i, 1], sibling)
-
-    for i in range(count):
-        local(i).start()
-        for k, d, rows in parts_of(i):
-            guarded(i, me, lambda: onward(i, 0, d, k, rows).start())
-        guarded(i, me, lambda: own(i).start())
-    for t in range(n - 1):
-        for i in range(count):
-            for k, d, rows in parts_of(i):
-
-                def step():
-                    arriving = onward(i, t, d, k, rows)
-                    arriving.wait_recv()
-                    if t < n - 2:
-                        onward(i, t + 1, d, k, rows).start()
-                    across(i, t + 1, d, k, rows, core).start()
-
-                guarded(i, block(t + 1, d, core), step)
+    steps = gather_steps(n, cuts, actives, x_refs, o_refs, own_sem, local_sem, sems)
+    next(steps)
+    for _ in range(n - 1):
+        next(steps)
         for _ in range(4):
             next(casting, None)
     for _ in casting:
         pass
-    for i in range(count):
-        local(i).wait()
-        guarded(i, me, lambda: own(i).wait_send())
-        guarded(i, sibling, lambda: own(i).wait_recv())
-        for t in range(n - 1):
-            for k, d, rows in parts_of(i):
-                guarded(i, block(t, d, core), lambda: onward(i, t, d, k, rows).wait_send())
-                guarded(i, block(t + 1, d, core), lambda: across(i, t + 1, d, k, rows, core).wait_send())
-                guarded(i, block(t + 1, d, 1 - core), lambda: across(i, t + 1, d, k, rows, 1 - core).wait_recv())
+    for _ in steps:
+        pass
     if shared is not None:
         swapped[shared].wait_recv()
         handed(core).start()
@@ -263,9 +289,9 @@
 def ring_gather_many(operands, collective_id, actives=None, swaps=(), shared=None, casts=()):
     devices = lax.axis_size("seq")
     n = devices // 2
-    cuts = [2 if x.shape[0] % 64 == 0 else 1 for x in operands]
+    cuts = [gather_cut(x.shape[0]) for x in operands]
     anywhere = pl.BlockSpec(memory_space=pl.ANY)
-    sems = [pltpu.SemaphoreType.DMA((n - 1, 2, cut)) for cut in cuts for _ in range(4)]
+    sems = gather_sems(n, cuts)
     return pl.pallas_call(
         functools.partial(gather_kernel, n, cuts, actives or [None] * len(operands), len(swaps), shared, len(casts)),
         out_shape=[jax.ShapeDtypeStruct((devices, *x.shape), x.dtype) for x in operands]
@@ -294,15 +320,25 @@
     return out.reshape(-1, x.shape[1]), taken
 
 
-def scatter_kernel(n, cut, swaps, *refs):
+def scatter_kernel(n, cut, swaps, beside, *refs):
     a_ref, w_ref = refs[:2]
-    o_ref = refs[2 + swaps]
-    stage, sibbuf, rbuf, sbuf, send, recv, fsend, frecv, swap_sems = refs[3 + 2 * swaps :]
+    gives, refs = refs[2 : 2 + swaps], refs[2 + swaps :]
+    if beside:
+        act_hbm, cn_hbm, *refs = refs
+    o_ref, takes, refs = refs[0], refs[1 : 1 + swaps], refs[1 + swaps :]
+    if beside:
+        nope_ref, rope_ref, expand_ref, *refs = refs
+    stage, sibbuf, rbuf, sbuf, send, recv, fsend, frecv, swap_sems, *refs = refs
+    if beside:
+        act, cn, sems = refs
+        loads = [pltpu.make_async_copy(act_hbm, act, sems.at[0]), pltpu.make_async_copy(cn_hbm, cn, sems.at[1])]
+        for load in loads:
+            load.start()
     me, core, r, _ = ring_place()
     targets = (ring_seq((r + 1) % n, core, n), ring_seq((r + n - 1) % n, core, n))
     sibling = ring_seq(r, 1 - core, n)
     greet((*targets, sibling), swaps > 0)
-    swapped = swap_copies(refs[2 : 2 + swaps], refs[3 + swaps : 3 + 2 * swaps], swap_sems)
+    swapped = swap_copies(gives, takes, swap_sems)
     for copy in swapped:
         copy.start()
     height, columns = o_ref.shape
@@ -343,6 +379,17 @@
                 onward(t, d).start()
             else:
                 o_ref[:, spans[d]] = value
+        if beside and t == 0:
+            for load in loads:
+                load.wait()
+        if beside:
+            slab = act.shape[1] // n
+            rows = slice(t * slab, (t + 1) * slab)
+            grad = mm_tn(act[:, rows], a_ref[...])
+            nope_ref[rows, :] = grad[:, :NOPE].astype(BF)
+            rope_ref[rows, :] = grad[:, KV_END:QK_END].astype(BF)
+        if beside and t == 1:
+            expand_ref[...] = mm_tn(cn[...], a_ref[:, NOPE:KV_END]).astype(BF)
     for t in range(n):
         for d in range(2):
             across(t, d).wait_send()
@@ -352,7 +399,7 @@
         copy.wait()
 
 
-def ring_scatter(a, w, collective_id, swaps=()):
+def ring_scatter(a, w, collective_id, swaps=(), beside=()):
     devices = lax.axis_size("seq")
     n = devices // 2
     rows = a.shape[0] // devices
@@ -360,11 +407,16 @@
     cut = columns // 256 * 128
     vmem = pl.BlockSpec(memory_space=pltpu.VMEM)
     anywhere = [pl.BlockSpec(memory_space=pl.ANY)] * len(swaps)
+    grads, held = [], []
+    if beside:
+        width, rank = (x.shape[1] for x in beside)
+        grads = [jax.ShapeDtypeStruct(shape, BF) for shape in ((width, NOPE), (width, ROPE), (rank, NOPE + V_DIM))]
+        held = [pltpu.VMEM(x.shape, BF) for x in beside] + [pltpu.SemaphoreType.DMA((2,))]
     out, *taken = pl.pallas_call(
-        functools.partial(scatter_kernel, n, cut, len(swaps)),
-        out_shape=[jax.ShapeDtypeStruct((rows, columns), F32)] + swap_shapes(swaps),
-        in_specs=[vmem, vmem] + anywhere,
-        out_specs=[vmem] + anywhere,
+        functools.partial(scatter_kernel, n, cut, len(swaps), len(beside) > 0),
+        out_shape=[jax.ShapeDtypeStruct((rows, columns), F32)] + swap_shapes(swaps) + grads,
+        in_specs=[vmem, vmem] + anywhere + [pl.BlockSpec(memory_space=pl.ANY)] * len(beside),
+        out_specs=[vmem] + anywhere + [vmem] * len(grads),
         scratch_shapes=[
             pltpu.VMEM((n, rows, columns), BF),
             pltpu.VMEM((n, rows, columns), BF),
@@ -373,14 +425,15 @@
         ]
         + [pltpu.SemaphoreType.DMA((n - 1, 2))] * 2
         + [pltpu.SemaphoreType.DMA((n, 2))] * 2
-        + [pltpu.SemaphoreType.DMA((max(1, len(swaps)), 2))],
+        + [pltpu.SemaphoreType.DMA((max(1, len(swaps)), 2))]
+        + held,
         compiler_params=pltpu.CompilerParams(
             collective_id=collective_id, has_side_effects=True, vmem_limit_bytes=VMEM_LIMIT
         ),
         cost_estimate=COST,
         name="ring_scatter",
-    )(a, w, *swap_arrays(swaps))
-    return out, taken
+    )(a, w, *swap_arrays(swaps), *beside)
+    return (out, *taken[len(swaps) :], taken[: len(swaps)])
 
 
 def fsdp_gather(x, other=None):
@@ -554,9 +607,9 @@
     )(*sum(pieces, ()), x, gain, lgain, cosine, sine, seg_col, seg_row, *swaps)
 
 
-def attend_back_kernel(
-    qh_ref, kh_ref, v_ref, lse_ref, heads_ref, da_ref, wo_ref, cos_ref, sin_ref, segc_ref, segr_ref, back_ref, gout_ref, dk_acc, dv_acc
-):
+def attend_back_kernel(*refs):
+    qh_ref, kh_ref, v_ref, lse_ref, heads_ref, da_ref, wo_ref, cos_ref, sin_ref, segc_ref, segr_ref = refs[:11]
+    back_ref, gout_ref, dk_acc, dv_acc = refs[11:]
     dk_acc[...] = jnp.zeros_like(dk_acc)
     dv_acc[...] = jnp.zeros_like(dv_acc)
     for start, step, low in spans_of(qh_ref.shape[0]):
@@ -582,17 +635,18 @@
     gout_ref[...] = mm_tn(heads_ref[...], da_ref[...]).astype(BF)
 
 
-def local_call(kernel, outs, scratch, name, *operands):
+def attend_back(*operands):
+    length, width = operands[5].shape
     vmem = pl.BlockSpec(memory_space=pltpu.VMEM)
     return pl.pallas_call(
-        kernel,
-        out_shape=[jax.ShapeDtypeStruct(shape, dtype) for shape, dtype in outs],
+        attend_back_kernel,
+        out_shape=[jax.ShapeDtypeStruct((length, QK_END + ROPE), BF), jax.ShapeDtypeStruct((V_DIM, width), BF)],
         in_specs=[vmem] * len(operands),
-        out_specs=[vmem] * len(outs),
-        scratch_shapes=scratch,
+        out_specs=[vmem, vmem],
+        scratch_shapes=[pltpu.VMEM((length, QD), F32), pltpu.VMEM((length, V_DIM), F32)],
         compiler_params=pltpu.CompilerParams(vmem_limit_bytes=VMEM_LIMIT),
         cost_estimate=COST,
-        name=name,
+        name="attend_back",
     )(*operands)
 
 
@@ -645,8 +699,8 @@
     wg_parts, wu_parts = refs[:count], refs[count : 2 * count]
     act_ref, slot_ref, share_ref, wsgu_ref, wsd_ref, g_ref = refs[2 * count : 2 * count + 6]
     gives, refs = refs[2 * count + 6 : 2 * count + 6 + swaps], refs[2 * count + 6 + swaps :]
-    xe_ref, ge_ref, ue_ref, he_ref, sh_ref, dye_ref, dsgu_ref = refs[:7]
-    takes, (wg, wu, sems, swap_sems) = refs[7 : 7 + swaps], refs[7 + swaps :]
+    xe_ref, ge_ref, ue_ref, he_ref, sh_ref, dye_ref, dsgu_ref, ys_ref, ds_ref = refs[:9]
+    takes, (wg, wu, sems, swap_sems) = refs[9 : 9 + swaps], refs[9 + swaps :]
     swapped = swap_copies(gives, takes, swap_sems) if swaps else []
     if swaps:
 
@@ -672,6 +726,8 @@
     dsh = mm_nt(g_ref[...], wsd_ref[...])
     dsgu_ref[:, :units] = (dsh * su * sig * (1.0 + sg * (1.0 - sig))).astype(BF)
     dsgu_ref[:, units:] = (dsh * sg * sig).astype(BF)
+    ys_ref[...] = mm(sh_ref[...], wsd_ref[...]).astype(BF)
+    ds_ref[...] = mm_nt(dsgu_ref[...], wsgu_ref[...]).astype(BF)
     wait_first(copies)
     for low, high in hidden_spans(wg.shape[1]):
         ge = mm(xe_ref[...], wg[:, low:high])
@@ -689,7 +745,7 @@
 
 def expert_out_kernel(count, most, swaps, *refs):
     wd_parts = refs[:count]
-    he_ref, slot_ref, share_ref, wsd_ref, sh_ref, y_ref, wd, sems, _ = refs[count:]
+    he_ref, slot_ref, share_ref, ys_ref, y_ref, wd, sems, _ = refs[count:]
     copies = [fill(wd_parts, wd, sems.at[0])]
     start_first(copies)
     wait_first(copies)
@@ -698,15 +754,15 @@
     for b in range(blocks):
         pick, share = picks(slot_ref, share_ref, b, most)
         ye = z[b * most : (b + 1) * most, :].astype(F32)
-        ys = mm(sh_ref[b * rows : (b + 1) * rows, :], wsd_ref[...])
+        ys = ys_ref[b * rows : (b + 1) * rows, :].astype(F32)
         y_ref[b * rows : (b + 1) * rows, :] = (ys + mm_tn(pick, (share * ye).astype(BF))).astype(BF)
 
 
 def expert_back_kernel(n, cut, count, most, swaps, *refs):
     wg_parts, wu_parts, wd_parts = refs[:count], refs[count : 2 * count], refs[2 * count : 3 * count]
-    dye_ref, slot_ref, share_ref, wsgu_ref, part_ref, ge_ref, ue_ref, dsgu_ref = refs[3 * count : 3 * count + 8]
-    dact_ref, dge_ref, due_ref, y_ref = refs[3 * count + 8 : 3 * count + 12]
-    wg, wu, wd, sems, _, *buffers = refs[3 * count + 12 :]
+    dye_ref, slot_ref, share_ref, part_ref, ge_ref, ue_ref, ds_ref = refs[3 * count : 3 * count + 7]
+    dact_ref, dge_ref, due_ref, y_ref = refs[3 * count + 7 : 3 * count + 11]
+    wg, wu, wd, sems, _, *buffers = refs[3 * count + 11 :]
     copies = [fill(p, w, sems.at[i]) for i, (p, w) in enumerate(((wg_parts, wg), (wu_parts, wu), (wd_parts, wd)))]
     start_first(copies)
     finish = scatter_in_grid(pl.program_id(0), n, cut, part_ref, y_ref, buffers)
@@ -722,7 +778,7 @@
     for b in range(blocks):
         pick, _ = picks(slot_ref, share_ref, b, most)
         block = slice(b * rows, (b + 1) * rows)
-        shared = mm_nt(dsgu_ref[block, :], wsgu_ref[...])
+        shared = ds_ref[block, :].astype(F32)
         dact_ref[block, :] = (shared + mm_tn(pick, dxe[b * most : (b + 1) * most, :])).astype(BF)
     finish()
 
@@ -766,25 +822,60 @@
     )(*sum(pieces, ()), tiled[0], slot, share, *whole, *tiled[1:], *swaps)
 
 
-def trim(stacked, share):
-    devices, room, width = stacked.shape
+def widen_query(nope, rope):
+    devices, rows, _ = nope.shape
+    steps = 8
+    step = rows // steps
+
+    def kernel(n_ref, r_ref, o_ref):
+        def put(first):
+            for d in range(devices):
+                o_ref[:, d * QD : d * QD + NOPE] = n_ref[d].astype(F32)
+                o_ref[:, d * QD + NOPE : (d + 1) * QD] = r_ref[d, :, first : first + ROPE].astype(F32)
+
+        low = pl.program_id(0) < steps // 2
+        pl.when(low)(lambda: put(0))
+        pl.when(jnp.logical_not(low))(lambda: put(ROPE))
+
+    return pl.pallas_call(
+        kernel,
+        grid=(steps,),
+        out_shape=jax.ShapeDtypeStruct((rows, devices * QD), F32),
+        in_specs=[
+            pl.BlockSpec((devices, step, NOPE), lambda i: (0, i, 0)),
+            pl.BlockSpec((devices, step, 2 * ROPE), lambda i: (0, i % (steps // 2), 0)),
+        ],
+        out_specs=pl.BlockSpec((step, devices * QD), lambda i: (i, 0)),
+        compiler_params=pltpu.CompilerParams(vmem_limit_bytes=VMEM_LIMIT),
+        cost_estimate=COST,
+        name="wide_query",
+    )(nope, rope)
+
+
+def trim(stacks, share):
+    devices, _, width = stacks[0].shape
     if share % 8:
-        return stacked[:, :share].reshape(-1, width).astype(F32)
-
-    def kernel(i_ref, o_ref):
-        for d in range(i_ref.shape[0]):
-            o_ref[d * share : (d + 1) * share, :] = i_ref[d, :share, :].astype(F32)
+        return jnp.concatenate(stacks, axis=1)[:, :share].reshape(-1, width).astype(F32)
+
+    def kernel(*refs):
+        *i_refs, o_ref = refs
+        for d in range(i_refs[0].shape[0]):
+            at = d * share
+            for i_ref in i_refs:
+                height = min(i_ref.shape[1], (d + 1) * share - at)
+                o_ref[at : at + height, :] = i_ref[d, :height, :].astype(F32)
+                at += height
 
     return pl.pallas_call(
         kernel,
         grid=(4,),
         out_shape=jax.ShapeDtypeStruct((devices * share, width), F32),
-        in_specs=[pl.BlockSpec((devices // 4, room, width), lambda i: (i, 0, 0))],
+        in_specs=[pl.BlockSpec((devices // 4, x.shape[1], width), lambda i: (i, 0, 0)) for x in stacks],
         out_specs=pl.BlockSpec((devices // 4 * share, width), lambda i: (i, 0)),
         compiler_params=pltpu.CompilerParams(vmem_limit_bytes=VMEM_LIMIT),
         cost_estimate=COST,
         name="trim",
-    )(stacked)
+    )(*stacks)
 
 
 def scatter_in_grid(t, n, cut, part_ref, o_ref, buffers):
@@ -810,9 +901,14 @@
     @pl.when(t == 0)
     def _():
         greet((*targets, sibling))
-        for step in range(n):
+        for step in range(2):
             for d in range(2):
                 across(step, d).start()
+
+    @pl.when(t < n - 2)
+    def _():
+        for d in range(2):
+            across(t + 2, d).start()
 
     for d in range(2):
         across(t, d).wait_recv()
@@ -982,6 +1078,9 @@
     gains = jnp.pad(gains, (0, gains_rows * 128 - gains_size)).reshape(gains_rows, 128)
     out_rows = out_weight.shape[0]
     early_latent = 2
+    share = shared_down.shape[0] // devices
+    share_pad = -(-share // 32) * 32
+    sdown = jnp.pad(rows_of(shared_down, at, share), ((0, share_pad - share), (0, 0)))
     early = (
         gains,
         columns_of(q_weight, at, QD),
@@ -1022,7 +1121,6 @@
     w_out = fsdp_pick(early[4], at * V_DIM // out_rows, others[4])
 
     hidden = shared_down.shape[0] * parts
-    share = shared_down.shape[0] // devices
 
     def shared_columns(weight):
         pieces = [
@@ -1030,9 +1128,7 @@
         ]
         return pieces
 
-    share_pad = -(-share // 32) * 32
     sgu = jnp.concatenate(shared_columns(shared_gate) + shared_columns(shared_up), axis=1).astype(BF)
-    sdown = jnp.pad(rows_of(shared_down, at, share), ((0, share_pad - share), (0, 0)))
 
     cosine, sine = rope_tables(length)
     seg_col, seg_row = segment_ids.reshape(length, 1), segment_ids
@@ -1070,7 +1166,7 @@
     ff = expert_gate.shape[2]
     units = parts * share
     steps = 4
-    xe, ge, ue, he, sh, dye, dsgu, *taken = expert_call(
+    xe, ge, ue, he, sh, dye, dsgu, ys, ds, *taken = expert_call(
         expert_in_kernel,
         "experts_in",
         (w_egate, w_eup),
@@ -1088,6 +1184,8 @@
             (length, units, BF),
             (packed, width, BF),
             (length, 2 * units, BF),
+            (length, width, BF),
+            (length, width, BF),
         ),
         crossing(edown),
         10 if pair else None,
@@ -1102,8 +1200,8 @@
         steps,
         slot,
         share_of,
-        (w_sdown,),
-        (he, sh),
+        (),
+        (he, ys),
         ((length, width, BF),),
     )
     dact_part, dge, due, y_sum = expert_call(
@@ -1114,8 +1212,8 @@
         devices // 2,
         slot,
         share_of,
-        (w_sgu, y_part.reshape(devices, rows, width)),
-        (dye, ge, ue, dsgu),
+        (y_part.reshape(devices, rows, width),),
+        (dye, ge, ue, ds),
         ((length, width, BF), (packed, ff, BF), (packed, ff, BF)),
         (),
         12,
@@ -1133,27 +1231,10 @@
     grad_sdown = fsdp_scatter(grad_sdown, sdown_taken).astype(BF)
     output = (x1 + y_sum).astype(BF)
 
-    back, grad_out = local_call(
-        attend_back_kernel,
-        [((length, QK_END + ROPE), BF), ((V_DIM, width), BF)],
-        [pltpu.VMEM((length, QD), F32), pltpu.VMEM((length, V_DIM), F32)],
-        "attend_back",
-        qh,
-        kh,
-        values,
-        lse,
-        heads,
-        dattn_all,
-        w_out,
-        cosine,
-        sine,
-        seg_col,
-        seg_row,
-    )
-    grad_back = mm_tn(act_one, back).astype(BF)
-    grad_query = jnp.concatenate([grad_back[:, :NOPE], grad_back[:, KV_END:QK_END]], 1)
-    grad_expand = mm_tn(cnorm, back[:, NOPE:KV_END]).astype(BF)
-    summed, taken = ring_scatter(back, w_back, 4, (given(grad_edown),) if pair else ())
+    back, grad_out = attend_back(qh, kh, values, lse, heads, dattn_all, w_out, cosine, sine, seg_col, seg_row)
+    summed, grad_nope, grad_rope, grad_expand, taken = ring_scatter(
+        back, w_back, 4, (given(grad_edown),) if pair else (), (act_one, cnorm)
+    )
     grad_edown = fsdp_scatter(grad_edown, *taken)
 
     r1 = norm_scale(own_xf)
@@ -1174,14 +1255,16 @@
     def in_part(device):
         return device * V_DIM // out_rows == lax.axis_index("fsdp")
 
-    sgu_all, sdown_all, dlatent_all, *taken = ring_gather_many(
-        [grad_sgu, grad_sdown, dlatent],
+    sgu_all, dlatent_all, sdown_all, *taken = ring_gather_many(
+        [grad_sgu, dlatent, grad_sdown],
         5,
         None,
-        (given(grad_query), given(grad_expand), grad_out, small, given(grad_egate)) if pair else (),
-    )
-    query_taken, expand_taken, out_taken, small_taken, egate_taken = crossed(taken, 5)
-    grad_query = fsdp_scatter(grad_query, query_taken).astype(BF)
+        (given(grad_nope), given(grad_rope), given(grad_expand), grad_out, small, given(grad_egate)) if pair else (),
+    )
+    nope_taken, rope_taken, expand_taken, out_taken, small_taken, egate_taken = crossed(taken, 6)
+    grad_nope = fsdp_scatter(grad_nope, nope_taken).astype(BF)
+    grad_rope = fsdp_scatter(grad_rope, rope_taken).astype(BF)
+    grad_rope = jnp.concatenate(jnp.split(grad_rope, 2, axis=0), axis=1)
     grad_expand = fsdp_scatter(grad_expand, expand_taken).astype(BF)
     grad_out = fsdp_sum(grad_out, out_taken)
     small = fsdp_sum(small, small_taken)
@@ -1198,10 +1281,10 @@
         )
     grad_latent = fsdp_scatter(grad_latent, latent_taken).astype(BF)
     latent_pad = -(-slab // 32) * 32
-    query_all, expand_all, out_all, latent_all, small_all, *taken = ring_gather_many(
-        [grad_query, grad_expand, grad_out, jnp.pad(grad_latent, ((0, latent_pad - slab), (0, 0))), small],
+    nope_all, rope_all, expand_all, out_all, latent_all, small_all, *taken = ring_gather_many(
+        [grad_nope, grad_rope, grad_expand, grad_out, jnp.pad(grad_latent, ((0, latent_pad - slab), (0, 0))), small],
         7,
-        [None, None, in_part, None, None],
+        [None, None, None, in_part, None, None],
         (given(grad_eup),) if pair else (),
     )
     (eup_taken,) = crossed(taken, 1)
@@ -1222,7 +1305,7 @@
         output[None],
         input_grad[None],
         own_gains[0],
-        widen(query_all, 1, 1, "wide_q")[0],
+        widen_query(nope_all, rope_all),
         latent_all.reshape(-1, grad_latent.shape[1]).astype(F32),
         own_gains[2],
         widen(expand_all, 1, 1, "wide_kv")[0],
@@ -1230,7 +1313,7 @@
         own_gains[1],
         wide_gate,
         wide_up,
-        trim(sdown_all, share),
+        trim([sdown_all], share),
         grad_egate[None],
         grad_eup[None],
         grad_edown[None],

time: 954 us -> 932 us (0.977)
  Pallas kernels: 835 us -> 820 us
  matrix products: 18.3 us -> 6.47 us
    dot_general x3 -> x1, matrix products: 13 us -> 0.7 us  [mm_tn(): lax.dot_general(a, b, (((0,), (0,)), ((), ())), preferred_element_type=F32)]
    pallas_call x3 -> x4, Pallas kernels: 155 us -> 165 us  [the longest x2 136 us: ring_scatter(): pl.pallas_call(functools.partial(scatter_kernel, n, cut, len(swaps), len(...]
    pallas_call x3 -> x2, Pallas kernels: 31.9 us -> 21.7 us  [widen(): pl.pallas_call(kernel, grid=(steps,), out_shape=[jax.ShapeDtypeStruct((ro...]
    pallas_call x3, Pallas kernels: 166 us -> 156 us  [expert_call(): pl.pallas_call(functools.partial(kernel, count, most, len(swaps)), grid=(...]
  transfers between devices with their start and end apart: 2 -> 2, of which waited for: 0 -> 0; matrix products, arithmetic and copies ran while one was open for 4% -> 4% of each run, Pallas kernels for 20% -> 21%
where the time goes in v4:
time: 932 us; the launch traced here: 927 us
  Pallas kernels  820 us (88%)
  other arithmetic  59 us (6%)
  local copies, waits for them, and re-layouts  25 us (3%)
  between operations  15.3 us (2%)
    pallas_call x5, Pallas kernels, ring_gather_many(): pl.pallas_call(functools.partial(gather_kernel, n, cuts, actives or [None...  366 us
    pallas_call x3, Pallas kernels, expert_call(): pl.pallas_call(functools.partial(kernel, count, most, len(swaps)), grid=(...  156 us
    pallas_call x2, Pallas kernels, ring_scatter(): pl.pallas_call(functools.partial(scatter_kernel, n, cut, len(swaps), len(...  136 us
    pallas_call x1, Pallas kernels, weight_grads(): pl.pallas_call(functools.partial(weight_grads_kernel, n, cut, parts), gri...  68.7 us
    pallas_call x1, Pallas kernels, front(): pl.pallas_call(functools.partial(front_kernel, count, len(swaps), chunks)...  34.2 us
    pallas_call x2, Pallas kernels, widen(): pl.pallas_call(kernel, grid=(steps,), out_shape=[jax.ShapeDtypeStruct((ro...  21.7 us
    pallas_call x1, Pallas kernels, attend_back(): pl.pallas_call(attend_back_kernel, out_shape=[jax.ShapeDtypeStruct((lengt...  18.7 us
  transfers between devices with their start and end apart: 2, of which 0 were waited for; matrix products, arithmetic and copies ran while one was open for 4% of the time, Pallas kernels for 21%

profile of v4, /device:TPU:9, one launch (start us, length us, event | category | flops | bytes accessed | tf_op | source)
XLA Modules:
  0.0 926.5 jit_solution(12751233815692588830)
XLA Ops:
  7.2 0.7 copy.73
  7.9 0.7 copy.74
  9.3 0.7 convert.30
  10.0 0.7 convert.29
  10.7 2.7 copy.51.refs_4_.refs_2_
  13.4 2.4 dynamic-slice_convert_fusion.2.refs_3_.refs_0_
  16.4 1.6 dynamic-slice_convert_fusion.8.refs_5_.refs_4_
  18.0 2.1 dynamic-slice_convert_fusion.1.refs_6_
  20.7 50.1 %ring_gather.5 = (bf16[16,128,2048]{2,1,0:T(8,128)(2,1)}, f32[16,16,128]{2,1,0:T(8,128)}, bf16[32,128]{1,0:T(8,128)(2,1)}, bf16[1024,192]{1,0:T(8,128)(2,1)}, bf...) custom-call(bf16[128,2048]{1,0:T(8,128)(2,1)} %bitcast.98, ...), custom_call_target="tpu_custom_call" | custom-call | bytes 1048576 | tf_op jit(solution)/shard_map/ring_gather/pallas_call | solution.py:295
  70.9 0.7 broadcast_select_fusion.8
  72.8 1.3 copy.52.refs_11_.refs_9_
  74.2 1.3 broadcast_select_fusion.4.refs_6_
  75.5 1.0 copy.53.refs_1_
  76.5 0.9 broadcast_compare_fusion
  77.7 1.2 dynamic-slice_convert_fusion.3
  78.9 0.8 pad.13.refs_14_
  79.7 2.5 dynamic-slice_convert_fusion.5
  82.3 1.4 pad_maximum_fusion.1.refs_13_
  83.7 34.2 %front.1 = (bf16[2048,2048]{1,0:T(8,128)(2,1)}, bf16[2048,512]{1,0:T(8,128)(2,1)}, bf16[2048,192]{1,0:T(8,128)(2,1)}, bf16[2048,192]{1,0:T(8,128)(2,1)}, bf16[20...) custom-call(bf16[1024,192]{1,0:T(8,128)(2,1)} %dynamic-slice_convert, ...), custom_call_target="tpu_custom_call" | custom-call | bytes 1048576 | tf_op jit(solution)/shard_map/front/pallas_call | solution.py:592
  118.0 67.5 %ring_scatter.2 = (f32[128,2048]{1,0:T(8,128)}, bf16[1024,1408]{1,0:T(8,128)(2,1)}) custom-call(bf16[2048,128]{1,0:T(8,128)(2,1)} %get-tuple-element.95.refs_0_.refs_4_, bf16[2048,128]{1,0:T(8,128)(2,1)} %copy.53.refs_1_, bf16[1024,1408]{1,0:T(8,128)(2,1)} %get-tuple-element.97.refs_2_.refs_0_), custom_call_target="tpu_custom_call" | custom-call | bytes 1048576 | tf_op jit(solution)/shard_map/ring_scatter/pallas_call | solution.py:415
  185.5 1.5 multiply_reduce_fusion.2
  187.0 0.9 multiply_convert_fusion.refs_0_
  188.0 67.0 %ring_gather.6 = (bf16[16,128,2048]{2,1,0:T(8,128)(2,1)}, bf16[1024,1408]{1,0:T(8,128)(2,1)}) custom-call(bf16[128,2048]{1,0:T(8,128)(2,1)} %multiply_convert_fusion.refs_0_, bf16[1024,1408]{1,0:T(8,128)(2,1)} %get-tuple-element.100.refs_1_.refs_2_), custom_call_target="tpu_custom_call" | custom-call | bytes 1048576 | tf_op jit(solution)/shard_map/ring_gather/pallas_call | solution.py:295
  255.0 1.6 broadcast_select_fusion.1
  256.6 1.5 multiply_reduce_fusion.5
  258.8 1.2 broadcast_select_fusion.6
  260.1 0.9 pad_maximum_fusion.2.refs_8_
  261.0 2.4 constant_dynamic-slice_fusion.2
  264.1 1.3 pad_maximum_fusion.refs_7_
  265.4 70.4 %experts_in.1 = (bf16[1536,2048]{1,0:T(8,128)(2,1)}, f32[1536,1408]{1,0:T(8,128)}, f32[1536,1408]{1,0:T(8,128)}, bf16[1536,1408]{1,0:T(8,128)(2,1)}, bf16[2048,1...) custom-call(bf16[1024,1408]{1,0:T(8,128)(2,1)} %get-tuple-element.97, ...), custom_call_target="tpu_custom_call" | custom-call | bytes 1048576 | tf_op jit(solution)/shard_map/experts_in/pallas_call | solution.py:802
  335.8 19.0 %experts_out.1 = bf16[2048,2048]{1,0:T(8,128)(2,1)} custom-call(bf16[704,2048]{1,0:T(8,128)(2,1)} %get-tuple-element.102.refs_10_.refs_0_.refs_4_, bf16[704,2048]{1,0:T(8,128)(2,1)} %get-tuple-element.108.refs_1_.refs_5_, bf16[1536,1408]{1,0:T(8,128)(2,1)} %get-tuple-element.110.refs_2_.refs_3_, ...), custom_call_target="tpu_custom_call" | custom-call | bytes 1048576 | tf_op jit(solution)/shard_map/experts_out/pallas_call | solution.py:802
  354.8 66.5 %experts_back.1 = (bf16[2048,2048]{1,0:T(8,128)(2,1)}, bf16[1536,1408]{1,0:T(8,128)(2,1)}, bf16[1536,1408]{1,0:T(8,128)(2,1)}, f32[128,2048]{1,0:T(8,128)}) custom-call(bf16[1024,1408]{1,0:T(8,128)(2,1)} %get-tuple-element.97.refs_2_.refs_0_, bf16[1024,1408]{1,0:T(8,128)(2,1)} %get-tuple-element.99.refs_1_, ...), custom_call_target="tpu_custom_call" | custom-call | bytes 1048576 | tf_op jit(solution)/shard_map/experts_back/pallas_call | solution.py:802
  421.3 68.7 %weight_grads.1 = (f32[128,2048]{1,0:T(8,128)}, bf16[2048,1408]{1,0:T(8,128)(2,1)}, bf16[2048,1408]{1,0:T(8,128)(2,1)}, bf16[1408,2048]{1,0:T(8,128)(2,1)}, bf16...) custom-call(bf16[1536,2048]{1,0:T(8,128)(2,1)} %get-tuple-element.116.refs_0_, ...), custom_call_target="tpu_custom_call" | custom-call | bytes 1048576 | tf_op jit(solution)/shard_map/weight_grads/pallas_call | solution.py:991
  490.0 1.5 multiply_reduce_fusion
  491.6 2.4 fusion.42.refs_0_
  494.0 47.7 %ring_gather.7 = (bf16[16,128,2048]{2,1,0:T(8,128)(2,1)}, bf16[1024,352]{1,0:T(8,128)(2,1)}, bf16[96,2048]{1,0:T(8,128)(2,1)}) custom-call(bf16[128,2048]{1,0:T(8,128)(2,1)} %fusion.42.refs_0_, bf16[2048,352]{1,0:T(8,128)(2,1)} %get-tuple-element.127.refs_1_, bf16[192,2048]{1,0:T(8,128)(2,1)} %get-tuple-element.128.refs_2_), custom_call_target="tpu_custom_call" | custom-call | bytes 1048576 | tf_op jit(solution)/shard_map/ring_gather/pallas_call | solution.py:295
  541.6 18.7 %attend_back.1 = (bf16[2048,512]{1,0:T(8,128)(2,1)}, bf16[128,2048]{1,0:T(8,128)(2,1)}) custom-call(bf16[2048,192]{1,0:T(8,128)(2,1)} %get-tuple-element.123.refs_0_, bf16[2048,192]{1,0:T(8,128)(2,1)} %get-tuple-element.124.refs_1_, bf16[2048,128]{1,0:T(8,128)(2,1)} %get-tuple-element.125.refs_2_, f32[2048,1]{1,0:T(8,128)} %get-tuple-element.126.refs_3_, ...), custom_call_target="tpu_custom_call" | custom-call | bytes 1048576 | tf_op jit(solution)/shard_map/attend_back/pallas_call | solution.py:641
  560.4 68.8 %ring_scatter.3 = (f32[128,2688]{1,0:T(8,128)}, bf16[704,2048]{1,0:T(8,128)(2,1)}, bf16[2048,128]{1,0:T(8,128)(2,1)}, bf16[2048,64]{1,0:T(8,128)(2,1)}, bf16[512,256]{1,0:T(8,128)(2,1)}) custom-call(bf16[2048,512]{1,0:T(8,128)(2,1)} %get-tuple-element.130.refs_0_, bf16[2688,512]{1,0:T(8,128)(2,1)} %get-tuple-element.131.refs_1_, ...), custom_call_target="tpu_custom_call" | custom-call | bytes 1048576 | tf_op jit(solution)/shard_map/ring_scatter/pallas_call | solution.py:415
  629.2 0.8 slice.57
  630.1 1.1 multiply_reduce_fusion.3
  631.2 1.1 subtract_convert_fusion
  632.3 4.2 fusion.22
  636.6 0.7 pad_maximum_fusion.3.refs_1_
  637.8 1.1 add_convert_fusion.refs_0_
  638.8 0.8 add_convert_fusion.2.refs_2_
  640.3 110.7 %ring_gather.8 = (bf16[16,1024,352]{2,1,0:T(8,128)(2,1)}, bf16[16,128,576]{2,1,0:T(8,128)(2,1)}, bf16[16,96,2048]{2,1,0:T(8,128)(2,1)}, bf16[1024,128]{1,0:T(8,1...) custom-call(bf16[1024,352]{1,0:T(8,128)(2,1)} %add_convert_fusion.re, ...), custom_call_target="tpu_custom_call" | custom-call | bytes 1048576 | tf_op jit(solution)/shard_map/ring_gather/pallas_call | solution.py:295
  751.1 2.0 add_convert_fusion.4.refs_0_
  753.0 1.1 add_convert_fusion.3
  754.2 2.0 add.194.refs_3_
  756.2 0.7 convolution_convert_fusion
  758.2 15.6 %wide_shared.1 = (f32[1024,2816]{1,0:T(8,128)}, f32[1024,2816]{1,0:T(8,128)}) custom-call(bf16[16,1024,352]{2,1,0:T(8,128)(2,1)} %get-tuple-element.156.i_ref), custom_call_target="tpu_custom_call" | custom-call | bytes 1048576 | tf_op jit(solution)/shard_map/wide_shared/pallas_call | solution.py:1025
  773.8 7.9 trim.1
  781.8 5.9 add_bitcast_fusion.2
  787.7 0.7 add_convert_fusion.5.refs_2_
  788.4 5.6 add_bitcast_fusion
  794.1 1.8 fusion.18
  796.0 0.8 pad_maximum_fusion.4.refs_1_
  797.4 90.7 %ring_gather.9 = (bf16[16,1024,128]{2,1,0:T(8,128)(2,1)}, bf16[16,512,128]{2,1,0:T(8,128)(2,1)}, bf16[16,256,256]{2,1,0:T(8,128)(2,1)}, bf16[16,128,2048]{2,1,0:...) custom-call(bf16[1024,128]{1,0:T(8,128)(2,1)} %add_convert_fusion.4.refs_0_, ...), custom_call_target="tpu_custom_call" | custom-call | bytes 1048576 | tf_op jit(solution)/shard_map/ring_gather/pallas_call | solution.py:295
  888.1 1.5 bitcast_convert_fusion
  889.6 2.0 copy.59
  891.6 6.1 wide_kv.1
  897.7 6.8 dynamic-slice_convert_fusion
  904.5 3.1 add_bitcast_fusion.1
  908.9 10.3 %wide_query.1 = f32[1024,3072]{1,0:T(8,128)} custom-call(bf16[16,1024,128]{2,1,0:T(8,128)(2,1)} %get-tuple-element.151.n_ref, bf16[16,512,128]{2,1,0:T(8,128)(2,1)} %get-tuple-element.152.r_ref), custom_call_target="tpu_custom_call" | custom-call | bytes 1048576 | tf_op jit(solution)/shard_map/wide_query/pallas_call | solution.py:840
  (138 shorter events, 9.4 us)
Async XLA Ops:
  7.2 258.2 %all-gather.2.cloned.1.call-start = ((), (), s32[]{:S(2)}) async-start(), calls=%async_computation | async-start | bytes 8912896 | tf_op jit(solution)/shard_map/all_gather | solution.py:1113
  20.7 52.1 %copy-start.33 = (s32[1,2048]{1,0:T(1,128)S(1)}, s32[1,2048]{1,0:T(1,128)}, u32[]{:S(2)}) copy-start(s32[1,2048]{1,0:T(1,128)} %refs_10_.2) | copy-start | bytes 24580
  75.5 8.1 copy-start.4
  77.4 180.8 %copy-start.31 = (f32[16,1,128]{2,1,0:T(1,128)}, f32[16,1,128]{2,1,0:T(1,128)S(1)}, u32[]{:S(2)}) copy-start(f32[16,1,128]{2,1,0:T(1,128)S(1)} %get-tuple-element.215.refs_6_.refs_4_.refs_8_) | copy-start | bytes 24580
  82.2 1.4 copy-start.9
  82.3 1.4 copy-start.11
  82.3 1.4 copy-start.13
  82.3 1.4 copy-start.15
  117.9 67.5 %copy-start.2 = (bf16[1,128,2048]{2,1,0:T(8,128)(2,1)S(1)}, bf16[1,128,2048]{2,1,0:T(8,128)(2,1)}, u32[]{:S(2)}) copy-start(bf16[1,128,2048]{2,1,0:T(8,128)(2,1)} %param.20) | copy-start | bytes 1572868
  187.0 68.0 %copy-start = (bf16[1024,576]{1,0:T(8,128)(2,1)S(1)}, bf16[1024,576]{1,0:T(8,128)(2,1)}, u32[]{:S(2)}) copy-start(bf16[1024,576]{1,0:T(8,128)(2,1)} %copy.51.refs_4_.refs_2_) | copy-start | bytes 3538948
  187.0 304.5 %copy-start.41 = (f32[128]{0:T(128)}, f32[128]{0:T(128)S(1)}, u32[]{:S(2)}) copy-start(f32[128]{0:T(128)S(1)} %add_rsqrt_fusion.2) | copy-start | bytes 1540
  187.0 445.2 %copy-start.34 = (f32[2048]{0:T(1024)}, f32[2048]{0:T(1024)S(1)}, u32[]{:S(2)}) copy-start(f32[2048]{0:T(1024)S(1)} %get-tuple-element.247) | copy-start | bytes 24580
  255.0 377.3 %copy-start.45 = (f32[128]{0:T(128)}, f32[128]{0:T(128)S(1)}, u32[]{:S(2)}) copy-start(f32[128]{0:T(128)S(1)} %add_rsqrt_fusion.1) | copy-start | bytes 1540
  256.6 3.5 copy-start.20
  256.6 3.5 copy-start.21
  256.6 2.2 copy-start.30
  258.2 5.2 copy-start.10
  258.2 5.2 copy-start.12
  258.2 5.2 copy-start.14
  258.2 5.2 copy-start.16
  258.2 5.2 copy-start.26
  421.3 70.3 %copy-start.3 = (bf16[1,128,2048]{2,1,0:T(8,128)(2,1)S(1)}, bf16[1,128,2048]{2,1,0:T(8,128)(2,1)}, u32[]{:S(2)}) copy-start(bf16[1,128,2048]{2,1,0:T(8,128)(2,1)} %param.24) | copy-start | bytes 1572868
  491.6 50.1 %copy-start.43 = (f32[128]{0:T(128)}, f32[128]{0:T(128)S(1)}, u32[]{:S(2)}) copy-start(f32[128]{0:T(128)S(1)} %broadcast_multiply_fusion.2) | copy-start | bytes 1540
  560.4 69.7 %copy-start.24 = (f32[128,512]{1,0:T(8,128)S(1)}, f32[128,512]{1,0:T(8,128)}, u32[]{:S(2)}) copy-start(f32[128,512]{1,0:T(8,128)} %get-tuple-element.245) | copy-start | bytes 786436
  631.2 8.5 copy-start.39
  632.3 5.5 copy-start.5
  632.3 5.5 copy-start.25
  636.5 114.5 %copy-start.37 = (f32[2048]{0:T(1024)}, f32[2048]{0:T(1024)S(1)}, u32[]{:S(2)}) copy-start(f32[2048]{0:T(1024)S(1)} %get-tuple-element.212) | copy-start | bytes 24580
  636.5 2.3 copy-start.19
  636.5 2.3 copy-start.29
  640.3 113.9 %copy-start.17 = (bf16[128,2048]{1,0:T(8,128)(2,1)S(1)}, bf16[128,2048]{1,0:T(8,128)(2,1)}, u32[]{:S(2)}) copy-start(bf16[128,2048]{1,0:T(8,128)(2,1)} %get-tuple-element.141.refs_6_) | copy-start | bytes 1572868
  751.1 5.1 copy-start.8
  751.1 5.1 copy-start.18
  754.2 3.4 copy-start.36
  754.2 3.4 copy-start.38
  754.2 3.4 copy-start.40
  756.9 39.8 %collective-permute-start = (bf16[64,576]{1,0:T(8,128)(2,1)S(1)}, bf16[64,576]{1,0:T(8,128)(2,1)S(1)}, u32[]{:S(2)}, u32[]{:S(2)}) collective-permute-start(bf16[64,576]{1,0:T(8,128)(2,1)S(1)} %constant_dynamic-slice_fusion), channel_id=1, source_target_pairs={{0,1},{1,0},{2,3},{3,2},{4,5},{5,4},{6,7},{7,6},{8,9},{9,8},{10,11... | collective-permute-start | bytes 221192 | tf_op jit(solution)/shard_map/ppermute | solution.py:1279
  781.8 5.9 copy-start.27
  781.8 5.9 copy-start.32
  781.8 6.6 copy-start.6
  788.4 5.7 copy-start.1
  788.4 5.7 copy-start.22
  788.4 5.7 copy-start.23
  788.4 5.7 copy-start.35
  788.4 5.7 copy-start.42
  788.4 5.7 copy-start.44
  788.4 5.7 copy-start.46
  788.4 5.7 copy-start.47
  891.6 12.9 %slice-start = ((s8[5767168]{0:T(1024)(128)(4,1)}), s8[1572864]{0:T(1024)(128)(4,1)S(1)}, s32[]{:S(2)}) async-start(s8[5767168]{0:T(1024)(128)(4,1)} %bitcast.90), calls=%async_computation.1 | async-start | bytes 3145728
  897.7 6.8 slice-start.1
  897.7 6.8 copy-start.7
  904.5 3.1 copy-start.28
Sparse Core Ops, SparseCore 0:
  71.0 81.2 all-gather.1

commit v5 on v4

--- a/solution.py
+++ b/solution.py
@@ -355,8 +355,11 @@
     def across(t, d):
         return remote(stage.at[t, :, spans[d]], sibbuf.at[t, :, spans[d]], fsend.at[t, d], frecv.at[t, d], sibling)
 
-    def onward(t, d):
-        return remote(sbuf.at[t, :, spans[d]], rbuf.at[t, :, spans[d]], send.at[t, d], recv.at[t, d], targets[d])
+    half = height // 2
+
+    def onward(t, d, k):
+        at = (t, pl.ds(k * half, half), spans[d])
+        return remote(sbuf.at[at], rbuf.at[at], send.at[t, d, k], recv.at[t, d, k], targets[d])
 
     def give(t, d):
         stage[t, :, spans[d]] = part(t, d, 1 - core).astype(BF)
@@ -365,20 +368,25 @@
     for d in range(2):
         give(0, d)
     for t in range(n):
+        values = []
         for d in range(2):
             if t < n - 1:
                 give(t + 1, d)
-            value = part(t, d, core)
-            across(t, d).wait_recv()
-            value = value + sibbuf[t, :, spans[d]].astype(F32)
-            if t > 0:
-                onward(t - 1, d).wait_recv()
-                value = value + rbuf[t - 1, :, spans[d]].astype(F32)
-            if t < n - 1:
-                sbuf[t, :, spans[d]] = value.astype(BF)
-                onward(t, d).start()
-            else:
-                o_ref[:, spans[d]] = value
+            values.append(part(t, d, core))
+        for k in range(2):
+            for d in range(2):
+                if k == 0:
+                    across(t, d).wait_recv()
+                rows = slice(k * half, (k + 1) * half)
+                value = values[d][rows] + sibbuf[t, rows, spans[d]].astype(F32)
+                if t > 0:
+                    onward(t - 1, d, k).wait_recv()
+                    value = value + rbuf[t - 1, rows, spans[d]].astype(F32)
+                if t < n - 1:
+                    sbuf[t, rows, spans[d]] = value.astype(BF)
+                    onward(t, d, k).start()
+                else:
+                    o_ref[rows, spans[d]] = value
         if beside and t == 0:
             for load in loads:
                 load.wait()
@@ -394,7 +402,8 @@
         for d in range(2):
             across(t, d).wait_send()
             if t < n - 1:
-                onward(t, d).wait_send()
+                for k in range(2):
+                    onward(t, d, k).wait_send()
     for copy in swapped:
         copy.wait()
 
@@ -423,7 +432,7 @@
             pltpu.VMEM((n - 1, rows, columns), BF),
             pltpu.VMEM((n - 1, rows, columns), BF),
         ]
-        + [pltpu.SemaphoreType.DMA((n - 1, 2))] * 2
+        + [pltpu.SemaphoreType.DMA((n - 1, 2, 2))] * 2
         + [pltpu.SemaphoreType.DMA((n, 2))] * 2
         + [pltpu.SemaphoreType.DMA((max(1, len(swaps)), 2))]
         + held,
@@ -765,7 +774,7 @@
     wg, wu, wd, sems, _, *buffers = refs[3 * count + 11 :]
     copies = [fill(p, w, sems.at[i]) for i, (p, w) in enumerate(((wg_parts, wg), (wu_parts, wu), (wd_parts, wd)))]
     start_first(copies)
-    finish = scatter_in_grid(pl.program_id(0), n, cut, part_ref, y_ref, buffers)
+    middle, finish = scatter_in_grid(pl.program_id(0), n, cut, part_ref, y_ref, buffers)
     blocks, rows = slot_ref.shape[0], slot_ref.shape[2]
     wait_first(copies)
     for low, high in hidden_spans(wg.shape[1]):
@@ -774,6 +783,7 @@
         sig = jax.nn.sigmoid(ge)
         dge_ref[:, low:high] = (dhe * ue * sig * (1.0 + ge * (1.0 - sig))).astype(BF)
         due_ref[:, low:high] = (dhe * ge * sig).astype(BF)
+    middle()
     dxe = (mm_nt(dge_ref[...], wg[...]) + mm_nt(due_ref[...], wu[...])).astype(BF)
     for b in range(blocks):
         pick, _ = picks(slot_ref, share_ref, b, most)
@@ -893,10 +903,11 @@
         source = part_ref.at[block(step, d, 1 - core), :, spans[d]]
         return remote(source, sibbuf.at[step, :, spans[d]], fsend.at[step, d], frecv.at[step, d], sibling)
 
-    def onward(step, d):
-        return remote(
-            sbuf.at[step, :, spans[d]], rbuf.at[step, :, spans[d]], send.at[step, d], recv.at[step, d], targets[d]
-        )
+    height = o_ref.shape[0] // 2
+
+    def onward(step, d, k):
+        at = (step, pl.ds(k * height, height), spans[d])
+        return remote(sbuf.at[at], rbuf.at[at], send.at[step, d, k], recv.at[step, d, k], targets[d])
 
     @pl.when(t == 0)
     def _():
@@ -910,27 +921,30 @@
         for d in range(2):
             across(t + 2, d).start()
 
-    for d in range(2):
-        across(t, d).wait_recv()
-
-        def both():
-            return part_ref[block(t, d, core), :, spans[d]].astype(F32) + sibbuf[t, :, spans[d]].astype(F32)
-
-        @pl.when(t == 0)
-        def _():
-            sbuf[0, :, spans[d]] = both().astype(BF)
-            onward(0, d).start()
-
-        @pl.when((t > 0) & (t < n - 1))
-        def _():
-            onward(t - 1, d).wait_recv()
-            sbuf[t, :, spans[d]] = (both() + rbuf[t - 1, :, spans[d]].astype(F32)).astype(BF)
-            onward(t, d).start()
-
-        @pl.when(t == n - 1)
-        def _():
-            onward(n - 2, d).wait_recv()
-            o_ref[:, spans[d]] = both() + rbuf[n - 2, :, spans[d]].astype(F32)
+    def advance(k):
+        rows = pl.ds(k * height, height)
+        for d in range(2):
+            if k == 0:
+                across(t, d).wait_recv()
+
+            def both():
+                return part_ref[block(t, d, core), rows, spans[d]].astype(F32) + sibbuf[t, rows, spans[d]].astype(F32)
+
+            @pl.when(t == 0)
+            def _():
+                sbuf[0, rows, spans[d]] = both().astype(BF)
+                onward(0, d, k).start()
+
+            @pl.when((t > 0) & (t < n - 1))
+            def _():
+                onward(t - 1, d, k).wait_recv()
+                sbuf[t, rows, spans[d]] = (both() + rbuf[t - 1, rows, spans[d]].astype(F32)).astype(BF)
+                onward(t, d, k).start()
+
+            @pl.when(t == n - 1)
+            def _():
+                onward(n - 2, d, k).wait_recv()
+                o_ref[rows, spans[d]] = both() + rbuf[n - 2, rows, spans[d]].astype(F32)
 
     def finish():
         @pl.when(t == n - 1)
@@ -939,15 +953,17 @@
                 for d in range(2):
                     across(step, d).wait_send()
                     if step < n - 1:
-                        onward(step, d).wait_send()
-
-    return finish
+                        for k in range(2):
+                            onward(step, d, k).wait_send()
+
+    advance(0)
+    return lambda: advance(1), finish
 
 
 def scatter_buffers(n, rows, columns):
     return (
         [pltpu.VMEM((n, rows, columns), BF), pltpu.VMEM((n - 1, rows, columns), BF), pltpu.VMEM((n - 1, rows, columns), BF)]
-        + [pltpu.SemaphoreType.DMA((n - 1, 2))] * 2
+        + [pltpu.SemaphoreType.DMA((n - 1, 2, 2))] * 2
         + [pltpu.SemaphoreType.DMA((n, 2))] * 2
     )
 
@@ -955,11 +971,12 @@
 def weight_grads_kernel(n, cut, parts, *refs):
     xe_ref, dge_ref, due_ref, he_ref, dye_ref, act_ref, dsgu_ref, sh_ref, g_ref, part_ref = refs[:10]
     o_ref, gate_ref, up_ref, down_ref, sgu_ref, sdown_ref = refs[10:16]
-    finish = scatter_in_grid(pl.program_id(0), n, cut, part_ref, o_ref, refs[16:])
+    middle, finish = scatter_in_grid(pl.program_id(0), n, cut, part_ref, o_ref, refs[16:])
     gate_ref[...] = mm_tn(xe_ref[...], dge_ref[...]).astype(BF)
+    sgu_ref[...] = mm_tn(act_ref[...], dsgu_ref[...]).astype(BF)
+    middle()
     up_ref[...] = mm_tn(xe_ref[...], due_ref[...]).astype(BF)
     down_ref[...] = mm_tn(he_ref[...], dye_ref[...]).astype(BF)
-    sgu_ref[...] = mm_tn(act_ref[...], dsgu_ref[...]).astype(BF)
     sdown = mm_tn(sh_ref[...], g_ref[...]).astype(BF)
     share = sdown.shape[0] // parts
     room = sdown_ref.shape[0] // parts

time: 932 us -> 923 us (level)
  no operation moved by 1% of the time
where the time goes in v5:
time: 923 us; the launch traced here: 918 us
  Pallas kernels  811 us (88%)
  other arithmetic  59 us (6%)
  local copies, waits for them, and re-layouts  25 us (3%)
  between operations  15.3 us (2%)
    pallas_call x5, Pallas kernels, ring_gather_many(): pl.pallas_call(functools.partial(gather_kernel, n, cuts, actives or [None...  360 us
    pallas_call x3, Pallas kernels, expert_call(): pl.pallas_call(functools.partial(kernel, count, most, len(swaps)), grid=(...  160 us
    pallas_call x2, Pallas kernels, ring_scatter(): pl.pallas_call(functools.partial(scatter_kernel, n, cut, len(swaps), len(...  137 us
    pallas_call x1, Pallas kernels, weight_grads(): pl.pallas_call(functools.partial(weight_grads_kernel, n, cut, parts), gri...  61.4 us
    pallas_call x1, Pallas kernels, front(): pl.pallas_call(functools.partial(front_kernel, count, len(swaps), chunks)...  34.2 us
    pallas_call x2, Pallas kernels, widen(): pl.pallas_call(kernel, grid=(steps,), out_shape=[jax.ShapeDtypeStruct((ro...  21.7 us
    pallas_call x1, Pallas kernels, attend_back(): pl.pallas_call(attend_back_kernel, out_shape=[jax.ShapeDtypeStruct((lengt...  18.7 us
  transfers between devices with their start and end apart: 2, of which 0 were waited for; matrix products, arithmetic and copies ran while one was open for 4% of the time, Pallas kernels for 21%

profile of v5, /device:TPU:9, one launch (start us, length us, event | category | flops | bytes accessed | tf_op | source)
XLA Modules:
  0.0 917.7 jit_solution(15251468369488832793)
XLA Ops:
  7.2 0.7 copy.73
  7.9 0.7 copy.74
  9.3 0.7 convert.30
  10.0 0.7 convert.29
  10.7 2.7 copy.51.refs_4_.refs_2_
  13.4 2.4 dynamic-slice_convert_fusion.2.refs_3_.refs_0_
  16.4 1.6 dynamic-slice_convert_fusion.8.refs_5_.refs_4_
  18.0 2.1 dynamic-slice_convert_fusion.1.refs_6_
  20.7 50.1 %ring_gather.5 = (bf16[16,128,2048]{2,1,0:T(8,128)(2,1)}, f32[16,16,128]{2,1,0:T(8,128)}, bf16[32,128]{1,0:T(8,128)(2,1)}, bf16[1024,192]{1,0:T(8,128)(2,1)}, bf...) custom-call(bf16[128,2048]{1,0:T(8,128)(2,1)} %bitcast.98, ...), custom_call_target="tpu_custom_call" | custom-call | bytes 1048576 | tf_op jit(solution)/shard_map/ring_gather/pallas_call | solution.py:295
  70.9 0.7 broadcast_select_fusion.8
  72.8 1.3 copy.52.refs_11_.refs_9_
  74.2 1.3 broadcast_select_fusion.4.refs_6_
  75.5 1.0 copy.53.refs_1_
  76.5 0.9 broadcast_compare_fusion
  77.7 1.2 dynamic-slice_convert_fusion.3
  78.9 0.8 pad.13.refs_14_
  79.7 2.5 dynamic-slice_convert_fusion.5
  82.3 1.4 pad_maximum_fusion.1.refs_13_
  83.7 34.2 %front.1 = (bf16[2048,2048]{1,0:T(8,128)(2,1)}, bf16[2048,512]{1,0:T(8,128)(2,1)}, bf16[2048,192]{1,0:T(8,128)(2,1)}, bf16[2048,192]{1,0:T(8,128)(2,1)}, bf16[20...) custom-call(bf16[1024,192]{1,0:T(8,128)(2,1)} %dynamic-slice_convert, ...), custom_call_target="tpu_custom_call" | custom-call | bytes 1048576 | tf_op jit(solution)/shard_map/front/pallas_call | solution.py:601
  118.0 67.5 %ring_scatter.2 = (f32[128,2048]{1,0:T(8,128)}, bf16[1024,1408]{1,0:T(8,128)(2,1)}) custom-call(bf16[2048,128]{1,0:T(8,128)(2,1)} %get-tuple-element.95.refs_0_.refs_4_, bf16[2048,128]{1,0:T(8,128)(2,1)} %copy.53.refs_1_, bf16[1024,1408]{1,0:T(8,128)(2,1)} %get-tuple-element.97.refs_2_.refs_0_), custom_call_target="tpu_custom_call" | custom-call | bytes 1048576 | tf_op jit(solution)/shard_map/ring_scatter/pallas_call | solution.py:424
  185.5 1.5 multiply_reduce_fusion.2
  187.1 0.9 multiply_convert_fusion.refs_0_
  188.0 64.7 %ring_gather.6 = (bf16[16,128,2048]{2,1,0:T(8,128)(2,1)}, bf16[1024,1408]{1,0:T(8,128)(2,1)}) custom-call(bf16[128,2048]{1,0:T(8,128)(2,1)} %multiply_convert_fusion.refs_0_, bf16[1024,1408]{1,0:T(8,128)(2,1)} %get-tuple-element.100.refs_1_.refs_2_), custom_call_target="tpu_custom_call" | custom-call | bytes 1048576 | tf_op jit(solution)/shard_map/ring_gather/pallas_call | solution.py:295
  252.7 1.6 broadcast_select_fusion.1
  254.3 1.5 multiply_reduce_fusion.5
  256.5 1.2 broadcast_select_fusion.6
  257.8 0.9 pad_maximum_fusion.2.refs_8_
  258.7 2.4 constant_dynamic-slice_fusion.2
  261.8 1.3 pad_maximum_fusion.refs_7_
  263.1 70.5 %experts_in.1 = (bf16[1536,2048]{1,0:T(8,128)(2,1)}, f32[1536,1408]{1,0:T(8,128)}, f32[1536,1408]{1,0:T(8,128)}, bf16[1536,1408]{1,0:T(8,128)(2,1)}, bf16[2048,1...) custom-call(bf16[1024,1408]{1,0:T(8,128)(2,1)} %get-tuple-element.97, ...), custom_call_target="tpu_custom_call" | custom-call | bytes 1048576 | tf_op jit(solution)/shard_map/experts_in/pallas_call | solution.py:812
  333.6 19.0 %experts_out.1 = bf16[2048,2048]{1,0:T(8,128)(2,1)} custom-call(bf16[704,2048]{1,0:T(8,128)(2,1)} %get-tuple-element.102.refs_10_.refs_0_.refs_4_, bf16[704,2048]{1,0:T(8,128)(2,1)} %get-tuple-element.108.refs_1_.refs_5_, bf16[1536,1408]{1,0:T(8,128)(2,1)} %get-tuple-element.110.refs_2_.refs_3_, ...), custom_call_target="tpu_custom_call" | custom-call | bytes 1048576 | tf_op jit(solution)/shard_map/experts_out/pallas_call | solution.py:812
  352.6 70.2 %experts_back.1 = (bf16[2048,2048]{1,0:T(8,128)(2,1)}, bf16[1536,1408]{1,0:T(8,128)(2,1)}, bf16[1536,1408]{1,0:T(8,128)(2,1)}, f32[128,2048]{1,0:T(8,128)}) custom-call(bf16[1024,1408]{1,0:T(8,128)(2,1)} %get-tuple-element.97.refs_2_.refs_0_, bf16[1024,1408]{1,0:T(8,128)(2,1)} %get-tuple-element.99.refs_1_, ...), custom_call_target="tpu_custom_call" | custom-call | bytes 1048576 | tf_op jit(solution)/shard_map/experts_back/pallas_call | solution.py:812
  422.8 61.4 %weight_grads.1 = (f32[128,2048]{1,0:T(8,128)}, bf16[2048,1408]{1,0:T(8,128)(2,1)}, bf16[2048,1408]{1,0:T(8,128)(2,1)}, bf16[1408,2048]{1,0:T(8,128)(2,1)}, bf16...) custom-call(bf16[1536,2048]{1,0:T(8,128)(2,1)} %get-tuple-element.116.refs_0_, ...), custom_call_target="tpu_custom_call" | custom-call | bytes 1048576 | tf_op jit(solution)/shard_map/weight_grads/pallas_call | solution.py:1008
  484.2 1.5 multiply_reduce_fusion
  485.8 2.4 fusion.42.refs_0_
  488.2 46.1 %ring_gather.7 = (bf16[16,128,2048]{2,1,0:T(8,128)(2,1)}, bf16[1024,352]{1,0:T(8,128)(2,1)}, bf16[96,2048]{1,0:T(8,128)(2,1)}) custom-call(bf16[128,2048]{1,0:T(8,128)(2,1)} %fusion.42.refs_0_, bf16[2048,352]{1,0:T(8,128)(2,1)} %get-tuple-element.127.refs_1_, bf16[192,2048]{1,0:T(8,128)(2,1)} %get-tuple-element.128.refs_2_), custom_call_target="tpu_custom_call" | custom-call | bytes 1048576 | tf_op jit(solution)/shard_map/ring_gather/pallas_call | solution.py:295
  534.3 18.7 %attend_back.1 = (bf16[2048,512]{1,0:T(8,128)(2,1)}, bf16[128,2048]{1,0:T(8,128)(2,1)}) custom-call(bf16[2048,192]{1,0:T(8,128)(2,1)} %get-tuple-element.123.refs_0_, bf16[2048,192]{1,0:T(8,128)(2,1)} %get-tuple-element.124.refs_1_, bf16[2048,128]{1,0:T(8,128)(2,1)} %get-tuple-element.125.refs_2_, f32[2048,1]{1,0:T(8,128)} %get-tuple-element.126.refs_3_, ...), custom_call_target="tpu_custom_call" | custom-call | bytes 1048576 | tf_op jit(solution)/shard_map/attend_back/pallas_call | solution.py:650
  553.0 69.3 %ring_scatter.3 = (f32[128,2688]{1,0:T(8,128)}, bf16[704,2048]{1,0:T(8,128)(2,1)}, bf16[2048,128]{1,0:T(8,128)(2,1)}, bf16[2048,64]{1,0:T(8,128)(2,1)}, bf16[512,256]{1,0:T(8,128)(2,1)}) custom-call(bf16[2048,512]{1,0:T(8,128)(2,1)} %get-tuple-element.130.refs_0_, bf16[2688,512]{1,0:T(8,128)(2,1)} %get-tuple-element.131.refs_1_, ...), custom_call_target="tpu_custom_call" | custom-call | bytes 1048576 | tf_op jit(solution)/shard_map/ring_scatter/pallas_call | solution.py:424
  622.3 0.8 slice.57
  623.2 1.1 multiply_reduce_fusion.3
  624.3 1.1 subtract_convert_fusion
  625.4 4.2 fusion.22
  630.9 1.1 add_convert_fusion.refs_0_
  631.9 0.8 add_convert_fusion.2.refs_2_
  633.4 108.6 %ring_gather.8 = (bf16[16,1024,352]{2,1,0:T(8,128)(2,1)}, bf16[16,128,576]{2,1,0:T(8,128)(2,1)}, bf16[16,96,2048]{2,1,0:T(8,128)(2,1)}, bf16[1024,128]{1,0:T(8,1...) custom-call(bf16[1024,352]{1,0:T(8,128)(2,1)} %add_convert_fusion.re, ...), custom_call_target="tpu_custom_call" | custom-call | bytes 1048576 | tf_op jit(solution)/shard_map/ring_gather/pallas_call | solution.py:295
  742.1 2.0 add_convert_fusion.4.refs_0_
  744.0 1.1 add_convert_fusion.3
  745.2 2.0 add.194.refs_3_
  747.2 0.7 convolution_convert_fusion
  747.9 0.9 collective-permute-start
  749.5 15.6 %wide_shared.1 = (f32[1024,2816]{1,0:T(8,128)}, f32[1024,2816]{1,0:T(8,128)}) custom-call(bf16[16,1024,352]{2,1,0:T(8,128)(2,1)} %get-tuple-element.156.i_ref), custom_call_target="tpu_custom_call" | custom-call | bytes 1048576 | tf_op jit(solution)/shard_map/wide_shared/pallas_call | solution.py:1042
  765.1 7.9 trim.1
  773.0 5.9 add_bitcast_fusion.2
  779.0 0.7 add_convert_fusion.5.refs_2_
  779.7 5.6 add_bitcast_fusion
  785.4 1.8 fusion.18
  787.2 0.8 pad_maximum_fusion.4.refs_1_
  788.7 90.6 %ring_gather.9 = (bf16[16,1024,128]{2,1,0:T(8,128)(2,1)}, bf16[16,512,128]{2,1,0:T(8,128)(2,1)}, bf16[16,256,256]{2,1,0:T(8,128)(2,1)}, bf16[16,128,2048]{2,1,0:...) custom-call(bf16[1024,128]{1,0:T(8,128)(2,1)} %add_convert_fusion.4.refs_0_, ...), custom_call_target="tpu_custom_call" | custom-call | bytes 1048576 | tf_op jit(solution)/shard_map/ring_gather/pallas_call | solution.py:295
  879.2 1.5 bitcast_convert_fusion
  880.7 2.0 copy.59
  882.7 6.1 wide_kv.1
  888.8 6.8 dynamic-slice_convert_fusion
  895.7 3.1 add_bitcast_fusion.1
  900.0 10.3 %wide_query.1 = f32[1024,3072]{1,0:T(8,128)} custom-call(bf16[16,1024,128]{2,1,0:T(8,128)(2,1)} %get-tuple-element.151.n_ref, bf16[16,512,128]{2,1,0:T(8,128)(2,1)} %get-tuple-element.152.r_ref), custom_call_target="tpu_custom_call" | custom-call | bytes 1048576 | tf_op jit(solution)/shard_map/wide_query/pallas_call | solution.py:850
  (138 shorter events, 9.4 us)
Async XLA Ops:
  7.2 255.9 %all-gather.2.cloned.1.call-start = ((), (), s32[]{:S(2)}) async-start(), calls=%async_computation | async-start | bytes 8912896 | tf_op jit(solution)/shard_map/all_gather | solution.py:1130
  20.7 52.1 %copy-start.33 = (s32[1,2048]{1,0:T(1,128)S(1)}, s32[1,2048]{1,0:T(1,128)}, u32[]{:S(2)}) copy-start(s32[1,2048]{1,0:T(1,128)} %refs_10_.2) | copy-start | bytes 24580
  75.5 8.1 copy-start.4
  77.4 178.5 %copy-start.31 = (f32[16,1,128]{2,1,0:T(1,128)}, f32[16,1,128]{2,1,0:T(1,128)S(1)}, u32[]{:S(2)}) copy-start(f32[16,1,128]{2,1,0:T(1,128)S(1)} %get-tuple-element.215.refs_6_.refs_4_.refs_8_) | copy-start | bytes 24580
  82.2 1.4 copy-start.9
  82.3 1.4 copy-start.11
  82.3 1.4 copy-start.13
  82.3 1.4 copy-start.15
  117.9 67.5 %copy-start.2 = (bf16[1,128,2048]{2,1,0:T(8,128)(2,1)S(1)}, bf16[1,128,2048]{2,1,0:T(8,128)(2,1)}, u32[]{:S(2)}) copy-start(bf16[1,128,2048]{2,1,0:T(8,128)(2,1)} %param.20) | copy-start | bytes 1572868
  187.0 65.7 %copy-start = (bf16[1024,576]{1,0:T(8,128)(2,1)S(1)}, bf16[1024,576]{1,0:T(8,128)(2,1)}, u32[]{:S(2)}) copy-start(bf16[1024,576]{1,0:T(8,128)(2,1)} %copy.51.refs_4_.refs_2_) | copy-start | bytes 3538948
  187.0 298.7 %copy-start.41 = (f32[128]{0:T(128)}, f32[128]{0:T(128)S(1)}, u32[]{:S(2)}) copy-start(f32[128]{0:T(128)S(1)} %add_rsqrt_fusion.2) | copy-start | bytes 1540
  187.1 438.3 %copy-start.34 = (f32[2048]{0:T(1024)}, f32[2048]{0:T(1024)S(1)}, u32[]{:S(2)}) copy-start(f32[2048]{0:T(1024)S(1)} %get-tuple-element.247) | copy-start | bytes 24580
  252.7 372.7 %copy-start.45 = (f32[128]{0:T(128)}, f32[128]{0:T(128)S(1)}, u32[]{:S(2)}) copy-start(f32[128]{0:T(128)S(1)} %add_rsqrt_fusion.1) | copy-start | bytes 1540
  254.3 3.5 copy-start.20
  254.3 3.5 copy-start.21
  254.3 2.2 copy-start.30
  255.9 5.2 copy-start.10
  255.9 5.2 copy-start.12
  255.9 5.2 copy-start.14
  255.9 5.2 copy-start.16
  255.9 5.2 copy-start.26
  422.8 63.0 %copy-start.3 = (bf16[1,128,2048]{2,1,0:T(8,128)(2,1)S(1)}, bf16[1,128,2048]{2,1,0:T(8,128)(2,1)}, u32[]{:S(2)}) copy-start(bf16[1,128,2048]{2,1,0:T(8,128)(2,1)} %param.24) | copy-start | bytes 1572868
  485.8 48.5 %copy-start.43 = (f32[128]{0:T(128)}, f32[128]{0:T(128)S(1)}, u32[]{:S(2)}) copy-start(f32[128]{0:T(128)S(1)} %broadcast_multiply_fusion.2) | copy-start | bytes 1540
  553.0 70.2 %copy-start.24 = (f32[128,512]{1,0:T(8,128)S(1)}, f32[128,512]{1,0:T(8,128)}, u32[]{:S(2)}) copy-start(f32[128,512]{1,0:T(8,128)} %get-tuple-element.245) | copy-start | bytes 786436
  624.3 8.5 copy-start.39
  625.4 5.5 copy-start.5
  625.4 5.5 copy-start.25
  629.6 112.4 %copy-start.37 = (f32[2048]{0:T(1024)}, f32[2048]{0:T(1024)S(1)}, u32[]{:S(2)}) copy-start(f32[2048]{0:T(1024)S(1)} %get-tuple-element.212) | copy-start | bytes 24580
  629.7 2.3 copy-start.19
  629.7 2.3 copy-start.29
  633.4 111.8 %copy-start.17 = (bf16[128,2048]{1,0:T(8,128)(2,1)S(1)}, bf16[128,2048]{1,0:T(8,128)(2,1)}, u32[]{:S(2)}) copy-start(bf16[128,2048]{1,0:T(8,128)(2,1)} %get-tuple-element.141.refs_6_) | copy-start | bytes 1572868
  742.0 5.1 copy-start.8
  742.0 5.1 copy-start.18
  745.2 3.7 copy-start.36
  745.2 3.7 copy-start.38
  745.2 3.7 copy-start.40
  747.9 40.1 %collective-permute-start = (bf16[64,576]{1,0:T(8,128)(2,1)S(1)}, bf16[64,576]{1,0:T(8,128)(2,1)S(1)}, u32[]{:S(2)}, u32[]{:S(2)}) collective-permute-start(bf16[64,576]{1,0:T(8,128)(2,1)S(1)} %constant_dynamic-slice_fusion), channel_id=1, source_target_pairs={{0,1},{1,0},{2,3},{3,2},{4,5},{5,4},{6,7},{7,6},{8,9},{9,8},{10,11... | collective-permute-start | bytes 221192 | tf_op jit(solution)/shard_map/ppermute | solution.py:1296
  773.0 6.0 copy-start.27
  773.0 6.0 copy-start.32
  773.0 6.6 copy-start.6
  779.7 5.7 copy-start.1
  779.7 5.7 copy-start.22
  779.7 5.7 copy-start.23
  779.7 5.7 copy-start.35
  779.7 5.7 copy-start.42
  779.7 5.7 copy-start.44
  779.7 5.7 copy-start.46
  779.7 5.7 copy-start.47
  882.7 12.9 %slice-start = ((s8[5767168]{0:T(1024)(128)(4,1)}), s8[1572864]{0:T(1024)(128)(4,1)S(1)}, s32[]{:S(2)}) async-start(s8[5767168]{0:T(1024)(128)(4,1)} %bitcast.90), calls=%async_computation.1 | async-start | bytes 3145728
  888.8 6.8 slice-start.1
  888.8 6.8 copy-start.7
  895.7 3.1 copy-start.28
Sparse Core Ops, SparseCore 0:
  71.0 86.8 all-gather.1

commit v6 on v5

--- a/solution.py
+++ b/solution.py
@@ -775,6 +775,7 @@
     copies = [fill(p, w, sems.at[i]) for i, (p, w) in enumerate(((wg_parts, wg), (wu_parts, wu), (wd_parts, wd)))]
     start_first(copies)
     middle, finish = scatter_in_grid(pl.program_id(0), n, cut, part_ref, y_ref, buffers)
+    middle()
     blocks, rows = slot_ref.shape[0], slot_ref.shape[2]
     wait_first(copies)
     for low, high in hidden_spans(wg.shape[1]):
@@ -783,7 +784,6 @@
         sig = jax.nn.sigmoid(ge)
         dge_ref[:, low:high] = (dhe * ue * sig * (1.0 + ge * (1.0 - sig))).astype(BF)
         due_ref[:, low:high] = (dhe * ge * sig).astype(BF)
-    middle()
     dxe = (mm_nt(dge_ref[...], wg[...]) + mm_nt(due_ref[...], wu[...])).astype(BF)
     for b in range(blocks):
         pick, _ = picks(slot_ref, share_ref, b, most)

time: 923 us -> 920 us (level)
  no operation moved by 1% of the time
where the time goes in v6:
time: 920 us; the launch traced here: 915 us
  Pallas kernels  808 us (88%)
  other arithmetic  59 us (6%)
  local copies, waits for them, and re-layouts  25 us (3%)
  between operations  15.3 us (2%)
    pallas_call x5, Pallas kernels, ring_gather_many(): pl.pallas_call(functools.partial(gather_kernel, n, cuts, actives or [None...  360 us
    pallas_call x3, Pallas kernels, expert_call(): pl.pallas_call(functools.partial(kernel, count, most, len(swaps)), grid=(...  157 us
    pallas_call x2, Pallas kernels, ring_scatter(): pl.pallas_call(functools.partial(scatter_kernel, n, cut, len(swaps), len(...  137 us
    pallas_call x1, Pallas kernels, weight_grads(): pl.pallas_call(functools.partial(weight_grads_kernel, n, cut, parts), gri...  61.5 us
    pallas_call x1, Pallas kernels, front(): pl.pallas_call(functools.partial(front_kernel, count, len(swaps), chunks)...  34.2 us
    pallas_call x2, Pallas kernels, widen(): pl.pallas_call(kernel, grid=(steps,), out_shape=[jax.ShapeDtypeStruct((ro...  21.7 us
    pallas_call x1, Pallas kernels, attend_back(): pl.pallas_call(attend_back_kernel, out_shape=[jax.ShapeDtypeStruct((lengt...  18.7 us
  transfers between devices with their start and end apart: 2, of which 0 were waited for; matrix products, arithmetic and copies ran while one was open for 4% of the time, Pallas kernels for 21%

profile of v6, /device:TPU:9, one launch (start us, length us, event | category | flops | bytes accessed | tf_op | source)
XLA Modules:
  0.0 914.6 jit_solution(11039765441737931038)
XLA Ops:
  7.2 0.7 copy.73
  7.9 0.7 copy.74
  9.3 0.7 convert.30
  10.0 0.7 convert.29
  10.7 2.7 copy.51.refs_4_.refs_2_
  13.4 2.4 dynamic-slice_convert_fusion.2.refs_3_.refs_0_
  16.4 1.6 dynamic-slice_convert_fusion.8.refs_5_.refs_4_
  18.0 2.1 dynamic-slice_convert_fusion.1.refs_6_
  20.7 50.1 %ring_gather.5 = (bf16[16,128,2048]{2,1,0:T(8,128)(2,1)}, f32[16,16,128]{2,1,0:T(8,128)}, bf16[32,128]{1,0:T(8,128)(2,1)}, bf16[1024,192]{1,0:T(8,128)(2,1)}, bf...) custom-call(bf16[128,2048]{1,0:T(8,128)(2,1)} %bitcast.98, ...), custom_call_target="tpu_custom_call" | custom-call | bytes 1048576 | tf_op jit(solution)/shard_map/ring_gather/pallas_call | solution.py:295
  70.9 0.7 broadcast_select_fusion.8
  72.8 1.3 copy.52.refs_11_.refs_9_
  74.2 1.3 broadcast_select_fusion.4.refs_6_
  75.5 1.0 copy.53.refs_1_
  76.5 0.9 broadcast_compare_fusion
  77.7 1.2 dynamic-slice_convert_fusion.3
  78.9 0.8 pad.13.refs_14_
  79.7 2.5 dynamic-slice_convert_fusion.5
  82.3 1.4 pad_maximum_fusion.1.refs_13_
  83.7 34.2 %front.1 = (bf16[2048,2048]{1,0:T(8,128)(2,1)}, bf16[2048,512]{1,0:T(8,128)(2,1)}, bf16[2048,192]{1,0:T(8,128)(2,1)}, bf16[2048,192]{1,0:T(8,128)(2,1)}, bf16[20...) custom-call(bf16[1024,192]{1,0:T(8,128)(2,1)} %dynamic-slice_convert, ...), custom_call_target="tpu_custom_call" | custom-call | bytes 1048576 | tf_op jit(solution)/shard_map/front/pallas_call | solution.py:601
  118.0 67.5 %ring_scatter.2 = (f32[128,2048]{1,0:T(8,128)}, bf16[1024,1408]{1,0:T(8,128)(2,1)}) custom-call(bf16[2048,128]{1,0:T(8,128)(2,1)} %get-tuple-element.95.refs_0_.refs_4_, bf16[2048,128]{1,0:T(8,128)(2,1)} %copy.53.refs_1_, bf16[1024,1408]{1,0:T(8,128)(2,1)} %get-tuple-element.97.refs_2_.refs_0_), custom_call_target="tpu_custom_call" | custom-call | bytes 1048576 | tf_op jit(solution)/shard_map/ring_scatter/pallas_call | solution.py:424
  185.5 1.5 multiply_reduce_fusion.2
  187.1 0.9 multiply_convert_fusion.refs_0_
  188.0 64.7 %ring_gather.6 = (bf16[16,128,2048]{2,1,0:T(8,128)(2,1)}, bf16[1024,1408]{1,0:T(8,128)(2,1)}) custom-call(bf16[128,2048]{1,0:T(8,128)(2,1)} %multiply_convert_fusion.refs_0_, bf16[1024,1408]{1,0:T(8,128)(2,1)} %get-tuple-element.100.refs_1_.refs_2_), custom_call_target="tpu_custom_call" | custom-call | bytes 1048576 | tf_op jit(solution)/shard_map/ring_gather/pallas_call | solution.py:295
  252.7 1.6 broadcast_select_fusion.1
  254.3 1.5 multiply_reduce_fusion.5
  256.5 1.2 broadcast_select_fusion.6
  257.8 0.9 pad_maximum_fusion.2.refs_8_
  258.7 2.4 constant_dynamic-slice_fusion.2
  261.8 1.3 pad_maximum_fusion.refs_7_
  263.1 70.5 %experts_in.1 = (bf16[1536,2048]{1,0:T(8,128)(2,1)}, f32[1536,1408]{1,0:T(8,128)}, f32[1536,1408]{1,0:T(8,128)}, bf16[1536,1408]{1,0:T(8,128)(2,1)}, bf16[2048,1...) custom-call(bf16[1024,1408]{1,0:T(8,128)(2,1)} %get-tuple-element.97, ...), custom_call_target="tpu_custom_call" | custom-call | bytes 1048576 | tf_op jit(solution)/shard_map/experts_in/pallas_call | solution.py:812
  333.6 19.0 %experts_out.1 = bf16[2048,2048]{1,0:T(8,128)(2,1)} custom-call(bf16[704,2048]{1,0:T(8,128)(2,1)} %get-tuple-element.102.refs_10_.refs_0_.refs_4_, bf16[704,2048]{1,0:T(8,128)(2,1)} %get-tuple-element.108.refs_1_.refs_5_, bf16[1536,1408]{1,0:T(8,128)(2,1)} %get-tuple-element.110.refs_2_.refs_3_, ...), custom_call_target="tpu_custom_call" | custom-call | bytes 1048576 | tf_op jit(solution)/shard_map/experts_out/pallas_call | solution.py:812
  352.6 67.2 %experts_back.1 = (bf16[2048,2048]{1,0:T(8,128)(2,1)}, bf16[1536,1408]{1,0:T(8,128)(2,1)}, bf16[1536,1408]{1,0:T(8,128)(2,1)}, f32[128,2048]{1,0:T(8,128)}) custom-call(bf16[1024,1408]{1,0:T(8,128)(2,1)} %get-tuple-element.97.refs_2_.refs_0_, bf16[1024,1408]{1,0:T(8,128)(2,1)} %get-tuple-element.99.refs_1_, ...), custom_call_target="tpu_custom_call" | custom-call | bytes 1048576 | tf_op jit(solution)/shard_map/experts_back/pallas_call | solution.py:812
  419.7 61.5 %weight_grads.1 = (f32[128,2048]{1,0:T(8,128)}, bf16[2048,1408]{1,0:T(8,128)(2,1)}, bf16[2048,1408]{1,0:T(8,128)(2,1)}, bf16[1408,2048]{1,0:T(8,128)(2,1)}, bf16...) custom-call(bf16[1536,2048]{1,0:T(8,128)(2,1)} %get-tuple-element.116.refs_0_, ...), custom_call_target="tpu_custom_call" | custom-call | bytes 1048576 | tf_op jit(solution)/shard_map/weight_grads/pallas_call | solution.py:1008
  481.2 1.5 multiply_reduce_fusion
  482.8 2.4 fusion.42.refs_0_
  485.2 46.2 %ring_gather.7 = (bf16[16,128,2048]{2,1,0:T(8,128)(2,1)}, bf16[1024,352]{1,0:T(8,128)(2,1)}, bf16[96,2048]{1,0:T(8,128)(2,1)}) custom-call(bf16[128,2048]{1,0:T(8,128)(2,1)} %fusion.42.refs_0_, bf16[2048,352]{1,0:T(8,128)(2,1)} %get-tuple-element.127.refs_1_, bf16[192,2048]{1,0:T(8,128)(2,1)} %get-tuple-element.128.refs_2_), custom_call_target="tpu_custom_call" | custom-call | bytes 1048576 | tf_op jit(solution)/shard_map/ring_gather/pallas_call | solution.py:295
  531.3 18.7 %attend_back.1 = (bf16[2048,512]{1,0:T(8,128)(2,1)}, bf16[128,2048]{1,0:T(8,128)(2,1)}) custom-call(bf16[2048,192]{1,0:T(8,128)(2,1)} %get-tuple-element.123.refs_0_, bf16[2048,192]{1,0:T(8,128)(2,1)} %get-tuple-element.124.refs_1_, bf16[2048,128]{1,0:T(8,128)(2,1)} %get-tuple-element.125.refs_2_, f32[2048,1]{1,0:T(8,128)} %get-tuple-element.126.refs_3_, ...), custom_call_target="tpu_custom_call" | custom-call | bytes 1048576 | tf_op jit(solution)/shard_map/attend_back/pallas_call | solution.py:650
  550.1 69.2 %ring_scatter.3 = (f32[128,2688]{1,0:T(8,128)}, bf16[704,2048]{1,0:T(8,128)(2,1)}, bf16[2048,128]{1,0:T(8,128)(2,1)}, bf16[2048,64]{1,0:T(8,128)(2,1)}, bf16[512,256]{1,0:T(8,128)(2,1)}) custom-call(bf16[2048,512]{1,0:T(8,128)(2,1)} %get-tuple-element.130.refs_0_, bf16[2688,512]{1,0:T(8,128)(2,1)} %get-tuple-element.131.refs_1_, ...), custom_call_target="tpu_custom_call" | custom-call | bytes 1048576 | tf_op jit(solution)/shard_map/ring_scatter/pallas_call | solution.py:424
  619.3 0.8 slice.57
  620.1 1.1 multiply_reduce_fusion.3
  621.3 1.1 subtract_convert_fusion
  622.4 4.2 fusion.22
  627.8 1.1 add_convert_fusion.refs_0_
  628.9 0.8 add_convert_fusion.2.refs_2_
  630.4 108.6 %ring_gather.8 = (bf16[16,1024,352]{2,1,0:T(8,128)(2,1)}, bf16[16,128,576]{2,1,0:T(8,128)(2,1)}, bf16[16,96,2048]{2,1,0:T(8,128)(2,1)}, bf16[1024,128]{1,0:T(8,1...) custom-call(bf16[1024,352]{1,0:T(8,128)(2,1)} %add_convert_fusion.re, ...), custom_call_target="tpu_custom_call" | custom-call | bytes 1048576 | tf_op jit(solution)/shard_map/ring_gather/pallas_call | solution.py:295
  739.1 2.0 add_convert_fusion.4.refs_0_
  741.0 1.1 add_convert_fusion.3
  742.2 2.0 add.194.refs_3_
  744.2 0.7 convolution_convert_fusion
  744.9 0.9 collective-permute-start
  746.4 15.6 %wide_shared.1 = (f32[1024,2816]{1,0:T(8,128)}, f32[1024,2816]{1,0:T(8,128)}) custom-call(bf16[16,1024,352]{2,1,0:T(8,128)(2,1)} %get-tuple-element.156.i_ref), custom_call_target="tpu_custom_call" | custom-call | bytes 1048576 | tf_op jit(solution)/shard_map/wide_shared/pallas_call | solution.py:1042
  762.0 7.9 trim.1
  770.0 5.9 add_bitcast_fusion.2
  775.9 0.7 add_convert_fusion.5.refs_2_
  776.7 5.6 add_bitcast_fusion
  782.4 1.8 fusion.18
  784.2 0.8 pad_maximum_fusion.4.refs_1_
  785.6 90.5 %ring_gather.9 = (bf16[16,1024,128]{2,1,0:T(8,128)(2,1)}, bf16[16,512,128]{2,1,0:T(8,128)(2,1)}, bf16[16,256,256]{2,1,0:T(8,128)(2,1)}, bf16[16,128,2048]{2,1,0:...) custom-call(bf16[1024,128]{1,0:T(8,128)(2,1)} %add_convert_fusion.4.refs_0_, ...), custom_call_target="tpu_custom_call" | custom-call | bytes 1048576 | tf_op jit(solution)/shard_map/ring_gather/pallas_call | solution.py:295
  876.2 1.5 bitcast_convert_fusion
  877.7 2.0 copy.59
  879.6 6.1 wide_kv.1
  885.8 6.8 dynamic-slice_convert_fusion
  892.6 3.1 add_bitcast_fusion.1
  897.0 10.3 %wide_query.1 = f32[1024,3072]{1,0:T(8,128)} custom-call(bf16[16,1024,128]{2,1,0:T(8,128)(2,1)} %get-tuple-element.151.n_ref, bf16[16,512,128]{2,1,0:T(8,128)(2,1)} %get-tuple-element.152.r_ref), custom_call_target="tpu_custom_call" | custom-call | bytes 1048576 | tf_op jit(solution)/shard_map/wide_query/pallas_call | solution.py:850
  (138 shorter events, 9.4 us)
Async XLA Ops:
  7.2 255.9 %all-gather.2.cloned.1.call-start = ((), (), s32[]{:S(2)}) async-start(), calls=%async_computation | async-start | bytes 8912896 | tf_op jit(solution)/shard_map/all_gather | solution.py:1130
  20.7 52.1 %copy-start.33 = (s32[1,2048]{1,0:T(1,128)S(1)}, s32[1,2048]{1,0:T(1,128)}, u32[]{:S(2)}) copy-start(s32[1,2048]{1,0:T(1,128)} %refs_10_.2) | copy-start | bytes 24580
  75.5 8.1 copy-start.4
  77.4 178.5 %copy-start.31 = (f32[16,1,128]{2,1,0:T(1,128)}, f32[16,1,128]{2,1,0:T(1,128)S(1)}, u32[]{:S(2)}) copy-start(f32[16,1,128]{2,1,0:T(1,128)S(1)} %get-tuple-element.215.refs_6_.refs_4_.refs_8_) | copy-start | bytes 24580
  82.2 1.4 copy-start.9
  82.3 1.4 copy-start.11
  82.3 1.4 copy-start.13
  82.3 1.4 copy-start.15
  117.9 67.5 %copy-start.2 = (bf16[1,128,2048]{2,1,0:T(8,128)(2,1)S(1)}, bf16[1,128,2048]{2,1,0:T(8,128)(2,1)}, u32[]{:S(2)}) copy-start(bf16[1,128,2048]{2,1,0:T(8,128)(2,1)} %param.20) | copy-start | bytes 1572868
  187.0 65.7 %copy-start = (bf16[1024,576]{1,0:T(8,128)(2,1)S(1)}, bf16[1024,576]{1,0:T(8,128)(2,1)}, u32[]{:S(2)}) copy-start(bf16[1024,576]{1,0:T(8,128)(2,1)} %copy.51.refs_4_.refs_2_) | copy-start | bytes 3538948
  187.0 295.7 %copy-start.41 = (f32[128]{0:T(128)}, f32[128]{0:T(128)S(1)}, u32[]{:S(2)}) copy-start(f32[128]{0:T(128)S(1)} %add_rsqrt_fusion.2) | copy-start | bytes 1540
  187.1 435.3 %copy-start.34 = (f32[2048]{0:T(1024)}, f32[2048]{0:T(1024)S(1)}, u32[]{:S(2)}) copy-start(f32[2048]{0:T(1024)S(1)} %get-tuple-element.247) | copy-start | bytes 24580
  252.7 369.6 %copy-start.45 = (f32[128]{0:T(128)}, f32[128]{0:T(128)S(1)}, u32[]{:S(2)}) copy-start(f32[128]{0:T(128)S(1)} %add_rsqrt_fusion.1) | copy-start | bytes 1540
  254.3 3.5 copy-start.20
  254.3 3.5 copy-start.21
  254.3 2.2 copy-start.30
  255.9 5.2 copy-start.10
  255.9 5.2 copy-start.12
  255.9 5.2 copy-start.14
  255.9 5.2 copy-start.16
  255.9 5.2 copy-start.26
  419.7 63.0 %copy-start.3 = (bf16[1,128,2048]{2,1,0:T(8,128)(2,1)S(1)}, bf16[1,128,2048]{2,1,0:T(8,128)(2,1)}, u32[]{:S(2)}) copy-start(bf16[1,128,2048]{2,1,0:T(8,128)(2,1)} %param.24) | copy-start | bytes 1572868
  482.7 48.6 %copy-start.43 = (f32[128]{0:T(128)}, f32[128]{0:T(128)S(1)}, u32[]{:S(2)}) copy-start(f32[128]{0:T(128)S(1)} %broadcast_multiply_fusion.2) | copy-start | bytes 1540
  550.0 70.1 %copy-start.24 = (f32[128,512]{1,0:T(8,128)S(1)}, f32[128,512]{1,0:T(8,128)}, u32[]{:S(2)}) copy-start(f32[128,512]{1,0:T(8,128)} %get-tuple-element.245) | copy-start | bytes 786436
  621.2 8.5 copy-start.39
  622.4 5.5 copy-start.5
  622.4 5.5 copy-start.25
  626.6 112.4 %copy-start.37 = (f32[2048]{0:T(1024)}, f32[2048]{0:T(1024)S(1)}, u32[]{:S(2)}) copy-start(f32[2048]{0:T(1024)S(1)} %get-tuple-element.212) | copy-start | bytes 24580
  626.6 2.3 copy-start.19
  626.6 2.3 copy-start.29
  630.4 111.8 %copy-start.17 = (bf16[128,2048]{1,0:T(8,128)(2,1)S(1)}, bf16[128,2048]{1,0:T(8,128)(2,1)}, u32[]{:S(2)}) copy-start(bf16[128,2048]{1,0:T(8,128)(2,1)} %get-tuple-element.141.refs_6_) | copy-start | bytes 1572868
  739.0 5.1 copy-start.8
  739.0 5.1 copy-start.18
  742.1 3.7 copy-start.36
  742.2 3.7 copy-start.38
  742.2 3.6 copy-start.40
  744.9 40.1 %collective-permute-start = (bf16[64,576]{1,0:T(8,128)(2,1)S(1)}, bf16[64,576]{1,0:T(8,128)(2,1)S(1)}, u32[]{:S(2)}, u32[]{:S(2)}) collective-permute-start(bf16[64,576]{1,0:T(8,128)(2,1)S(1)} %constant_dynamic-slice_fusion), channel_id=1, source_target_pairs={{0,1},{1,0},{2,3},{3,2},{4,5},{5,4},{6,7},{7,6},{8,9},{9,8},{10,11... | collective-permute-start | bytes 221192 | tf_op jit(solution)/shard_map/ppermute | solution.py:1296
  770.0 6.0 copy-start.27
  770.0 6.0 copy-start.32
  770.0 6.6 copy-start.6
  776.6 5.7 copy-start.1
  776.6 5.7 copy-start.22
  776.6 5.7 copy-start.23
  776.6 5.7 copy-start.35
  776.6 5.7 copy-start.42
  776.6 5.7 copy-start.44
  776.7 5.7 copy-start.46
  776.7 5.7 copy-start.47
  879.6 12.9 %slice-start = ((s8[5767168]{0:T(1024)(128)(4,1)}), s8[1572864]{0:T(1024)(128)(4,1)S(1)}, s32[]{:S(2)}) async-start(s8[5767168]{0:T(1024)(128)(4,1)} %bitcast.90), calls=%async_computation.1 | async-start | bytes 3145728
  885.8 6.8 slice-start.1
  885.8 6.8 copy-start.7
  892.6 3.1 copy-start.28
Sparse Core Ops, SparseCore 0:
  71.0 86.8 all-gather.1
